TPU v7x, 128 devices: a whole 4x4x4 slice. The times are simulated.
128 devices in a mesh: grp: 4 (over x_lo, core), dom: 32 (over x_hi, z, y).
Axes of the slice: x: 4 (x_hi: 2, x_lo: 2; x = x_hi * 2 + x_lo), y: 4, z: 4, core: 2. Of those that a mesh axis runs over, the one named last changes fastest.
Arguments:
- ice_depth: float32 [131072], P('dom'), may hold values from 1 to 3
- heat_state: float32 [20, 131072], P(None, 'dom'), may hold values from -1 to 1
- elevation_slope_components: float32 [2, 131072], P(None, 'dom'), may hold values from -3 to 3
- sliding_drag: float32 [131072], P('dom'), may hold values from 0.1 to 1
- adjacent_polygons: int32 [6, 131072], P(None, 'dom'), may hold values from 0 to 131071, as said below
- edge_timing_ratio: float32 [6, 131072], P(None, 'dom'), may hold values from 0.02 to 0.15
- edge_average_normal_speed: float32 [6, 131072], P(None, 'dom'), may hold values from -4 to 4
- tier_edge_normal_speed: float32 [20, 6, 131072], P('grp', None, 'dom'), may hold values from -4 to 4
- position_donor_polygons: int32 [32, 4, 32, 64], P('dom'), may hold values from -1 to 4095, as said below
- shaft_holding_position: int32 [128, 512], P('dom', 'grp'), may hold values from 0 to 2047, as said below
- prior_node_motion: float32 [2, 21, 128, 512], P(None, None, 'dom', 'grp'), may hold values from -3 to 3
Outputs:
- transported_ice_depth: float32 [131072], P('dom')
- transported_heat_state: float32 [20, 131072], P('grp', 'dom')
- node_velocity: float32 [2, 21, 128, 512], P(None, None, 'dom', 'grp')
- polygon_tier_motion: float32 [2, 20, 131072], P(None, 'grp', 'dom')
Inputs may be any that keep to these rules, and one draw needn't show every extreme that they name: `adjacent_polygons`: each entry is the index of another cell at most 1024 positions away from its own cell in the global order; the distance 1024 occurs. `shaft_holding_position`: slot block p of a device's buffer (slots p * 64 to p * 64 + 63) holds data of owner partition p. The columns of one device take distinct slots; for each device one owner's block is full and the others hold at most 64 columns of it. `position_donor_polygons`: cells are numbered within partition p. An entry is -1 exactly when no column of device (g, d) uses that slot; a cell may be named by several slots or by none.
All inputs are finite; a program needn't handle non-finite values.
Results may differ from a plain program's by a relative error of at most 0.00002.
Values sent between devices are 32-bit elements; how exact they have to be, the bound alone decides.
No kernel may reach another device: no remote copies, remote signals or barrier semaphores. Data moves between devices by JAX's collectives and lax.ppermute only.
A program may use at most 64 MiB of HBM per device.

v0:
```python
import math

import jax
import jax.numpy as jnp
import numpy as np
from jax import lax
from jax.sharding import PartitionSpec as P

PICARD = 2


HSTEP = 0.25
OMEGA = 0.5
EPS_RATE = 0.01


def padded_2(cells, sides, width):
    for axis, dim in sides:
        count = lax.axis_size(axis)
        ends = count - 1
        head = lax.slice_in_dim(cells, 0, width, axis=dim)
        tail = lax.slice_in_dim(cells, cells.shape[dim] - width, cells.shape[dim], axis=dim)
        cells = jnp.concatenate(
            [
                lax.ppermute(tail, axis, [(i, (i + 1) % count) for i in range(ends)]),
                cells,
                lax.ppermute(head, axis, [((i + 1) % count, i) for i in range(ends)]),
            ],
            axis=dim,
        )
    return cells


def basis_tables():
    lower_point = 0.5 - 0.5 / math.sqrt(3.0)
    points = (lower_point, 1.0 - lower_point)
    table_x = np.zeros((8, 8))
    table_y = np.zeros((8, 8))
    table_z = np.zeros((8, 8))
    for qpoint in range(8):
        point_z, point_x, point_y = (
            points[qpoint // 4],
            points[qpoint // 2 % 2],
            points[qpoint % 2],
        )
        for corner in range(8):
            upper_z, upper_x, upper_y = (corner // 4, corner // 2 % 2, corner % 2)
            value_z = point_z if upper_z else 1.0 - point_z
            value_x = point_x if upper_x else 1.0 - point_x
            value_y = point_y if upper_y else 1.0 - point_y
            slope_z = 1.0 if upper_z else -1.0
            slope_x = 1.0 if upper_x else -1.0
            slope_y = 1.0 if upper_y else -1.0
            table_x[qpoint, corner] = slope_x * value_y * value_z
            table_y[qpoint, corner] = value_x * slope_y * value_z
            table_z[qpoint, corner] = value_x * value_y * slope_z
    return (table_x, table_y, table_z)


def corner_sum(array):
    return array[..., :-1, :-1] + array[..., 1:, :-1] + array[..., :-1, 1:] + array[..., 1:, 1:]


def element_geometry(geometry_ext):
    tier_pile = geometry_ext.shape[0] - 1
    layer_depth = corner_sum(geometry_ext[0]) * (0.25 / tier_pile)
    hardness = jnp.exp(-0.25 * corner_sum(geometry_ext[1:]))
    return (layer_depth, hardness)


def corner_views(field_ext, tier_pile):
    span_x = field_ext.shape[2] - 1
    span_y = field_ext.shape[3] - 1
    corner_list = []
    for corner in range(8):
        upper_z, upper_x, upper_y = (corner // 4, corner // 2 % 2, corner % 2)
        corner_list.append(
            field_ext[
                :,
                upper_z : upper_z + tier_pile,
                upper_x : upper_x + span_x,
                upper_y : upper_y + span_y,
            ]
        )
    return corner_list


def point_gradients(corner_list, tables, qpoint, layer_depth):
    table_x, table_y, table_z = tables
    grad_x = float(table_x[qpoint, 0]) * corner_list[0]
    grad_y = float(table_y[qpoint, 0]) * corner_list[0]
    grad_z = float(table_z[qpoint, 0]) * corner_list[0]
    for corner in range(1, 8):
        grad_x = grad_x + float(table_x[qpoint, corner]) * corner_list[corner]
        grad_y = grad_y + float(table_y[qpoint, corner]) * corner_list[corner]
        grad_z = grad_z + float(table_z[qpoint, corner]) * corner_list[corner]
    return (grad_x / HSTEP, grad_y / HSTEP, grad_z / layer_depth)


def effective_viscosity(corner_list, tables, layer_depth, hardness):
    result = []
    for qpoint in range(8):
        grad_x, grad_y, grad_z = point_gradients(corner_list, tables, qpoint, layer_depth)
        shear = grad_y[0] + grad_x[1]
        strain_rate = (
            grad_x[0] * grad_x[0]
            + grad_y[1] * grad_y[1]
            + grad_x[0] * grad_y[1]
            + 0.25 * shear * shear
            + 0.25 * (grad_z[0] * grad_z[0] + grad_z[1] * grad_z[1])
            + EPS_RATE
        )
        result.append(0.5 * hardness * strain_rate ** (-1.0 / 3.0))
    return result


def element_forces(corner_list, tables, layer_depth, viscous):
    table_x, table_y, table_z = tables
    weight = layer_depth * (HSTEP * HSTEP / 8.0) / HSTEP
    forces = [jnp.zeros_like(corner_list[0]) for corner in range(8)]
    for qpoint in range(8):
        grad_x, grad_y, grad_z = point_gradients(corner_list, tables, qpoint, layer_depth)
        visc_point = viscous[qpoint]
        shear = visc_point * (grad_y[0] + grad_x[1])
        flux_x = jnp.stack([visc_point * (4.0 * grad_x[0] + 2.0 * grad_y[1]), shear]) * weight
        flux_y = jnp.stack([shear, visc_point * (4.0 * grad_y[1] + 2.0 * grad_x[0])]) * weight
        flux_z = jnp.stack([visc_point * grad_z[0], visc_point * grad_z[1]]) * (HSTEP * HSTEP / 8.0)
        for corner in range(8):
            forces[corner] = (
                forces[corner]
                + float(table_x[qpoint, corner]) * flux_x
                + float(table_y[qpoint, corner]) * flux_y
                + float(table_z[qpoint, corner]) * flux_z
            )
    return forces


def element_diagonal(tables, layer_depth, viscous):
    table_x, table_y, table_z = tables
    weight = layer_depth * (HSTEP * HSTEP / 8.0) / (HSTEP * HSTEP)
    vertical = HSTEP * HSTEP / 8.0 / layer_depth
    parts = [None] * 8
    for qpoint in range(8):
        visc_point = viscous[qpoint]
        for corner in range(8):
            along_x = float(table_x[qpoint, corner]) ** 2 * visc_point * weight
            along_y = float(table_y[qpoint, corner]) ** 2 * visc_point * weight
            along_z = float(table_z[qpoint, corner]) ** 2 * visc_point * vertical
            term = jnp.stack([4.0 * along_x + along_y + along_z, along_x + 4.0 * along_y + along_z])
            parts[corner] = term if parts[corner] is None else parts[corner] + term
    return parts


def gather_nodes(parts):
    span_x = parts[0].shape[2] - 1
    span_y = parts[0].shape[3] - 1
    summed = None
    for corner in range(8):
        upper_z, upper_x, upper_y = (corner // 4, corner // 2 % 2, corner % 2)
        padded = jnp.pad(parts[corner], ((0, 0), (upper_z, 1 - upper_z), (0, 0), (0, 0)))
        node_part = padded[
            :, :, 1 - upper_x : 1 - upper_x + span_x, 1 - upper_y : 1 - upper_y + span_y
        ]
        summed = node_part if summed is None else summed + node_part
    return summed


def node_rims(array):
    return padded_2(array, (("grp", 2), ("dom", 1)), 1)


def shards(
    ice_depth,
    heat_state,
    elevation_slope_components,
    sliding_drag,
    adjacent_polygons,
    edge_timing_ratio,
    edge_average_normal_speed,
    tier_edge_normal_speed,
    position_donor_polygons,
    shaft_holding_position,
    prior_node_motion,
):
    batch_ordinal = lax.axis_index("grp")
    domain_index = lax.axis_index("dom")
    groups = lax.axis_size("grp")
    domains = lax.axis_size("dom")
    cell_count = ice_depth.shape[0]
    tier_pile = heat_state.shape[0]
    tiers_in_batch = tier_edge_normal_speed.shape[0]
    rim_width = cell_count // 4
    slot_width = position_donor_polygons.shape[3]
    own_heat_state = lax.dynamic_slice_in_dim(
        heat_state, batch_ordinal * tiers_in_batch, tiers_in_batch, 0
    )
    piled_fields = jnp.concatenate([ice_depth[None], own_heat_state], 0)
    extended = padded_2(piled_fields, (("dom", 1),), rim_width)
    local_ids = adjacent_polygons - (domain_index * cell_count - rim_width)
    beside = extended[:, local_ids]
    transported_ice_depth = ice_depth - jnp.sum(
        edge_timing_ratio
        * (
            jnp.maximum(edge_average_normal_speed, 0.0) * ice_depth[None]
            + jnp.minimum(edge_average_normal_speed, 0.0) * beside[0]
        ),
        0,
    )
    leaving_tier = jnp.maximum(tier_edge_normal_speed, 0.0) * own_heat_state[:, None]
    incoming_layer = jnp.minimum(tier_edge_normal_speed, 0.0) * beside[1:]
    transported_heat_state = own_heat_state - jnp.sum(
        edge_timing_ratio[None] * (leaving_tier + incoming_layer), 1
    )
    shaft_fields = jnp.concatenate(
        [ice_depth[None], elevation_slope_components, sliding_drag[None], heat_state], 0
    )
    requests = lax.dynamic_index_in_dim(
        position_donor_polygons[0], batch_ordinal, 0, keepdims=False
    )
    outgoing = shaft_fields[:, jnp.maximum(requests, 0)]
    incoming = lax.all_to_all(outgoing, "dom", split_axis=1, concat_axis=1, tiled=True)
    column = incoming.reshape(shaft_fields.shape[0], -1)[:, shaft_holding_position]
    column_thick = column[0]
    column_slope = column[1:3]
    column_friction = column[3]
    geometry = jnp.concatenate([column[0:1], column[4:]], 0)
    span_x, span_y = shaft_holding_position.shape
    tables = basis_tables()
    driving = -(column_thick[None] * column_slope)[:, None]
    current_guess = prior_node_motion
    velocity_rows = 2 * (tier_pile + 1)
    for picard_step in range(PICARD):
        flat_field = current_guess.reshape(velocity_rows, span_x, span_y)
        if picard_step == 0 and 0 == 0:
            joined = node_rims(jnp.concatenate([flat_field, geometry], 0))
            field_ext = joined[:velocity_rows]
            layer_depth, hardness = element_geometry(joined[velocity_rows:])
        else:
            field_ext = node_rims(flat_field)
        field_ext = field_ext.reshape(2, tier_pile + 1, span_x + 2, span_y + 2)
        corner_list = corner_views(field_ext, tier_pile)
        viscous = effective_viscosity(corner_list, tables, layer_depth, hardness)
        diagonal = gather_nodes(element_diagonal(tables, layer_depth, viscous))
        diagonal = diagonal.at[:, 0].add(column_friction)
        forces = gather_nodes(element_forces(corner_list, tables, layer_depth, viscous))
        forces = forces.at[:, 0].add(column_friction * current_guess[:, 0])
        current_guess = current_guess + OMEGA * (driving - forces) / diagonal
    layer_mean = 0.5 * (current_guess[:, :-1] + current_guess[:, 1:])
    by_block = jnp.transpose(
        layer_mean.reshape(2, groups, tiers_in_batch, span_x * span_y), (1, 0, 2, 3)
    )
    buffer = jnp.zeros((groups, 2, tiers_in_batch, domains * slot_width), jnp.float32)
    buffer = buffer.at[:, :, :, shaft_holding_position.reshape(-1)].set(by_block)
    buffer = buffer.reshape(groups, 2 * tiers_in_batch, domains, slot_width)
    joint_layout = jnp.transpose(buffer, (0, 2, 1, 3)).reshape(
        groups * domains, 2 * tiers_in_batch, slot_width
    )
    arrived = lax.all_to_all(joint_layout, ("grp", "dom"), split_axis=0, concat_axis=0, tiled=True)
    values = jnp.moveaxis(arrived, 1, 0).reshape(2 * tiers_in_batch, -1)
    owner_ids = position_donor_polygons[0].reshape(-1)
    safe_ids = jnp.where(owner_ids >= 0, owner_ids, cell_count)
    cell_sums = jax.vmap(
        lambda values_row: jax.ops.segment_sum(values_row, safe_ids, cell_count + 1)
    )(values)[:, :cell_count]
    counts = jax.ops.segment_sum(jnp.ones(safe_ids.shape, jnp.float32), safe_ids, cell_count + 1)[
        :cell_count
    ]
    polygon_tier_motion = (cell_sums / jnp.maximum(counts, 1.0)).reshape(
        2, tiers_in_batch, cell_count
    )
    return (transported_ice_depth, transported_heat_state, current_guess, polygon_tier_motion)


def solution(mesh):
    in_specs = (
        P("dom"),
        P(None, "dom"),
        P(None, "dom"),
        P("dom"),
        P(None, "dom"),
        P(None, "dom"),
        P(None, "dom"),
        P("grp", None, "dom"),
        P("dom", None, None, None),
        P("dom", "grp"),
        P(None, None, "dom", "grp"),
    )
    out_specs = (P("dom"), P("grp", "dom"), P(None, None, "dom", "grp"), P(None, "grp", "dom"))
    return jax.shard_map(shards, mesh=mesh, in_specs=in_specs, out_specs=out_specs, check_vma=False)
```

profile of v0, /device:TPU:1, one launch (start us, length us, event | category | flops | bytes accessed | tf_op | source)
XLA Modules:
  0.0 413.3 jit_solution(5405600360198839048)
XLA Ops:
  1.4 1.1 pad_maximum_fusion.1
  3.2 5.5 %gather_fusion.1 = f32[2048,24]{1,0:T(8,128)S(1)} fusion(f32[24,4096]{0,1:T(8,128)S(1)} %copy.68, s32[2048]{0:T(1024)S(1)} %broadcast_clamp_fusion.1), kind=kCustom, calls=%fused_computation.1 | custom fusion | bytes 401408 | tf_op jit(solution)/shard_map/gather | solution.py:220
  9.0 0.9 reshape.483
  10.0 11.3 %all-to-all-start = ((f32[32,1,1536]{2,1,0:T(1,128)}), f32[32,1,1536]{2,1,0:T(1,128)S(1)}, u32[]{:S(2)}, u32[]{:S(2)}) async-start(f32[32,1,1536]{2,1,0:T(1,128)} %reshape.483), calls=%async_computation | async-start | bytes 393216 | tf_op jit(solution)/shard_map/all_to_all | solution.py:221
  21.3 1.0 constant_dynamic-slice_fusion
  22.9 3.7 collective-permute-start
  26.7 1.3 collective-permute-start.1
  28.9 46.2 %scatter_custom_fusion.2 = f32[4097]{0:T(1024)S(1)} fusion(s32[8192]{0:T(1024)S(1)} %bitcast.1001, f32[8192]{0:T(1024)S(1)} %broadcast.650, f32[]{:T(128)} %constant.313.clone.1), kind=kCustom, calls=%fused_computation.1019 | custom fusion | flops 8192 | bytes 16392 | tf_op jit(solution)/shard_map/scatter-add | solution.py:265
  76.3 1.1 reduce.8
  77.9 1.0 gather_fusion.2
  79.3 3.6 collective-permute-start.2
  82.9 1.9 collective-permute-start.3
  85.4 3.7 collective-permute-done.3
  89.6 3.9 collective-permute-start.4
  93.6 1.8 collective-permute-start.5
  95.4 3.2 collective-permute-done.5
  103.1 0.8 fusion.490
  104.6 0.8 fusion.487
  106.6 1.0 fusion.163
  107.6 1.0 add_add_fusion.4
  108.7 1.0 add_add_fusion.5
  109.7 1.2 multiply_add_fusion.9
  110.9 1.0 multiply_add_fusion.10
  111.9 1.0 add_add_fusion.6
  112.9 1.0 add_add_fusion.7
  113.9 1.0 fusion.184
  117.1 0.8 fusion.570
  117.8 3.2 collective-permute-start.6
  121.0 1.9 collective-permute-start.7
  123.0 1.5 pad_maximum_fusion.19
  124.5 1.9 copy.66
  126.4 89.3 %gather_fusion = f32[24576,6]{1,0:T(8,128)} fusion(f32[6,6144]{0,1:T(8,128)S(1)} %copy.66, s32[24576]{0:T(1024)} %broadcast_clamp_fusion), kind=kCustom, calls=%fused_computation | custom fusion | bytes 1277952 | tf_op jit(solution)/shard_map/gather | solution.py:200
  215.7 8.5 %copy.67 = f32[6,4096,6]{1,0,2:T(8,128)S(1)} copy(f32[6,4096,6]{2,1,0:T(8,128)} %bitcast.976) | data formatting | bytes 1179648 | tf_op jit(solution)/shard_map/gather | solution.py:200
  224.2 1.3 pad_maximum_fusion.38
  225.5 2.4 collective-permute-start.8
  227.9 1.5 collective-permute-start.9
  229.4 1.0 fusion.4
  230.4 4.0 collective-permute-done.9
  234.4 1.2 pad_maximum_fusion.2
  238.6 0.8 fusion.466
  239.5 0.8 fusion.463
  241.5 1.0 multiply_bitcast_fusion.9
  243.0 1.0 fusion.121
  244.0 1.0 add_add_fusion
  245.1 1.0 add_add_fusion.1
  246.1 1.0 multiply_add_fusion.4
  247.1 1.3 multiply_add_fusion.5
  248.4 1.0 add_add_fusion.2
  249.4 1.0 add_add_fusion.3
  250.4 1.0 fusion.142
  253.8 1.8 copy.73
  255.6 3.9 broadcast_in_dim.25
  259.5 52.0 %scatter_fusion = f32[4,2,5,2048]{2,0,3,1:T(4,128)} fusion(f32[4,2,5,2048]{2,0,3,1:T(4,128)} %broadcast_in_dim.25, s32[512]{0:T(512)S(1)} %bitcast.1004, f32[512,4,2,5]{3,1,2,0:T(4,128)} %copy.73), kind=kCustom, calls=%fused_computation.3 | custom fusion | bytes 247808 | tf_op jit(solution)/shard_map/scatter | solution.py:253
  311.5 6.8 %copy.74 = f32[4,2,5,2048]{3,0,2,1:T(4,128)S(1)} copy(f32[4,2,5,2048]{2,0,3,1:T(4,128)} %scatter_fusion) | data formatting | bytes 655360 | tf_op jit(solution)/shard_map/scatter | solution.py:253
  319.2 1.2 reshape.485
  320.4 24.9 %all-to-all-start.1 = ((f32[128,1,640]{2,1,0:T(1,128)}), f32[128,1,640]{2,1,0:T(1,128)S(1)}, u32[]{:S(2)}, u32[]{:S(2)}) async-start(f32[128,1,640]{2,1,0:T(1,128)} %reshape.485), calls=%async_computation.1 | async-start | bytes 655360 | tf_op jit(solution)/shard_map/all_to_all | solution.py:258
  345.3 1.6 fusion.571
  347.6 9.4 %all-to-all-done.1 = f32[128,1,640]{2,1,0:T(1,128)S(1)} async-done(((f32[128,1,640]{2,1,0:T(1,128)}), f32[128,1,640]{2,1,0:T(1,128)S(1)}, u32[]{:S(2)}, u32[]{:S(2)}) %all-to-all-start.1) | async-done | bytes 327712 | tf_op jit(solution)/shard_map/all_to_all | solution.py:258
  357.0 1.4 reduce.9
  359.1 2.7 copy.77
  361.8 46.4 %scatter_custom_fusion.1 = f32[10,4097]{0,1:T(8,128)S(1)} fusion(s32[8192]{0:T(1024)} %bitcast.1002, f32[8192,10]{1,0:T(8,128)} %copy.77, f32[]{:T(128)} %constant.313.clone.1), kind=kCustom, calls=%fused_computation.6 | custom fusion | flops 81920 | bytes 164392 | tf_op jit(solution)/shard_map/vmap()/scatter-add | solution.py:263
  408.2 1.5 slice.1001
  409.7 2.2 copy.80
  412.0 0.8 copy.79
  (158 shorter events, 23.7 us)
Async XLA Ops:
  3.2 19.1 %copy-start.14 = (f32[4096]{0:T(1024)S(1)}, f32[4096]{0:T(1024)}, u32[]{:S(2)}) copy-start(f32[4096]{0:T(1024)} %param.19) | copy-start | bytes 49156
  3.2 24.8 %copy-start.21 = (s32[1,4,32,64]{3,2,1,0:T(8,128)S(1)}, s32[1,4,32,64]{3,2,1,0:T(8,128)}, u32[]{:S(2)}) copy-start(s32[1,4,32,64]{3,2,1,0:T(8,128)} %param.27) | copy-start | bytes 98308
  3.2 24.9 %copy-start.27 = (s32[4,128]{1,0:T(4,128)S(1)}, s32[4,128]{1,0:T(4,128)}, u32[]{:S(2)}) copy-start(s32[4,128]{1,0:T(4,128)} %param.28) | copy-start | bytes 6148
  3.2 25.0 %copy-start.19 = (s32[6,4096]{1,0:T(8,128)S(1)}, s32[6,4096]{1,0:T(8,128)}, u32[]{:S(2)}) copy-start(s32[6,4096]{1,0:T(8,128)} %param.23) | copy-start | bytes 294916
  9.0 70.1 %copy-start = (f32[2,21,4,128]{3,2,1,0:T(4,128)S(1)}, f32[2,21,4,128]{3,2,1,0:T(4,128)}, u32[]{:S(2)}) copy-start(f32[2,21,4,128]{3,2,1,0:T(4,128)} %param.29) | copy-start | bytes 258052
  10.0 65.8 %all-to-all-start = ((f32[32,1,1536]{2,1,0:T(1,128)}), f32[32,1,1536]{2,1,0:T(1,128)S(1)}, u32[]{:S(2)}, u32[]{:S(2)}) async-start(f32[32,1,1536]{2,1,0:T(1,128)} %reshape.483), calls=%async_computation | async-start | bytes 393216 | tf_op jit(solution)/shard_map/all_to_all | solution.py:221
  22.9 100.0 %collective-permute-start = (f32[6,1024]{1,0:T(8,128)}, f32[6,1024]{1,0:T(8,128)}, u32[]{:S(2)}, u32[]{:S(2)}) collective-permute-start(f32[6,1024]{1,0:T(8,128)} %get-tuple-element.615), channel_id=1, source_target_pairs={{0,1},{1,2},{2,3},{3,4},{4,5},{5,6},{6,7},{7,8},{8,9},{9,10},{10,1... | collective-permute-start | bytes 73736 | tf_op jit(solution)/shard_map/ppermute | solution.py:25
  26.7 96.3 %collective-permute-start.1 = (f32[6,1024]{1,0:T(8,128)}, f32[6,1024]{1,0:T(8,128)}, u32[]{:S(2)}, u32[]{:S(2)}) collective-permute-start(f32[6,1024]{1,0:T(8,128)} %get-tuple-element.616), channel_id=1, source_target_pairs={{1,0},{2,1},{3,2},{4,3},{5,4},{6,5},{7,6},{8,7},{9,8},{10,9},{11,1... | collective-permute-start | bytes 73736 | tf_op jit(solution)/shard_map/ppermute | solution.py:27
  28.1 71.0 %copy-start.23 = (s32[8192,1]{0,1:T(1,128)}, s32[8192,1]{0,1:T(1,128)S(1)}, u32[]{:S(2)}) copy-start(s32[8192,1]{0,1:T(1,128)S(1)} %compare_select_fusion.1) | copy-start | bytes 98308
  79.1 37.9 %copy-start.24 = (f32[4,128]{1,0:T(4,128)}, f32[4,128]{1,0:T(4,128)S(1)}, u32[]{:S(2)}) copy-start(f32[4,128]{1,0:T(4,128)S(1)} %get-tuple-element.623) | copy-start | bytes 6148
  79.3 6.2 %collective-permute-start.2 = (f32[63,4,1]{2,1,0:T(4,128)S(1)}, f32[63,4,1]{2,1,0:T(4,128)S(1)}, u32[]{:S(2)}, u32[]{:S(2)}) collective-permute-start(f32[63,4,1]{2,1,0:T(4,128)S(1)} %get-tuple-element.617), channel_id=1, source_target_pairs={{0,32},{32,64},{64,96},{1,33},{33,65},{65,97},{2,34},{34,66},{66,9... | collective-permute-start | bytes 3032 | tf_op jit(solution)/shard_map/ppermute | solution.py:25
  82.9 6.3 %collective-permute-start.3 = (f32[63,4,1]{2,1,0:T(4,128)S(1)}, f32[63,4,1]{2,1,0:T(4,128)S(1)}, u32[]{:S(2)}, u32[]{:S(2)}) collective-permute-start(f32[63,4,1]{2,1,0:T(4,128)S(1)} %get-tuple-element.618), channel_id=1, source_target_pairs={{32,0},{64,32},{96,64},{33,1},{65,33},{97,65},{34,2},{66,34},{98,6... | collective-permute-start | bytes 3032 | tf_op jit(solution)/shard_map/ppermute | solution.py:27
  89.6 5.8 %collective-permute-start.4 = (f32[63,1,130]{2,1,0:T(1,128)S(1)}, f32[63,1,130]{2,1,0:T(1,128)S(1)}, u32[]{:S(2)}, u32[]{:S(2)}) collective-permute-start(f32[63,1,130]{2,1,0:T(1,128)S(1)} %get-tuple-element.189), channel_id=1, source_target_pairs={{0,1},{1,2},{2,3},{3,4},{4,5},{5,6},{6,7},{7,8},{8,9},{9,10},{10,1... | collective-permute-start | bytes 98288 | tf_op jit(solution)/shard_map/ppermute | solution.py:25
  93.6 5.0 %collective-permute-start.5 = (f32[63,1,130]{2,1,0:T(1,128)S(1)}, f32[63,1,130]{2,1,0:T(1,128)S(1)}, u32[]{:S(2)}, u32[]{:S(2)}) collective-permute-start(f32[63,1,130]{2,1,0:T(1,128)S(1)} %get-tuple-element.190), channel_id=1, source_target_pairs={{1,0},{2,1},{3,2},{4,3},{5,4},{6,5},{7,6},{8,7},{9,8},{10,9},{11,1... | collective-permute-start | bytes 98288 | tf_op jit(solution)/shard_map/ppermute | solution.py:27
  98.8 1.5 copy-start.17
  98.8 7.4 %copy-start.6 = (f32[5,129]{1,0:T(8,128)}, f32[5,129]{1,0:T(8,128)S(1)}, u32[]{:S(2)}) copy-start(f32[5,129]{1,0:T(8,128)S(1)} %get-tuple-element.626) | copy-start | bytes 7744
  98.8 7.4 %copy-start.8 = (f32[5,129]{1,0:T(8,128)}, f32[5,129]{1,0:T(8,128)S(1)}, u32[]{:S(2)}) copy-start(f32[5,129]{1,0:T(8,128)S(1)} %get-tuple-element.627) | copy-start | bytes 7744
  98.8 7.4 %copy-start.10 = (f32[5,129]{1,0:T(8,128)}, f32[5,129]{1,0:T(8,128)S(1)}, u32[]{:S(2)}) copy-start(f32[5,129]{1,0:T(8,128)S(1)} %get-tuple-element.628) | copy-start | bytes 7744
  98.8 7.4 %copy-start.12 = (f32[5,129]{1,0:T(8,128)}, f32[5,129]{1,0:T(8,128)S(1)}, u32[]{:S(2)}) copy-start(f32[5,129]{1,0:T(8,128)S(1)} %get-tuple-element.629) | copy-start | bytes 7744
  116.5 6.5 %copy-start.15 = (f32[4096]{0:T(1024)S(1)}, f32[4096]{0:T(1024)}, u32[]{:S(2)}) copy-start(f32[4096]{0:T(1024)} %param.19) | copy-start | bytes 49156
  117.8 106.3 %collective-permute-start.6 = (f32[42,4,1]{2,1,0:T(4,128)}, f32[42,4,1]{2,1,0:T(4,128)}, u32[]{:S(2)}, u32[]{:S(2)}) collective-permute-start(f32[42,4,1]{2,1,0:T(4,128)} %get-tuple-element.619), channel_id=1, source_target_pairs={{0,32},{32,64},{64,96},{1,33},{33,65},{65,97},{2,34},{34,66},{66,9... | collective-permute-start | bytes 2024 | tf_op jit(solution)/shard_map/ppermute | solution.py:25
  121.0 103.1 %collective-permute-start.7 = (f32[42,4,1]{2,1,0:T(4,128)}, f32[42,4,1]{2,1,0:T(4,128)}, u32[]{:S(2)}, u32[]{:S(2)}) collective-permute-start(f32[42,4,1]{2,1,0:T(4,128)} %get-tuple-element.620), channel_id=1, source_target_pairs={{32,0},{64,32},{96,64},{33,1},{65,33},{97,65},{34,2},{66,34},{98,6... | collective-permute-start | bytes 2024 | tf_op jit(solution)/shard_map/ppermute | solution.py:27
  215.7 13.8 %copy-start.2 = (f32[5,6,4096]{2,1,0:T(8,128)S(1)}, f32[5,6,4096]{2,1,0:T(8,128)}, u32[]{:S(2)}) copy-start(f32[5,6,4096]{2,1,0:T(8,128)} %param.26) | copy-start | bytes 1474564
  215.7 13.8 %copy-start.3 = (f32[6,4096]{1,0:T(8,128)S(1)}, f32[6,4096]{1,0:T(8,128)}, u32[]{:S(2)}) copy-start(f32[6,4096]{1,0:T(8,128)} %param.24) | copy-start | bytes 294916
  215.7 19.9 %copy-start.18 = (f32[5,129]{1,0:T(8,128)S(1)}, f32[5,129]{1,0:T(8,128)}, u32[]{:S(2)}) copy-start(f32[5,129]{1,0:T(8,128)} %copy-done.17) | copy-start | bytes 7744
  225.5 4.9 %collective-permute-start.8 = (f32[42,1,130]{2,1,0:T(1,128)S(1)}, f32[42,1,130]{2,1,0:T(1,128)S(1)}, u32[]{:S(2)}, u32[]{:S(2)}) collective-permute-start(f32[42,1,130]{2,1,0:T(1,128)S(1)} %get-tuple-element.249), channel_id=1, source_target_pairs={{0,1},{1,2},{2,3},{3,4},{4,5},{5,6},{6,7},{7,8},{8,9},{9,10},{10,1... | collective-permute-start | bytes 65528 | tf_op jit(solution)/shard_map/ppermute | solution.py:25
  227.9 6.5 %collective-permute-start.9 = (f32[42,1,130]{2,1,0:T(1,128)S(1)}, f32[42,1,130]{2,1,0:T(1,128)S(1)}, u32[]{:S(2)}, u32[]{:S(2)}) collective-permute-start(f32[42,1,130]{2,1,0:T(1,128)S(1)} %get-tuple-element.250), channel_id=1, source_target_pairs={{1,0},{2,1},{3,2},{4,3},{5,4},{6,5},{7,6},{8,7},{9,8},{10,9},{11,1... | collective-permute-start | bytes 65528 | tf_op jit(solution)/shard_map/ppermute | solution.py:27
  239.4 1.5 copy-start.7
  239.4 1.5 copy-start.9
  239.4 1.5 copy-start.11
  239.4 1.5 copy-start.13
  252.9 0.7 copy-start.25
  253.7 5.8 %copy-start.1 = (f32[2,21,4,128]{3,2,1,0:T(4,128)}, f32[2,21,4,128]{3,2,1,0:T(4,128)S(1)}, u32[]{:S(2)}) copy-start(f32[2,21,4,128]{3,2,1,0:T(4,128)S(1)} %divide_add_fusion) | copy-start | bytes 258052
  255.6 3.9 copy-start.26
  318.4 26.9 %copy-start.5 = (f32[5,4096]{1,0:T(8,128)S(1)}, f32[5,4096]{1,0:T(8,128)}, u32[]{:S(2)}) copy-start(f32[5,4096]{1,0:T(8,128)} %fusion.4) | copy-start | bytes 245764
  318.4 28.5 %copy-start.4 = (f32[6,4096]{1,0:T(8,128)S(1)}, f32[6,4096]{1,0:T(8,128)}, u32[]{:S(2)}) copy-start(f32[6,4096]{1,0:T(8,128)} %param.24) | copy-start | bytes 294916
  318.4 28.5 %copy-start.16 = (f32[4096]{0:T(1024)S(1)}, f32[4096]{0:T(1024)}, u32[]{:S(2)}) copy-start(f32[4096]{0:T(1024)} %param.19) | copy-start | bytes 49156
  318.4 28.5 %copy-start.20 = (f32[6,4096]{1,0:T(8,128)S(1)}, f32[6,4096]{1,0:T(8,128)}, u32[]{:S(2)}) copy-start(f32[6,4096]{1,0:T(8,128)} %param.25) | copy-start | bytes 294916
  320.4 36.6 %all-to-all-start.1 = ((f32[128,1,640]{2,1,0:T(1,128)}), f32[128,1,640]{2,1,0:T(1,128)S(1)}, u32[]{:S(2)}, u32[]{:S(2)}) async-start(f32[128,1,640]{2,1,0:T(1,128)} %reshape.485), calls=%async_computation.1 | async-start | bytes 655360 | tf_op jit(solution)/shard_map/all_to_all | solution.py:258
  408.2 3.7 copy-start.22
where the time goes:
time: 421 us; the launch traced here: 413 us
  local copies, waits for them, and re-layouts  186 us (44%)
  other arithmetic  143 us (34%)
  starting transfers between devices  61.6 us (15%)
  waiting for transfers between devices  20.3 us (5%)
    gather x2, local copies, waits for them, and re-layouts, shards(): beside = extended[:, local_ids]  97.7 us
    scatter x2, local copies, waits for them, and re-layouts, shards(): buffer.at[:, :, :, shaft_holding_position.reshape(-1)].set(by_block)  58.9 us
    scatter-add x1, other arithmetic, shards(): jax.ops.segment_sum(values_row, safe_ids, cell_count + 1)  46.4 us
    scatter-add x1, other arithmetic, shards(): jax.ops.segment_sum(jnp.ones(safe_ids.shape, jnp.float32), safe_ids, cell...  46.2 us
    all_to_all x1, starting transfers between devices, shards(): lax.all_to_all(joint_layout, ('grp', 'dom'), split_axis=0, concat_axis=0,...  24.9 us
    ppermute x5, starting transfers between devices, padded_2(): lax.ppermute(tail, axis, [(i, (i + 1) % count) for i in range(ends)])  16.9 us
    add x16, other arithmetic, element_forces(): forces[corner] + float(table_x[qpoint, corner]) * flux_x  16.7 us
    all_to_all x1, starting transfers between devices, shards(): lax.all_to_all(outgoing, 'dom', split_axis=1, concat_axis=1, tiled=True)  11.3 us
  transfers between devices with their start and end apart: 12, of which 4 were waited for; matrix products, arithmetic and copies ran while one was open for 43% of the time, Pallas kernels for 0%

commit v1 on v0

v1 whole, which is shorter than its diff:
```python
import math

import jax
import jax.numpy as jnp
from jax import lax
from jax.experimental import pallas as pl
from jax.experimental.pallas import tpu as pltpu
from jax.sharding import PartitionSpec as P

KAPPA = 1.0 / math.sqrt(3.0)
EPS_RATE = 0.01
LOG2E = math.log2(math.e)
SCALE = 4096.0
LAYERS = 20
LEVELS = 21
FIELDS = 24
PAIRS = 12
BLOCK_ROWS = 40
MSG_ROWS = 136
SPLITS = 2
f32 = jnp.float32
bf16 = jnp.bfloat16
PARAMS = pltpu.CompilerParams(vmem_limit_bytes=32 * 1024 * 1024)


def lanes_of(table, index):
    return jnp.take_along_axis(table, index, axis=1, mode="promise_in_bounds")


def iota(shape, dim):
    return lax.broadcasted_iota(jnp.int32, shape, dim)


def row_of(ref, row, rows):
    return jnp.broadcast_to(ref[pl.ds(row, 1), :], (rows, 128))


def halves(first, second, lane):
    even = jnp.where(lane < 64, first, pltpu.roll(second, 64, 1))
    odd = jnp.where(lane < 64, pltpu.roll(first, 64, 1), second)
    return even, odd


def pack_kernel(ice, heat, slope, drag, donor, shaft, prior, out, near, far, own):
    g = lax.axis_index("grp")
    d = lax.axis_index("dom")
    ids = jnp.concatenate(
        [donor[0, g, pl.ds(0, 16, stride=2), :], donor[0, g, pl.ds(1, 16, stride=2), :]], axis=1
    )
    ids = jnp.maximum(ids, 0)
    high = ids >> 7
    low = ids & 127
    lane = iota((16, 128), 1)

    def table(field, k):
        if field == 0:
            part = ice[k : k + 1, :]
        elif field < 3:
            part = slope[field - 1 : field, 128 * k : 128 * k + 128]
        elif field == 3:
            part = drag[k : k + 1, :]
        else:
            part = heat[field - 4 : field - 3, 128 * k : 128 * k + 128]
        return jnp.broadcast_to(part, (16, 128))

    for pair0 in range(0, PAIRS, 3):
        pairs = range(pair0, pair0 + 3)
        fields = [p for p in pairs] + [p + PAIRS for p in pairs]
        found = {f: jnp.zeros((16, 128), f32) for f in fields}
        for k in range(32):
            here = high == k
            for f in fields:
                found[f] = jnp.where(here, lanes_of(table(f, k), low), found[f])
        for p in pairs:
            even, odd = halves(found[p], found[p + PAIRS], lane)
            out[pl.ds(12 + p, 16, stride=80), :] = even
            out[pl.ds(40 + p, 16, stride=80), :] = even
            out[pl.ds(64 + p, 15, stride=80), :] = even[1:]
            out[pl.ds(52 + p, 16, stride=80), :] = odd
            out[pl.ds(24 + p, 16, stride=80), :] = odd
            out[pl.ds(80 + p, 15, stride=80), :] = odd[:15]
    out[0:12, :] = jnp.zeros((12, 128), f32)
    out[31 * 40 + 24 : 31 * 40 + 36, :] = jnp.zeros((12, 128), f32)
    for k in range(32):
        out[40 * k + 36 : 40 * k + 40, :] = jnp.zeros((4, 128), f32)

    def message(msg, row0, chunk0):
        for c in range(2):
            for z in range(LEVELS):
                at = 2 * (c * LEVELS + z)
                msg[at : at + 2, :] = prior[c, z, row0 : row0 + 2, :]
        msg[84:86, :] = shaft[row0 : row0 + 2, :].astype(f32)
        msg[86:88, :] = jnp.zeros((2, 128), f32)
        for i in range(6):
            msg[88 + 8 * i : 96 + 8 * i, :] = own[i, chunk0 : chunk0 + 8, :]

    own[0] = ice[...]
    for part in range(4):

        @pl.when(g == part)
        def _():
            for i in range(5):
                layer = 5 * part + i
                for k in range(32):
                    own[i + 1, k : k + 1, :] = heat[layer : layer + 1, 128 * k : 128 * k + 128]

    even_device = d % 2 == 0

    @pl.when(even_device)
    def _():
        message(near, 2, 24)
        message(far, 0, 0)

    @pl.when(jnp.logical_not(even_device))
    def _():
        message(near, 0, 0)
        message(far, 2, 24)


def advect_kernel(own, adjacent, ratio, mean_speed, tier_speed, near, far, depth_out, heat_out, ext):
    d = lax.axis_index("dom")
    even_device = d % 2 == 0
    for i in range(6):
        a = near[88 + 8 * i : 96 + 8 * i, :]
        b = far[88 + 8 * i : 96 + 8 * i, :]
        ext[i, 0:8, :] = jnp.where(even_device, b, a)
        ext[i, 40:48, :] = jnp.where(even_device, a, b)
        ext[i, 8:40, :] = own[i]

    @pl.loop(0, 32)
    def _(k):
        span = pl.ds(pl.multiple_of(128 * k, 128), 128)
        cell = adjacent[:, span] - (d * 4096 - 1024)
        low = cell & 127
        turn = (cell >> 7) - k
        beside = [jnp.zeros((6, 128), f32) for _ in range(6)]
        for r in range(17):
            here = turn == r
            for i in range(6):
                rows = jnp.broadcast_to(ext[i, pl.ds(k + r, 1), :], (6, 128))
                beside[i] = jnp.where(here, lanes_of(rows, low), beside[i])
        weight = ratio[:, span]
        for i in range(6):
            here = ext[i, pl.ds(k + 8, 1), :]
            speed = mean_speed[:, span] if i == 0 else tier_speed[i - 1, :, span]
            flow = weight * (jnp.maximum(speed, 0.0) * here + jnp.minimum(speed, 0.0) * beside[i])
            result = here - jnp.sum(flow, axis=0, keepdims=True)
            if i == 0:
                depth_out[pl.ds(k, 1), :] = result
            else:
                heat_out[i - 1 : i, span] = result


def column_kernel(arrived, shaft, near, far, prior, geo, vext, edge, slots):
    d = lax.axis_index("dom")
    even_device = d % 2 == 0
    row = iota((8, 128), 0)
    lane = iota((8, 128), 1)

    def sides(start, count):
        a = near[start : start + count, :]
        b = far[start : start + count, :]
        return jnp.where(even_device, b, a), jnp.where(even_device, a, b)

    left, right = sides(84, 2)
    slots[0:2, :] = left.astype(jnp.int32)
    slots[2:6, :] = shaft[...]
    slots[6:8, :] = right.astype(jnp.int32)
    slot = slots[...]
    owner = slot >> 6
    low = slot & 63
    low2 = low + 64
    found = [jnp.zeros((8, 128), f32) for _ in range(FIELDS)]
    upper = row < 2
    middle = row < 6
    for p in range(32):
        here = owner == p
        for f in range(PAIRS):
            at = BLOCK_ROWS * p + f
            rows = jnp.where(
                upper,
                row_of(arrived, at, 8),
                jnp.where(middle, row_of(arrived, at + 12, 8), row_of(arrived, at + 24, 8)),
            )
            found[f] = jnp.where(here, lanes_of(rows, low), found[f])
            found[f + PAIRS] = jnp.where(here, lanes_of(rows, low2), found[f + PAIRS])
    first = jnp.where(d == 0, 2, 0)
    last = jnp.where(d == lax.axis_size("dom") - 1, 5, 7)
    inside = jnp.logical_and(row >= first, row <= last)
    found = [jnp.where(inside, value, 0.0) for value in found]
    load_u = -(found[0] * found[1]) * SCALE
    load_v = -(found[0] * found[2]) * SCALE
    friction = found[3] * SCALE
    geo[0] = found[0]
    geo[1] = load_u
    geo[2] = load_v
    geo[3] = friction
    for l in range(LAYERS):
        geo[4 + l] = found[4 + l]
    for cz in range(2 * LEVELS):
        left, right = sides(2 * cz, 2)
        vext[cz, 0:2, :] = left
        vext[cz, 2:6, :] = prior[cz // LEVELS, cz % LEVELS]
        vext[cz, 6:8, :] = right
    group = lane // LEVELS
    pick = jnp.where(group < 2, group, jnp.where(group < 4, 124 + group, 0))
    level = lane - group * LEVELS
    for c in range(2):
        value = jnp.zeros((8, 128), f32)
        for z in range(LEVELS):
            value = jnp.where(level == z, lanes_of(vext[c * LEVELS + z], pick), value)
        edge[8 * c : 8 * c + 8, :] = value
    value = jnp.zeros((8, 128), f32)
    for l in range(LAYERS):
        value = jnp.where(level == l, lanes_of(found[4 + l], pick), value)
    edge[16:24, :] = value
    edge[24:32, :] = lanes_of(found[0], pick)
    edge[32:40, :] = lanes_of(load_u, pick)
    edge[40:48, :] = lanes_of(load_v, pick)
    edge[48:56, :] = jnp.where(level == 0, lanes_of(friction, pick), 0.0)


def interpolate(a, b):
    diff = b - a
    total = a + b
    part = KAPPA * diff
    return diff, total - part, total + part


def spread(a, b):
    total = a + b
    part = KAPPA * (a - b)
    return total, part


def spread_square(a, b):
    total = (1.0 + KAPPA * KAPPA) * (a + b)
    part = (2.0 * KAPPA) * (a - b)
    return total + part, total - part


def up_x(value):
    return pltpu.roll(value, 7, 0)


def down_x(value):
    return pltpu.roll(value, 1, 0)


def level_terms(value, value_y):
    dy, ya, yb = interpolate(value, value_y)
    _, along_y0, along_y1 = interpolate(dy, up_x(dy))
    along_x0, z00, z10 = interpolate(ya, up_x(ya))
    along_x1, z01, z11 = interpolate(yb, up_x(yb))
    return [along_x0, along_x1, along_y0, along_y1, z00, z01, z10, z11]


def element(low_u, top_u, low_v, top_v, hardness, inverse2, keep=None):
    def gradients(low, top):
        x = [interpolate(low[q], top[q])[1:] for q in (0, 1)]
        y = [interpolate(low[2 + q], top[2 + q])[1:] for q in (0, 1)]
        z = [top[4 + q] - low[4 + q] for q in range(4)]
        return x, y, z

    ux, uy, uz = gradients(low_u, top_u)
    vx, vy, vz = gradients(low_v, top_v)
    vertical = [
        (uz[q] * uz[q] + vz[q] * vz[q]) * (0.25 * inverse2) + EPS_RATE for q in range(4)
    ]
    vy2 = [[vy[a][b] * vy[a][b] for b in (0, 1)] for a in (0, 1)]
    ex, ey, ez = {}, {}, {}
    ev, eu, wx, wy = {}, {}, {}, {}

    def put(store, key, value):
        store[key] = value if key not in store else store[key] + value

    for qx in (0, 1):
        for qy in (0, 1):
            for qz in (0, 1):
                a = ux[qy][qz]
                b = vy[qx][qz]
                shear = uy[qx][qz] + vx[qy][qz]
                rate = (
                    a * (a + b) + vy2[qx][qz] + 0.25 * (shear * shear) + vertical[2 * qx + qy]
                )
                eta = jnp.exp2(hardness - jnp.log2(rate) * (1.0 / 3.0))
                if keep is not None:
                    eta = jnp.where(keep, eta, 0.0)
                put(ex, (qy, qz), eta)
                put(ey, (qx, qz), eta)
                put(ez, 2 * qx + qy, eta)
                put(ev, (qy, qz), eta * b)
                put(eu, (qx, qz), eta * a)
                w = eta * shear
                put(wx, (qy, qz), w)
                put(wy, (qx, qz), w)
    ez = [ez[q] * inverse2 for q in range(4)]
    lows, tops = [], []

    def add_spread(a, b):
        total, part = spread(a, b)
        lows.append(total + part)
        tops.append(total - part)

    def flux(e, g, s):
        half = (g + g) * e + s
        return half + half

    for q in (0, 1):
        add_spread(*[flux(ex[q, z], ux[q][z], ev[q, z]) for z in (0, 1)])
    for q in (0, 1):
        add_spread(wy[q, 0], wy[q, 1])
    for q in range(4):
        value = ez[q] * uz[q]
        lows.append(-value)
        tops.append(value)
    for q in (0, 1):
        add_spread(wx[q, 0], wx[q, 1])
    for q in (0, 1):
        add_spread(*[flux(ey[q, z], vy[q][z], eu[q, z]) for z in (0, 1)])
    for q in range(4):
        value = ez[q] * vz[q]
        lows.append(-value)
        tops.append(value)
    for q in (0, 1):
        a, b = spread_square(ex[q, 0], ex[q, 1])
        lows.append(a)
        tops.append(b)
    for q in (0, 1):
        a, b = spread_square(ey[q, 0], ey[q, 1])
        lows.append(a)
        tops.append(b)
    lows += ez
    tops += ez
    return lows, tops


def node_parts(acc):
    results = []
    for c in (0, 1):
        x0, x1, y0, y1, z00, z01, z10, z11 = acc[8 * c : 8 * c + 8]
        total, part = spread(y0, y1)
        hd = (total + part) + down_x(total - part)
        both = []
        for along, a, b in ((x0, z00, z10), (x1, z01, z11)):
            total, part = spread(a, b)
            part = part - along
            both.append((total + part) + down_x(total - part))
        total, part = spread(both[0], both[1])
        part = part - hd
        results.append((total + part, total - part))
    x0, x1, y0, y1, z00, z01, z10, z11 = acc[16:24]
    hx = [x0 + down_x(x0), x1 + down_x(x1)]
    a, b = spread_square(y0, y1)
    hy = a + down_x(b)
    hz = []
    for za, zb in ((z00, z10), (z01, z11)):
        a, b = spread_square(za, zb)
        hz.append(a + down_x(b))
    a, b = spread_square(4.0 * hx[0] + hz[0], 4.0 * hx[1] + hz[1])
    results.append((a + hy, b + hy))
    hy4 = 4.0 * hy
    a, b = spread_square(hx[0] + hz[0], hx[1] + hz[1])
    results.append((a + hy4, b + hy4))
    return results


def ice_kernel(geo, vext, edges, shaft, out_v, send, hard, first, second, means):
    g = lax.axis_index("grp")
    d = lax.axis_index("dom")
    groups = lax.axis_size("grp")
    domains = lax.axis_size("dom")
    row = iota((8, 128), 0)
    lane = iota((8, 128), 1)
    group = lane // LEVELS
    level = lane - group * LEVELS

    def at_lane(value, index):
        return lanes_of(value, jnp.full((8, 128), index, jnp.int32))

    base = 56 * g
    before = pl.multiple_of(jnp.maximum(base - 56, 0), 8)
    after = pl.multiple_of(jnp.minimum(base + 56, 56 * (groups - 1)), 8)

    def edge_field(i):
        own = edges[pl.ds(pl.multiple_of(base + 8 * i, 8), 8), :]
        left = jnp.where(g > 0, edges[pl.ds(before + 8 * i, 8), :], 0.0)
        right = jnp.where(g < groups - 1, edges[pl.ds(after + 8 * i, 8), :], 0.0)
        return jnp.where(
            lane < 42,
            pltpu.roll(left, 86, 1),
            jnp.where(
                lane < 63,
                pltpu.roll(own, 42, 1),
                jnp.where(lane < 84, own, pltpu.roll(right, 84, 1)),
            ),
        )

    edge_u, edge_v, edge_t, edge_h, edge_fu, edge_fv, edge_b = [edge_field(i) for i in range(7)]

    def up_y(value, beyond):
        return jnp.where(lane == 127, beyond, pltpu.roll(value, 127, 1))

    def edge_up(value):
        return pltpu.roll(value, 107, 1)

    def corners(value, value_y):
        pair = value + value_y
        return pair + up_x(pair)

    def geometry(depth4):
        dz = depth4 * (0.25 / LAYERS)
        dz = jnp.where(dz > 0.0, dz, 1.0)
        inverse = 0.25 / dz
        return jnp.log2(dz * 16.0), inverse * inverse

    depth = geo[0]
    main_log, main_inv2 = geometry(corners(depth, up_y(depth, at_lane(edge_h, 84))))
    edge_log, edge_inv2 = geometry(corners(edge_h, edge_up(edge_h)))
    edge_hard = edge_log - (0.25 * LOG2E) * corners(edge_t, edge_up(edge_t))

    @pl.loop(0, LAYERS)
    def _(l):
        warm = geo[4 + l]
        hard[l] = main_log - (0.25 * LOG2E) * corners(warm, up_y(warm, at_lane(edge_t, 84 + l)))

    load_u = geo[1]
    load_v = geo[2]
    friction = geo[3]
    not_top = jnp.logical_and(level != LAYERS, lane < 6 * LEVELS)
    first_row = jnp.where(d == 0, 2, 1)
    last_row = jnp.where(d == domains - 1, 5, 6)
    inside = jnp.logical_and(row >= first_row, row <= last_row)
    edge_inside = jnp.logical_and(
        inside,
        jnp.logical_or(
            jnp.logical_and(group == 1, g > 0),
            jnp.logical_and(group == 4, g < groups - 1),
        ),
    )

    def edge_parts(u, v):
        low_u = level_terms(u, edge_up(u))
        low_v = level_terms(v, edge_up(v))
        top_u = [pltpu.roll(t, 127, 1) for t in low_u]
        top_v = [pltpu.roll(t, 127, 1) for t in low_v]
        lows, tops = element(low_u, top_u, low_v, top_v, edge_hard, edge_inv2, not_top)
        acc = [a + pltpu.roll(b, 1, 1) for a, b in zip(lows, tops)]
        return node_parts(acc)

    def stepped(value, load, force, diagonal, drag):
        return value + 0.5 * (load - force - drag * value) / (diagonal + drag)

    def sweep(source, target, eu, ev, parts, keep):
        beyond = [part[1] for part in parts]

        def node(z, acc, drag):
            results = node_parts(acc)
            fu, fv, du, dv = [
                a + jnp.where(lane == 0, at_lane(e, 42 - LEVELS + z), pltpu.roll(b, 1, 1))
                for (a, b), e in zip(results, beyond)
            ]
            u = stepped(source[z], load_u, fu, du, drag)
            v = stepped(source[LEVELS + z], load_v, fv, dv, drag)
            target[z] = jnp.where(keep, u, 0.0)
            target[LEVELS + z] = jnp.where(keep, v, 0.0)

        def terms(z):
            u = source[z]
            v = source[LEVELS + z]
            return level_terms(u, up_y(u, at_lane(eu, 84 + z))) + level_terms(
                v, up_y(v, at_lane(ev, 84 + z))
            )

        def body(z, carry):
            low, tops = carry[:16], carry[16:]
            top = terms(z + 1)
            lows, next_tops = element(low[:8], top[:8], low[8:], top[8:], hard[z], main_inv2)
            node(z, [a + b for a, b in zip(lows, tops)], jnp.where(z == 0, friction, 0.0))
            return (*top, *next_tops)

        zero = jnp.zeros((8, 128), f32)
        carry = lax.fori_loop(0, LAYERS, body, (*terms(0), *([zero] * 24)))
        node(LAYERS, list(carry[16:]), zero)

    parts = edge_parts(edge_u, edge_v)
    sweep(vext, first, edge_u, edge_v, parts, inside)

    def edge_final(c, value, load):
        (fa, fb), (da, db) = parts[c], parts[2 + c]
        force = fa + pltpu.roll(fb, LEVELS, 1)
        diagonal = da + pltpu.roll(db, LEVELS, 1)
        return jnp.where(edge_inside, stepped(value, load, force, diagonal, edge_b), 0.0)

    edge_u = edge_final(0, edge_u, edge_fu)
    edge_v = edge_final(1, edge_v, edge_fv)
    for z in range(LEVELS):
        here = lane == 42 + z
        edge_u = jnp.where(here, at_lane(first[z], 0), edge_u)
        edge_v = jnp.where(here, at_lane(first[LEVELS + z], 0), edge_v)
    parts = edge_parts(edge_u, edge_v)
    own_rows = jnp.logical_and(row >= 2, row < 6)
    sweep(first, second, edge_u, edge_v, parts, own_rows)
    for c in range(2):
        for z in range(LEVELS):
            out_v[c, z] = second[c * LEVELS + z, 2:6, :]
    for c in range(2):
        for l in range(LAYERS):
            at = c * LEVELS + l
            means[8 * (c * LAYERS + l) : 8 * (c * LAYERS + l) + 8, :] = 0.5 * (
                second[at] + second[at + 1]
            )

    slot_row = iota((16, 128), 0)
    place = iota((16, 128), 1).astype(f32)
    low_row = iota((128, 128), 0)
    where_from = jnp.zeros((32, 128), f32)
    for x in range(4):
        slot = shaft[x : x + 1, :]
        here = slot_row == jnp.broadcast_to(slot >> 7, (16, 128))
        left = jnp.concatenate(
            [jnp.where(here, float(x), 0.0), jnp.where(here, place, 0.0)], axis=0
        )
        right = jnp.where(low_row == jnp.broadcast_to(slot & 127, (128, 128)), 1.0, 0.0)
        where_from = where_from + lax.dot_general(
            left.astype(bf16),
            right.astype(bf16),
            (((1,), (1,)), ((), ())),
            preferred_element_type=f32,
        )
    from_x = where_from[0:16].astype(jnp.int32)
    from_y = where_from[16:32].astype(jnp.int32) & 127
    lane16 = iota((16, 128), 1)
    here = [from_x == x for x in range(4)]
    send[...] = jnp.zeros(send.shape, f32)
    for l in range(LAYERS):
        pair = []
        for c in range(2):
            at = 8 * (c * LAYERS + l) + 2
            value = lanes_of(row_of(means, at, 16), from_y)
            for x in range(1, 4):
                value = jnp.where(here[x], lanes_of(row_of(means, at + x, 16), from_y), value)
            pair.append(value)
        even, odd = halves(pair[0], pair[1], lane16)
        start = (l // 5) * 256 + l % 5
        send[pl.ds(start, 16, stride=16), :] = even
        send[pl.ds(start + 8, 16, stride=16), :] = odd


def total_kernel(arrived, donor, out, ids, left, right, sums):
    lane = iota((8, 128), 1)
    row = iota((8, 128), 0)
    row256 = iota((256, 128), 0)
    for g in range(4):
        ids[16 * g : 16 * g + 16, :] = jnp.concatenate(
            [donor[0, g, pl.ds(0, 16, stride=2), :], donor[0, g, pl.ds(1, 16, stride=2), :]],
            axis=1,
        )

    @pl.loop(0, 8)
    def _(step):
        for part in range(8):
            chunk = 8 * step + part
            span = slice(128 * part, 128 * part + 128)
            x = arrived[pl.ds(pl.multiple_of(16 * chunk, 16), 16), :]
            u, v = halves(x[:8], x[8:], lane)
            u = jnp.where(row < 5, u, jnp.where(row == 5, 1.0, 0.0))
            v = jnp.where(row < 5, v, 0.0)
            rest = jnp.concatenate([u, v], axis=0)
            values = []
            for s in range(SPLITS):
                piece = rest.astype(bf16)
                values.append(piece)
                rest = rest - piece.astype(f32)
            cell = ids[pl.ds(chunk, 1), :]
            high = jnp.broadcast_to(cell >> 8, (16, 128))
            low = jnp.broadcast_to(cell & 255, (256, 128))
            right[:, span] = jnp.where(row256 == low, 1.0, 0.0).astype(bf16)
            for h in range(16):
                here = jnp.where(high == h, 1.0, 0.0).astype(bf16)
                for s in range(SPLITS):
                    at = 16 * (SPLITS * h + s)
                    left[at : at + 16, span] = values[s] * here
        product = lax.dot_general(
            left[...], right[...], (((1,), (1,)), ((), ())), preferred_element_type=f32
        )

        @pl.when(step == 0)
        def _():
            sums[...] = product

        @pl.when(step > 0)
        def _():
            sums[...] += product

    for h in range(16):
        at = 16 * SPLITS * h
        total = sums[at : at + 16, :]
        for s in range(1, SPLITS):
            total = total + sums[at + 16 * s : at + 16 * s + 16, :]
        count = jnp.maximum(total[5:6, :], 1.0)
        span = slice(256 * h, 256 * h + 256)
        out[0, :, span] = total[0:5, :] / count
        out[1, :, span] = total[8:13, :] / count


def shape(*sizes):
    return jax.ShapeDtypeStruct(sizes, f32)


def near_pairs(count):
    even = [(i, i ^ 1) for i in range(count)]
    odd = []
    for i in range(1, count - 1, 2):
        odd += [(i, i + 1), (i + 1, i)]
    return even, odd


def shards(
    ice_depth,
    heat_state,
    elevation_slope_components,
    sliding_drag,
    adjacent_polygons,
    edge_timing_ratio,
    edge_average_normal_speed,
    tier_edge_normal_speed,
    position_donor_polygons,
    shaft_holding_position,
    prior_node_motion,
):
    ice = ice_depth.reshape(32, 128)
    drag = sliding_drag.reshape(32, 128)
    outgoing, near, far, own = pl.pallas_call(
        pack_kernel,
        out_shape=(
            shape(32 * BLOCK_ROWS, 128),
            shape(MSG_ROWS, 128),
            shape(MSG_ROWS, 128),
            shape(6, 32, 128),
        ),
        compiler_params=PARAMS,
        name="pack",
    )(
        ice,
        heat_state,
        elevation_slope_components,
        drag,
        position_donor_polygons,
        shaft_holding_position,
        prior_node_motion,
    )
    arrived = lax.all_to_all(outgoing, "dom", split_axis=0, concat_axis=0, tiled=True)
    even, odd = near_pairs(lax.axis_size("dom"))
    near = lax.ppermute(near, "dom", even)
    far = lax.ppermute(far, "dom", odd)
    geo, vext, edge = pl.pallas_call(
        column_kernel,
        out_shape=(shape(FIELDS, 8, 128), shape(2 * LEVELS, 8, 128), shape(56, 128)),
        scratch_shapes=[pltpu.VMEM((8, 128), jnp.int32)],
        compiler_params=PARAMS,
        name="columns",
    )(arrived, shaft_holding_position, near, far, prior_node_motion)
    edges = lax.all_gather(edge, "grp", axis=0, tiled=True)
    node_velocity, send = pl.pallas_call(
        ice_kernel,
        out_shape=(shape(2, LEVELS, 4, 128), shape(1024, 128)),
        scratch_shapes=[
            pltpu.VMEM((LAYERS, 8, 128), f32),
            pltpu.VMEM((2 * LEVELS, 8, 128), f32),
            pltpu.VMEM((2 * LEVELS, 8, 128), f32),
            pltpu.VMEM((2 * LAYERS * 8, 128), f32),
        ],
        compiler_params=PARAMS,
        name="velocity",
    )(geo, vext, edges, shaft_holding_position)
    back = lax.all_to_all(send, ("grp", "dom"), split_axis=0, concat_axis=0, tiled=True)
    depth, heat = pl.pallas_call(
        advect_kernel,
        out_shape=(shape(32, 128), shape(5, 4096)),
        scratch_shapes=[pltpu.VMEM((6, 48, 128), f32)],
        compiler_params=PARAMS,
        name="advect",
    )(
        own,
        adjacent_polygons,
        edge_timing_ratio,
        edge_average_normal_speed,
        tier_edge_normal_speed,
        near,
        far,
    )
    tier_motion = pl.pallas_call(
        total_kernel,
        out_shape=shape(2, 5, 4096),
        scratch_shapes=[
            pltpu.VMEM((64, 128), jnp.int32),
            pltpu.VMEM((256 * SPLITS, 1024), bf16),
            pltpu.VMEM((256, 1024), bf16),
            pltpu.VMEM((256 * SPLITS, 256), f32),
        ],
        compiler_params=PARAMS,
        name="totals",
    )(back, position_donor_polygons)
    return (depth.reshape(4096), heat, node_velocity, tier_motion)


def solution(mesh):
    in_specs = (
        P("dom"),
        P(None, "dom"),
        P(None, "dom"),
        P("dom"),
        P(None, "dom"),
        P(None, "dom"),
        P(None, "dom"),
        P("grp", None, "dom"),
        P("dom", None, None, None),
        P("dom", "grp"),
        P(None, None, "dom", "grp"),
    )
    out_specs = (P("dom"), P("grp", "dom"), P(None, None, "dom", "grp"), P(None, "grp", "dom"))
    return jax.shard_map(shards, mesh=mesh, in_specs=in_specs, out_specs=out_specs, check_vma=False)
```

time: 421 us -> 83.6 us (0.20); the launches traced: 413 us -> 83 us
  local copies, waits for them, and re-layouts: 186 us -> 6.41 us
  other arithmetic: 143 us -> 0 us
  starting transfers between devices: 61.6 us -> 18.1 us
  Pallas kernels: 0 us -> 32.4 us
  blocking collectives: 0 us -> 7.98 us
    gather x6 -> x0, local copies, waits for them, and re-layouts: 105 us -> none  [the longest x2 97.7 us: shards(): beside = extended[:, local_ids]]
    scatter-add x4 -> x0, other arithmetic: 92.7 us -> none  [the longest x1 46.4 us: shards(): jax.ops.segment_sum(values_row, safe_ids, cell_count + 1)]
    scatter x2 -> x0, local copies, waits for them, and re-layouts: 58.9 us -> none  [shards(): buffer.at[:, :, :, shaft_holding_position.reshape(-1)].set(by_block)]
    pallas_call x0 -> x5, Pallas kernels: none -> 32.4 us  [the longest x1 14.2 us: shards(): pl.pallas_call(ice_kernel, out_shape=(shape(2, LEVELS, 4, 128), shape(102...]
    ppermute x10 -> x2, starting transfers between devices: 25.3 us -> 1.96 us  [the longest x1 1.31 us: shards(): near = lax.ppermute(near, 'dom', even)]
    add x38 -> x0, other arithmetic: 20.7 us -> none  [the longest x16 16.7 us: element_forces(): forces[corner] + float(table_x[qpoint, corner]) * flux_x]
    all_to_all x2, starting transfers between devices: 36.2 us -> 16.1 us  [the longest x1 11.5 us: shards(): lax.all_to_all(outgoing, 'dom', split_axis=0, concat_axis=0, tiled=True)]
    another operation x19 -> x0, other arithmetic: 8.61 us -> none  [the longest x12 5.41 us: element_forces(): jnp.stack([visc_point * (4.0 * grad_x[0] + 2.0 * grad_y[1]), shear])]
  transfers between devices with their start and end apart: 12 -> 4, of which waited for: 4 -> 3; matrix products, arithmetic and copies ran while one was open for 43% -> 0% of each run, Pallas kernels for 0% -> 8%
where the time goes in v1:
time: 83.6 us; the launch traced here: 83 us
  Pallas kernels  32.4 us (39%)
  starting transfers between devices  18.1 us (22%)
  waiting for transfers between devices  17.4 us (21%)
  blocking collectives  7.98 us (10%)
  local copies, waits for them, and re-layouts  6.41 us (8%)
    pallas_call x1, Pallas kernels, shards(): pl.pallas_call(ice_kernel, out_shape=(shape(2, LEVELS, 4, 128), shape(102...  14.2 us
    all_to_all x1, starting transfers between devices, shards(): lax.all_to_all(outgoing, 'dom', split_axis=0, concat_axis=0, tiled=True)  11.5 us
    all_gather x1, blocking collectives, shards(): edges = lax.all_gather(edge, 'grp', axis=0, tiled=True)  7.98 us
    pallas_call x1, Pallas kernels, shards(): pl.pallas_call(advect_kernel, out_shape=(shape(32, 128), shape(5, 4096)),...  6.83 us
    all_to_all x1, waiting for transfers between devices, shards(): lax.all_to_all(send, ('grp', 'dom'), split_axis=0, concat_axis=0, tiled=T...  6.82 us
    unnamed x27, local copies, waits for them, and re-layouts  6.41 us
    all_to_all x1, waiting for transfers between devices, shards(): lax.all_to_all(outgoing, 'dom', split_axis=0, concat_axis=0, tiled=True)  5.55 us
    pallas_call x1, Pallas kernels, shards(): pl.pallas_call(total_kernel, out_shape=shape(2, 5, 4096), scratch_shapes=...  5.47 us
  transfers between devices with their start and end apart: 4, of which 3 were waited for; matrix products, arithmetic and copies ran while one was open for 0% of the time, Pallas kernels for 8%

profile of v1, /device:TPU:1, one launch (start us, length us, event | category | flops | bytes accessed | tf_op | source)
XLA Modules:
  0.0 83.0 jit_solution(15396150473569978256)
XLA Ops:
  0.6 0.0 copy-start.10
  0.6 0.7 copy-done.10
  1.3 0.0 copy-start.1
  1.3 1.0 %copy-done.1 = f32[20,4096]{1,0:T(8,128)S(1)} copy-done((f32[20,4096]{1,0:T(8,128)S(1)}, f32[20,4096]{1,0:T(8,128)}, u32[]{:S(2)}) %copy-start.1) | copy-done | bytes 327704
  2.3 0.0 copy-start.2
  2.3 0.9 %copy-done.2 = f32[2,21,4,128]{3,2,1,0:T(4,128)S(1)} copy-done((f32[2,21,4,128]{3,2,1,0:T(4,128)S(1)}, f32[2,21,4,128]{3,2,1,0:T(4,128)}, u32[]{:S(2)}) %copy-start.2) | copy-done | bytes 86040
  3.2 0.0 copy-start.4
  3.2 0.8 %copy-done.4 = s32[1,4,32,64]{3,2,1,0:T(8,128)S(1)} copy-done((s32[1,4,32,64]{3,2,1,0:T(8,128)S(1)}, s32[1,4,32,64]{3,2,1,0:T(8,128)}, u32[]{:S(2)}) %copy-start.4) | copy-done | bytes 32792
  4.0 0.0 copy-start.9
  4.0 0.8 copy-done.9
  4.8 0.0 copy-start.11
  4.8 0.7 copy-done.11
  5.5 0.0 copy-start.12
  5.5 0.7 copy-done.12
  6.2 4.8 %pack.1 = (f32[1280,128]{1,0:T(8,128)}, f32[136,128]{1,0:T(8,128)S(1)}, f32[136,128]{1,0:T(8,128)S(1)}, f32[6,32,128]{2,1,0:T(8,128)S(1)}) custom-call(f32[32,128]{1,0:T(8,128)S(1)} %bitcast.9, f32[20,4096]{1,0:T(8,128)S(1)} %copy-done.1, f32[2,4096]{1,0:T(2,128)S(1)} %copy-done.9, f32[32,128]{1,0:T(8,128)S(1)} %bitcast.10, s32[1,4,32,64]{3,2,1,0:T(8,128)S(1)} %copy-done.4, ...), custom_call_target="tpu_custom_call" | custom-call | tf_op jit(solution)/shard_map/pack/pallas_call | solution.py:634
  11.0 0.0 copy-start.3
  11.0 11.5 %all-to-all-start = ((f32[32,40,128]{2,1,0:T(8,128)}), f32[32,40,128]{2,1,0:T(8,128)S(1)}, u32[]{:S(2)}, u32[]{:S(2)}) async-start(f32[32,40,128]{2,1,0:T(8,128)} %bitcast.3), calls=%async_computation | async-start | bytes 1310720 | tf_op jit(solution)/shard_map/all_to_all | solution.py:653
  22.5 1.3 %collective-permute-start = (f32[136,128]{1,0:T(8,128)S(1)}, f32[136,128]{1,0:T(8,128)S(1)}, u32[]{:S(2)}, u32[]{:S(2)}) collective-permute-start(f32[136,128]{1,0:T(8,128)S(1)} %get-tuple-element.16), channel_id=1, source_target_pairs={{0,1},{1,0},{2,3},{3,2},{4,5},{5,4},{6,7},{7,6},{8,9},{9,8},{10,11... | collective-permute-start | bytes 208904 | tf_op jit(solution)/shard_map/ppermute | solution.py:655
  23.8 0.7 collective-permute-start.1
  24.5 5.0 %collective-permute-done.near = f32[136,128]{1,0:T(8,128)S(1)} collective-permute-done((f32[136,128]{1,0:T(8,128)S(1)}, f32[136,128]{1,0:T(8,128)S(1)}, u32[]{:S(2)}, u32[]{:S(2)}) %collective-permute-start) | collective-permute-done | bytes 69664 | tf_op jit(solution)/shard_map/ppermute | solution.py:655
  29.5 0.0 collective-permute-done.1.far
  29.5 5.5 %all-to-all-done = f32[32,40,128]{2,1,0:T(8,128)S(1)} async-done(((f32[32,40,128]{2,1,0:T(8,128)}), f32[32,40,128]{2,1,0:T(8,128)S(1)}, u32[]{:S(2)}, u32[]{:S(2)}) %all-to-all-start) | async-done | bytes 655392 | tf_op jit(solution)/shard_map/all_to_all | solution.py:653
  35.1 0.0 copy-done.3
  35.1 1.1 %columns.1 = (f32[24,8,128]{2,1,0:T(8,128)S(1)}, f32[42,8,128]{2,1,0:T(8,128)S(1)}, f32[56,128]{1,0:T(8,128)S(1)}) custom-call(f32[1280,128]{1,0:T(8,128)S(1)} %bitcast.7, s32[4,128]{1,0:T(4,128)S(1)} %copy-done.10, f32[136,128]{1,0:T(8,128)S(1)} %collective-permute-done.near, f32[136,128]{1,0:T(8,128)S(1)} %collective-permute-done.1.far, ...), custom_call_target="tpu_custom_call" | custom-call | tf_op jit(solution)/shard_map/columns/pallas_call | solution.py:657
  36.1 8.0 %all_gather.3.edges = f32[224,128]{1,0:T(8,128)S(1)} all-gather(f32[56,128]{1,0:T(8,128)S(1)} %get-tuple-element.23), channel_id=1, replica_groups=mesh['grp'=4,'dom'=32] {'grp'}, dimensions={0}, use_global_device_ids=true | all-gather | bytes 143360 | tf_op jit(solution)/shard_map/all_gather | solution.py:664
  44.1 0.0 copy-start
  44.1 14.2 %velocity.1 = (f32[2,21,4,128]{3,2,1,0:T(4,128)}, f32[1024,128]{1,0:T(8,128)}) custom-call(f32[24,8,128]{2,1,0:T(8,128)S(1)} %get-tuple-element.21.geo, f32[42,8,128]{2,1,0:T(8,128)S(1)} %get-tuple-element.22.vext, f32[224,128]{1,0:T(8,128)S(1)} %all_gather.3.edges, s32[4,128]{1,0:T(4,128)S(1)} %copy-done.10), custom_call_target="tpu_custom_call" | custom-call | tf_op jit(solution)/shard_map/velocity/pallas_call | solution.py:665
  58.4 0.0 copy-start.6
  58.4 0.0 copy-start.7
  58.4 0.0 copy-start.8
  58.4 4.7 %all-to-all-start.1 = ((f32[128,8,128]{2,1,0:T(8,128)}), f32[128,8,128]{2,1,0:T(8,128)S(1)}, u32[]{:S(2)}, u32[]{:S(2)}) async-start(f32[128,8,128]{2,1,0:T(8,128)} %bitcast.5), calls=%async_computation.1 | async-start | bytes 1048576 | tf_op jit(solution)/shard_map/all_to_all | solution.py:677
  63.0 0.0 copy-done
  63.0 0.0 copy-done.6
  63.1 0.0 copy-done.7
  63.1 0.0 copy-done.8
  63.1 0.0 copy-start.5
  63.1 6.8 %advect.1 = (f32[32,128]{1,0:T(8,128)}, f32[5,4096]{1,0:T(8,128)}) custom-call(f32[6,32,128]{2,1,0:T(8,128)S(1)} %get-tuple-element.15.own, s32[6,4096]{1,0:T(8,128)S(1)} %copy-done.6, f32[6,4096]{1,0:T(8,128)S(1)} %copy-done.7, f32[6,4096]{1,0:T(8,128)S(1)} %copy-done.8, f32[5,6,4096]{2,1,0:T(8,128)S(1)} %copy-done, ...), custom_call_target="tpu_custom_call" | custom-call | tf_op jit(solution)/shard_map/advect/pallas_call | solution.py:678
  69.9 6.8 %all-to-all-done.1 = f32[128,8,128]{2,1,0:T(8,128)S(1)} async-done(((f32[128,8,128]{2,1,0:T(8,128)}), f32[128,8,128]{2,1,0:T(8,128)S(1)}, u32[]{:S(2)}, u32[]{:S(2)}) %all-to-all-start.1) | async-done | bytes 524320 | tf_op jit(solution)/shard_map/all_to_all | solution.py:677
  76.7 0.0 copy-done.5
  76.7 5.5 %totals.1 = f32[2,5,4096]{2,1,0:T(8,128)S(1)} custom-call(f32[1024,128]{1,0:T(8,128)S(1)} %bitcast.8, s32[1,4,32,64]{3,2,1,0:T(8,128)S(1)} %copy-done.5), custom_call_target="tpu_custom_call" | custom-call | tf_op jit(solution)/shard_map/totals/pallas_call | solution.py:693
  82.2 0.8 copy.15
Async XLA Ops:
  0.6 0.7 copy-start.10
  1.3 1.0 %copy-start.1 = (f32[20,4096]{1,0:T(8,128)S(1)}, f32[20,4096]{1,0:T(8,128)}, u32[]{:S(2)}) copy-start(f32[20,4096]{1,0:T(8,128)} %heat.1) | copy-start | bytes 983044
  2.3 0.9 %copy-start.2 = (f32[2,21,4,128]{3,2,1,0:T(4,128)S(1)}, f32[2,21,4,128]{3,2,1,0:T(4,128)}, u32[]{:S(2)}) copy-start(f32[2,21,4,128]{3,2,1,0:T(4,128)} %prior.3) | copy-start | bytes 258052
  3.2 0.8 %copy-start.4 = (s32[1,4,32,64]{3,2,1,0:T(8,128)S(1)}, s32[1,4,32,64]{3,2,1,0:T(8,128)}, u32[]{:S(2)}) copy-start(s32[1,4,32,64]{3,2,1,0:T(8,128)} %donor.3) | copy-start | bytes 98308
  4.0 0.8 copy-start.9
  4.8 0.7 copy-start.11
  5.5 0.7 copy-start.12
  11.0 24.1 %copy-start.3 = (f32[2,21,4,128]{3,2,1,0:T(4,128)S(1)}, f32[2,21,4,128]{3,2,1,0:T(4,128)}, u32[]{:S(2)}) copy-start(f32[2,21,4,128]{3,2,1,0:T(4,128)} %prior.3) | copy-start | bytes 258052
  11.0 24.1 %all-to-all-start = ((f32[32,40,128]{2,1,0:T(8,128)}), f32[32,40,128]{2,1,0:T(8,128)S(1)}, u32[]{:S(2)}, u32[]{:S(2)}) async-start(f32[32,40,128]{2,1,0:T(8,128)} %bitcast.3), calls=%async_computation | async-start | bytes 1310720 | tf_op jit(solution)/shard_map/all_to_all | solution.py:653
  22.5 7.0 %collective-permute-start = (f32[136,128]{1,0:T(8,128)S(1)}, f32[136,128]{1,0:T(8,128)S(1)}, u32[]{:S(2)}, u32[]{:S(2)}) collective-permute-start(f32[136,128]{1,0:T(8,128)S(1)} %get-tuple-element.16), channel_id=1, source_target_pairs={{0,1},{1,0},{2,3},{3,2},{4,5},{5,4},{6,7},{7,6},{8,9},{9,8},{10,11... | collective-permute-start | bytes 208904 | tf_op jit(solution)/shard_map/ppermute | solution.py:655
  23.8 5.7 %collective-permute-start.1 = (f32[136,128]{1,0:T(8,128)S(1)}, f32[136,128]{1,0:T(8,128)S(1)}, u32[]{:S(2)}, u32[]{:S(2)}) collective-permute-start(f32[136,128]{1,0:T(8,128)S(1)} %get-tuple-element.17), channel_id=1, source_target_pairs={{1,2},{2,1},{3,4},{4,3},{5,6},{6,5},{7,8},{8,7},{9,10},{10,9},{11,... | collective-permute-start | bytes 208904 | tf_op jit(solution)/shard_map/ppermute | solution.py:656
  44.1 18.9 %copy-start = (f32[5,6,4096]{2,1,0:T(8,128)S(1)}, f32[5,6,4096]{2,1,0:T(8,128)}, u32[]{:S(2)}) copy-start(f32[5,6,4096]{2,1,0:T(8,128)} %tier_speed.1) | copy-start | bytes 1474564
  58.4 4.7 %copy-start.6 = (s32[6,4096]{1,0:T(8,128)S(1)}, s32[6,4096]{1,0:T(8,128)}, u32[]{:S(2)}) copy-start(s32[6,4096]{1,0:T(8,128)} %adjacent.1) | copy-start | bytes 294916
  58.4 4.7 %copy-start.7 = (f32[6,4096]{1,0:T(8,128)S(1)}, f32[6,4096]{1,0:T(8,128)}, u32[]{:S(2)}) copy-start(f32[6,4096]{1,0:T(8,128)} %ratio.1) | copy-start | bytes 294916
  58.4 4.7 %copy-start.8 = (f32[6,4096]{1,0:T(8,128)S(1)}, f32[6,4096]{1,0:T(8,128)}, u32[]{:S(2)}) copy-start(f32[6,4096]{1,0:T(8,128)} %mean_speed.1) | copy-start | bytes 294916
  58.4 18.4 %all-to-all-start.1 = ((f32[128,8,128]{2,1,0:T(8,128)}), f32[128,8,128]{2,1,0:T(8,128)S(1)}, u32[]{:S(2)}, u32[]{:S(2)}) async-start(f32[128,8,128]{2,1,0:T(8,128)} %bitcast.5), calls=%async_computation.1 | async-start | bytes 1048576 | tf_op jit(solution)/shard_map/all_to_all | solution.py:677
  63.1 13.7 %copy-start.5 = (s32[1,4,32,64]{3,2,1,0:T(8,128)S(1)}, s32[1,4,32,64]{3,2,1,0:T(8,128)}, u32[]{:S(2)}) copy-start(s32[1,4,32,64]{3,2,1,0:T(8,128)} %donor.3) | copy-start | bytes 98308

commit v2 on v1

--- a/solution.py
+++ b/solution.py
@@ -18,9 +18,12 @@
 BLOCK_ROWS = 40
 MSG_ROWS = 136
 SPLITS = 2
+STEPS = 4
+UNROLL = 4
 f32 = jnp.float32
 bf16 = jnp.bfloat16
 PARAMS = pltpu.CompilerParams(vmem_limit_bytes=32 * 1024 * 1024)
+WIDE = pltpu.CompilerParams(vmem_limit_bytes=60 * 1024 * 1024)
 
 
 def lanes_of(table, index):
@@ -41,12 +44,35 @@
     return even, odd
 
 
-def pack_kernel(ice, heat, slope, drag, donor, shaft, prior, out, near, far, own):
+def joined_rows(rows):
+    return jnp.concatenate([rows[pl.ds(0, 16, stride=2), :], rows[pl.ds(1, 16, stride=2), :]], axis=1)
+
+
+def pack_kernel(
+    ice_in, heat_in, slope_in, drag_in, donor_in, shaft_in, prior_in, out, near, far, own,
+    ice, heat, slope, drag, donor, shaft, prior, arrivals,
+):
     g = lax.axis_index("grp")
     d = lax.axis_index("dom")
-    ids = jnp.concatenate(
-        [donor[0, g, pl.ds(0, 16, stride=2), :], donor[0, g, pl.ds(1, 16, stride=2), :]], axis=1
+    pairs = (
+        (donor_in.at[0, g], donor),
+        (ice_in, ice),
+        (slope_in, slope),
+        (drag_in, drag),
+        (heat_in, heat),
+        (shaft_in, shaft),
+        (prior_in, prior),
     )
+    copies = [pltpu.make_async_copy(a, b, arrivals.at[i]) for i, (a, b) in enumerate(pairs)]
+    for copy in copies:
+        copy.start()
+    out[0:12, :] = jnp.zeros((12, 128), f32)
+    out[31 * 40 + 24 : 31 * 40 + 36, :] = jnp.zeros((12, 128), f32)
+    for k in range(32):
+        out[40 * k + 36 : 40 * k + 40, :] = jnp.zeros((4, 128), f32)
+    for copy in copies:
+        copy.wait()
+    ids = joined_rows(donor)
     ids = jnp.maximum(ids, 0)
     high = ids >> 7
     low = ids & 127
@@ -79,10 +105,6 @@
             out[pl.ds(52 + p, 16, stride=80), :] = odd
             out[pl.ds(24 + p, 16, stride=80), :] = odd
             out[pl.ds(80 + p, 15, stride=80), :] = odd[:15]
-    out[0:12, :] = jnp.zeros((12, 128), f32)
-    out[31 * 40 + 24 : 31 * 40 + 36, :] = jnp.zeros((12, 128), f32)
-    for k in range(32):
-        out[40 * k + 36 : 40 * k + 40, :] = jnp.zeros((4, 128), f32)
 
     def message(msg, row0, chunk0):
         for c in range(2):
@@ -255,7 +277,7 @@
     return [along_x0, along_x1, along_y0, along_y1, z00, z01, z10, z11]
 
 
-def element(low_u, top_u, low_v, top_v, hardness, inverse2, keep=None):
+def element(low_u, top_u, low_v, top_v, hard, inverse2, keep=None):
     def gradients(low, top):
         x = [interpolate(low[q], top[q])[1:] for q in (0, 1)]
         y = [interpolate(low[2 + q], top[2 + q])[1:] for q in (0, 1)]
@@ -283,7 +305,7 @@
                 rate = (
                     a * (a + b) + vy2[qx][qz] + 0.25 * (shear * shear) + vertical[2 * qx + qy]
                 )
-                eta = jnp.exp2(hardness - jnp.log2(rate) * (1.0 / 3.0))
+                eta = jnp.exp2(hard - jnp.log2(rate) * (1.0 / 3.0))
                 if keep is not None:
                     eta = jnp.where(keep, eta, 0.0)
                 put(ex, (qy, qz), eta)
@@ -365,7 +387,74 @@
     return results
 
 
-def ice_kernel(geo, vext, edges, shaft, out_v, send, hard, first, second, means):
+def corners(value, value_y):
+    pair = value + value_y
+    return pair + up_x(pair)
+
+
+def geometry(depth4):
+    dz = depth4 * (0.25 / LAYERS)
+    dz = jnp.where(dz > 0.0, dz, 1.0)
+    inverse = 0.25 / dz
+    return jnp.log2(dz * 16.0), inverse * inverse
+
+
+def hardness(log_depth, warmth4):
+    return log_depth - (0.25 * LOG2E) * warmth4
+
+
+def at_lane(value, index):
+    return lanes_of(value, jnp.full((8, 128), index, jnp.int32))
+
+
+def up_y(value):
+    return pltpu.roll(value, 127, 1)
+
+
+def down_y(value):
+    return pltpu.roll(value, 1, 1)
+
+
+def levels(source, next_u, next_v, hard, inverse2, finish):
+    def terms(z):
+        u = source[z]
+        v = source[LEVELS + z]
+        return level_terms(u, next_u(z, u)) + level_terms(v, next_v(z, v))
+
+    def body(z, carry):
+        low, tops = carry[:16], carry[16:]
+        top = terms(z + 1)
+        lows, next_tops = element(low[:8], top[:8], low[8:], top[8:], hard(z), inverse2)
+        finish(z, node_parts([a + b for a, b in zip(lows, tops)]))
+        return (*top, *next_tops)
+
+    zero = jnp.zeros((8, 128), f32)
+    carry = lax.fori_loop(0, LAYERS, body, (*terms(0), *([zero] * 24)), unroll=UNROLL)
+    finish(LAYERS, node_parts(list(carry[16:])))
+
+
+def inner_kernel(geo, vext, partial):
+    lane = iota((8, 128), 1)
+    depth = geo[0]
+    log_depth, inverse2 = geometry(corners(depth, up_y(depth)))
+
+    def hard(z):
+        warm = geo[4 + z]
+        return hardness(log_depth, corners(warm, up_y(warm)))
+
+    def beside(z, value):
+        return up_y(value)
+
+    def finish(z, results):
+        for q, (a, b) in enumerate(results):
+            partial[q * LEVELS + z] = jnp.where(lane == 127, 0.0, a) + jnp.where(
+                lane == 0, 0.0, down_y(b)
+            )
+
+    levels(vext, beside, beside, hard, inverse2, finish)
+
+
+def ice_kernel(geo, vext, partial, edge, edge_near, edge_far, origin, out_v, send, hard, first, second, means):
     g = lax.axis_index("grp")
     d = lax.axis_index("dom")
     groups = lax.axis_size("grp")
@@ -374,18 +463,15 @@
     lane = iota((8, 128), 1)
     group = lane // LEVELS
     level = lane - group * LEVELS
-
-    def at_lane(value, index):
-        return lanes_of(value, jnp.full((8, 128), index, jnp.int32))
-
-    base = 56 * g
-    before = pl.multiple_of(jnp.maximum(base - 56, 0), 8)
-    after = pl.multiple_of(jnp.minimum(base + 56, 56 * (groups - 1)), 8)
+    even_group = g % 2 == 0
 
     def edge_field(i):
-        own = edges[pl.ds(pl.multiple_of(base + 8 * i, 8), 8), :]
-        left = jnp.where(g > 0, edges[pl.ds(before + 8 * i, 8), :], 0.0)
-        right = jnp.where(g < groups - 1, edges[pl.ds(after + 8 * i, 8), :], 0.0)
+        span = slice(8 * i, 8 * i + 8)
+        own = edge[span, :]
+        a = edge_near[span, :]
+        b = edge_far[span, :]
+        left = jnp.where(even_group, b, a)
+        right = jnp.where(even_group, a, b)
         return jnp.where(
             lane < 42,
             pltpu.roll(left, 86, 1),
@@ -398,36 +484,24 @@
 
     edge_u, edge_v, edge_t, edge_h, edge_fu, edge_fv, edge_b = [edge_field(i) for i in range(7)]
 
-    def up_y(value, beyond):
-        return jnp.where(lane == 127, beyond, pltpu.roll(value, 127, 1))
-
     def edge_up(value):
         return pltpu.roll(value, 107, 1)
 
-    def corners(value, value_y):
-        pair = value + value_y
-        return pair + up_x(pair)
-
-    def geometry(depth4):
-        dz = depth4 * (0.25 / LAYERS)
-        dz = jnp.where(dz > 0.0, dz, 1.0)
-        inverse = 0.25 / dz
-        return jnp.log2(dz * 16.0), inverse * inverse
-
+    def joined(value, beyond, index):
+        return jnp.where(lane == 127, at_lane(beyond, index), up_y(value))
+
+    edge_log, edge_inv2 = geometry(corners(edge_h, edge_up(edge_h)))
+    edge_hard = hardness(edge_log, corners(edge_t, edge_up(edge_t)))
     depth = geo[0]
-    main_log, main_inv2 = geometry(corners(depth, up_y(depth, at_lane(edge_h, 84))))
-    edge_log, edge_inv2 = geometry(corners(edge_h, edge_up(edge_h)))
-    edge_hard = edge_log - (0.25 * LOG2E) * corners(edge_t, edge_up(edge_t))
-
-    @pl.loop(0, LAYERS)
-    def _(l):
+    main_log, main_inv2 = geometry(corners(depth, joined(depth, edge_h, 84)))
+    for l in range(LAYERS):
         warm = geo[4 + l]
-        hard[l] = main_log - (0.25 * LOG2E) * corners(warm, up_y(warm, at_lane(edge_t, 84 + l)))
+        hard[l] = hardness(main_log, corners(warm, joined(warm, edge_t, 84 + l)))
 
     load_u = geo[1]
     load_v = geo[2]
     friction = geo[3]
-    not_top = jnp.logical_and(level != LAYERS, lane < 6 * LEVELS)
+    keep = jnp.logical_and(level != LAYERS, lane < 6 * LEVELS)
     first_row = jnp.where(d == 0, 2, 1)
     last_row = jnp.where(d == domains - 1, 5, 6)
     inside = jnp.logical_and(row >= first_row, row <= last_row)
@@ -442,49 +516,25 @@
     def edge_parts(u, v):
         low_u = level_terms(u, edge_up(u))
         low_v = level_terms(v, edge_up(v))
-        top_u = [pltpu.roll(t, 127, 1) for t in low_u]
-        top_v = [pltpu.roll(t, 127, 1) for t in low_v]
-        lows, tops = element(low_u, top_u, low_v, top_v, edge_hard, edge_inv2, not_top)
-        acc = [a + pltpu.roll(b, 1, 1) for a, b in zip(lows, tops)]
-        return node_parts(acc)
+        top_u = [up_y(t) for t in low_u]
+        top_v = [up_y(t) for t in low_v]
+        lows, tops = element(low_u, top_u, low_v, top_v, edge_hard, edge_inv2, keep)
+        return node_parts([a + down_y(b) for a, b in zip(lows, tops)])
 
     def stepped(value, load, force, diagonal, drag):
         return value + 0.5 * (load - force - drag * value) / (diagonal + drag)
 
-    def sweep(source, target, eu, ev, parts, keep):
-        beyond = [part[1] for part in parts]
-
-        def node(z, acc, drag):
-            results = node_parts(acc)
-            fu, fv, du, dv = [
-                a + jnp.where(lane == 0, at_lane(e, 42 - LEVELS + z), pltpu.roll(b, 1, 1))
-                for (a, b), e in zip(results, beyond)
-            ]
-            u = stepped(source[z], load_u, fu, du, drag)
-            v = stepped(source[LEVELS + z], load_v, fv, dv, drag)
-            target[z] = jnp.where(keep, u, 0.0)
-            target[LEVELS + z] = jnp.where(keep, v, 0.0)
-
-        def terms(z):
-            u = source[z]
-            v = source[LEVELS + z]
-            return level_terms(u, up_y(u, at_lane(eu, 84 + z))) + level_terms(
-                v, up_y(v, at_lane(ev, 84 + z))
-            )
-
-        def body(z, carry):
-            low, tops = carry[:16], carry[16:]
-            top = terms(z + 1)
-            lows, next_tops = element(low[:8], top[:8], low[8:], top[8:], hard[z], main_inv2)
-            node(z, [a + b for a, b in zip(lows, tops)], jnp.where(z == 0, friction, 0.0))
-            return (*top, *next_tops)
-
-        zero = jnp.zeros((8, 128), f32)
-        carry = lax.fori_loop(0, LAYERS, body, (*terms(0), *([zero] * 24)))
-        node(LAYERS, list(carry[16:]), zero)
-
     parts = edge_parts(edge_u, edge_v)
-    sweep(vext, first, edge_u, edge_v, parts, inside)
+    for z in range(LEVELS):
+        sums = []
+        for q, (a, b) in enumerate(parts):
+            rim = jnp.where(lane == 127, at_lane(a, 63 + z), 0.0)
+            rim = jnp.where(lane == 0, at_lane(b, 21 + z), rim)
+            sums.append(partial[q * LEVELS + z] + rim)
+        fu, fv, du, dv = sums
+        drag = friction if z == 0 else 0.0
+        first[z] = jnp.where(inside, stepped(vext[z], load_u, fu, du, drag), 0.0)
+        first[LEVELS + z] = jnp.where(inside, stepped(vext[LEVELS + z], load_v, fv, dv, drag), 0.0)
 
     def edge_final(c, value, load):
         (fa, fb), (da, db) = parts[c], parts[2 + c]
@@ -498,9 +548,25 @@
         here = lane == 42 + z
         edge_u = jnp.where(here, at_lane(first[z], 0), edge_u)
         edge_v = jnp.where(here, at_lane(first[LEVELS + z], 0), edge_v)
-    parts = edge_parts(edge_u, edge_v)
-    own_rows = jnp.logical_and(row >= 2, row < 6)
-    sweep(first, second, edge_u, edge_v, parts, own_rows)
+    beyond = [b for _, b in edge_parts(edge_u, edge_v)]
+
+    def finish(z, results):
+        fu, fv, du, dv = [
+            a + jnp.where(lane == 0, at_lane(e, 21 + z), down_y(b))
+            for (a, b), e in zip(results, beyond)
+        ]
+        drag = jnp.where(z == 0, friction, 0.0)
+        second[z] = stepped(first[z], load_u, fu, du, drag)
+        second[LEVELS + z] = stepped(first[LEVELS + z], load_v, fv, dv, drag)
+
+    levels(
+        first,
+        lambda z, value: joined(value, edge_u, 84 + z),
+        lambda z, value: joined(value, edge_v, 84 + z),
+        lambda z: hard[z],
+        main_inv2,
+        finish,
+    )
     for c in range(2):
         for z in range(LEVELS):
             out_v[c, z] = second[c * LEVELS + z, 2:6, :]
@@ -511,6 +577,26 @@
                 second[at] + second[at + 1]
             )
 
+    from_x = origin[0:16]
+    from_y = origin[16:32]
+    lane16 = iota((16, 128), 1)
+    here = [from_x == x for x in range(4)]
+    send[...] = jnp.zeros(send.shape, f32)
+    for l in range(LAYERS):
+        pair = []
+        for c in range(2):
+            at = 8 * (c * LAYERS + l) + 2
+            value = lanes_of(row_of(means, at, 16), from_y)
+            for x in range(1, 4):
+                value = jnp.where(here[x], lanes_of(row_of(means, at + x, 16), from_y), value)
+            pair.append(value)
+        even, odd = halves(pair[0], pair[1], lane16)
+        start = (l // 5) * 256 + l % 5
+        send[pl.ds(start, 16, stride=16), :] = even
+        send[pl.ds(start + 8, 16, stride=16), :] = odd
+
+
+def prepare_kernel(shaft, origin):
     slot_row = iota((16, 128), 0)
     place = iota((16, 128), 1).astype(f32)
     low_row = iota((128, 128), 0)
@@ -528,80 +614,51 @@
             (((1,), (1,)), ((), ())),
             preferred_element_type=f32,
         )
-    from_x = where_from[0:16].astype(jnp.int32)
-    from_y = where_from[16:32].astype(jnp.int32) & 127
-    lane16 = iota((16, 128), 1)
-    here = [from_x == x for x in range(4)]
-    send[...] = jnp.zeros(send.shape, f32)
-    for l in range(LAYERS):
-        pair = []
-        for c in range(2):
-            at = 8 * (c * LAYERS + l) + 2
-            value = lanes_of(row_of(means, at, 16), from_y)
-            for x in range(1, 4):
-                value = jnp.where(here[x], lanes_of(row_of(means, at + x, 16), from_y), value)
-            pair.append(value)
-        even, odd = halves(pair[0], pair[1], lane16)
-        start = (l // 5) * 256 + l % 5
-        send[pl.ds(start, 16, stride=16), :] = even
-        send[pl.ds(start + 8, 16, stride=16), :] = odd
-
-
-def total_kernel(arrived, donor, out, ids, left, right, sums):
+    origin[...] = where_from.astype(jnp.int32) & 127
+
+
+def total_kernel(arrived, donor, out, left, hot):
     lane = iota((8, 128), 1)
     row = iota((8, 128), 0)
-    row256 = iota((256, 128), 0)
-    for g in range(4):
-        ids[16 * g : 16 * g + 16, :] = jnp.concatenate(
-            [donor[0, g, pl.ds(0, 16, stride=2), :], donor[0, g, pl.ds(1, 16, stride=2), :]],
-            axis=1,
-        )
-
-    @pl.loop(0, 8)
-    def _(step):
-        for part in range(8):
-            chunk = 8 * step + part
-            span = slice(128 * part, 128 * part + 128)
-            x = arrived[pl.ds(pl.multiple_of(16 * chunk, 16), 16), :]
+    row256 = iota((256, 128), 0).astype(bf16)
+    one = jnp.ones((), bf16)
+    zero = jnp.zeros((), bf16)
+    ids = [joined_rows(donor.at[0, g]) for g in range(4)]
+    sums = jnp.zeros((256 * SPLITS, 256), f32)
+    for step in range(STEPS):
+        for part in range(64 // STEPS):
+            chunk = 64 // STEPS * step + part
+            span = slice(128 * chunk, 128 * chunk + 128)
+            x = arrived[16 * chunk : 16 * chunk + 16, :]
             u, v = halves(x[:8], x[8:], lane)
             u = jnp.where(row < 5, u, jnp.where(row == 5, 1.0, 0.0))
             v = jnp.where(row < 5, v, 0.0)
             rest = jnp.concatenate([u, v], axis=0)
-            values = []
+            cell = ids[chunk // 16][chunk % 16 : chunk % 16 + 1]
+            high = jnp.broadcast_to(cell >> 8, (16, 128)).astype(bf16)
+            low = jnp.broadcast_to(cell & 255, (256, 128)).astype(bf16)
+            hot[:, span] = jnp.where(row256 == low, one, zero)
             for s in range(SPLITS):
                 piece = rest.astype(bf16)
-                values.append(piece)
                 rest = rest - piece.astype(f32)
-            cell = ids[pl.ds(chunk, 1), :]
-            high = jnp.broadcast_to(cell >> 8, (16, 128))
-            low = jnp.broadcast_to(cell & 255, (256, 128))
-            right[:, span] = jnp.where(row256 == low, 1.0, 0.0).astype(bf16)
-            for h in range(16):
-                here = jnp.where(high == h, 1.0, 0.0).astype(bf16)
-                for s in range(SPLITS):
-                    at = 16 * (SPLITS * h + s)
-                    left[at : at + 16, span] = values[s] * here
-        product = lax.dot_general(
-            left[...], right[...], (((1,), (1,)), ((), ())), preferred_element_type=f32
+                for h in range(16):
+                    at = 256 * s + 16 * h
+                    left[at : at + 16, span] = jnp.where(high == h, piece, zero)
+        span = slice(8192 // STEPS * step, 8192 // STEPS * (step + 1))
+        sums = sums + lax.dot_general(
+            left[:, span], hot[:, span], (((1,), (1,)), ((), ())), preferred_element_type=f32
         )
-
-        @pl.when(step == 0)
-        def _():
-            sums[...] = product
-
-        @pl.when(step > 0)
-        def _():
-            sums[...] += product
-
     for h in range(16):
-        at = 16 * SPLITS * h
-        total = sums[at : at + 16, :]
+        total = sums[16 * h : 16 * h + 16]
         for s in range(1, SPLITS):
-            total = total + sums[at + 16 * s : at + 16 * s + 16, :]
+            total = total + sums[256 * s + 16 * h : 256 * s + 16 * h + 16]
         count = jnp.maximum(total[5:6, :], 1.0)
         span = slice(256 * h, 256 * h + 256)
-        out[0, :, span] = total[0:5, :] / count
-        out[1, :, span] = total[8:13, :] / count
+        u = total[0:5, :] / count
+        v = total[8:13, :] / count
+        for l in range(5):
+            out[l, 0:1, span] = u[l : l + 1]
+            out[l, 1:2, span] = v[l : l + 1]
 
 
 def shape(*sizes):
@@ -631,7 +688,7 @@
 ):
     ice = ice_depth.reshape(32, 128)
     drag = sliding_drag.reshape(32, 128)
-    outgoing, near, far, own = pl.pallas_call(
+    outgoing, near_out, far_out, own = pl.pallas_call(
         pack_kernel,
         out_shape=(
             shape(32 * BLOCK_ROWS, 128),
@@ -639,7 +696,18 @@
             shape(MSG_ROWS, 128),
             shape(6, 32, 128),
         ),
-        compiler_params=PARAMS,
+        in_specs=[pl.BlockSpec(memory_space=pltpu.HBM)] * 7,
+        scratch_shapes=[
+            pltpu.VMEM((32, 128), f32),
+            pltpu.VMEM((LAYERS, 4096), f32),
+            pltpu.VMEM((2, 4096), f32),
+            pltpu.VMEM((32, 128), f32),
+            pltpu.VMEM((32, 64), jnp.int32),
+            pltpu.VMEM((4, 128), jnp.int32),
+            pltpu.VMEM((2, LEVELS, 4, 128), f32),
+            pltpu.SemaphoreType.DMA((7,)),
+        ],
+        compiler_params=WIDE,
         name="pack",
     )(
         ice,
@@ -652,8 +720,16 @@
     )
     arrived = lax.all_to_all(outgoing, "dom", split_axis=0, concat_axis=0, tiled=True)
     even, odd = near_pairs(lax.axis_size("dom"))
-    near = lax.ppermute(near, "dom", even)
-    far = lax.ppermute(far, "dom", odd)
+    near = lax.ppermute(near_out, "dom", even)
+    far = lax.ppermute(far_out, "dom", odd)
+    shaft, near_out = lax.optimization_barrier((shaft_holding_position, near_out))
+    origin = pl.pallas_call(
+        prepare_kernel,
+        out_shape=jax.ShapeDtypeStruct((32, 128), jnp.int32),
+        compiler_params=PARAMS,
+        name="prepare",
+    )(shaft)
+    arrived, origin = lax.optimization_barrier((arrived, origin))
     geo, vext, edge = pl.pallas_call(
         column_kernel,
         out_shape=(shape(FIELDS, 8, 128), shape(2 * LEVELS, 8, 128), shape(56, 128)),
@@ -661,7 +737,15 @@
         compiler_params=PARAMS,
         name="columns",
     )(arrived, shaft_holding_position, near, far, prior_node_motion)
-    edges = lax.all_gather(edge, "grp", axis=0, tiled=True)
+    even, odd = near_pairs(lax.axis_size("grp"))
+    edge_near = lax.ppermute(edge, "grp", even)
+    edge_far = lax.ppermute(edge, "grp", odd)
+    partial = pl.pallas_call(
+        inner_kernel,
+        out_shape=shape(4 * LEVELS, 8, 128),
+        compiler_params=PARAMS,
+        name="inner",
+    )(geo, vext)
     node_velocity, send = pl.pallas_call(
         ice_kernel,
         out_shape=(shape(2, LEVELS, 4, 128), shape(1024, 128)),
@@ -673,7 +757,7 @@
         ],
         compiler_params=PARAMS,
         name="velocity",
-    )(geo, vext, edges, shaft_holding_position)
+    )(geo, vext, partial, edge, edge_near, edge_far, origin)
     back = lax.all_to_all(send, ("grp", "dom"), split_axis=0, concat_axis=0, tiled=True)
     depth, heat = pl.pallas_call(
         advect_kernel,
@@ -692,17 +776,12 @@
     )
     tier_motion = pl.pallas_call(
         total_kernel,
-        out_shape=shape(2, 5, 4096),
-        scratch_shapes=[
-            pltpu.VMEM((64, 128), jnp.int32),
-            pltpu.VMEM((256 * SPLITS, 1024), bf16),
-            pltpu.VMEM((256, 1024), bf16),
-            pltpu.VMEM((256 * SPLITS, 256), f32),
-        ],
+        out_shape=shape(5, 2, 4096),
+        scratch_shapes=[pltpu.VMEM((256 * SPLITS, 8192), bf16), pltpu.VMEM((256, 8192), bf16)],
         compiler_params=PARAMS,
         name="totals",
     )(back, position_donor_polygons)
-    return (depth.reshape(4096), heat, node_velocity, tier_motion)
+    return (depth.reshape(4096), heat, node_velocity, jnp.transpose(tier_motion, (1, 0, 2)))
 
 
 def solution(mesh):

time: 83.6 us -> 68.6 us (0.82)
  starting transfers between devices: 18.1 us -> 26.5 us
  blocking collectives: 7.98 us -> 0 us
  local copies, waits for them, and re-layouts: 6.41 us -> 0.05 us
  Pallas kernels: 32.4 us -> 26.2 us
  waiting for transfers between devices: 17.4 us -> 14.7 us
    pallas_call x1, Pallas kernels: 14.2 us -> 6.15 us  [shards(): pl.pallas_call(ice_kernel, out_shape=(shape(2, LEVELS, 4, 128), shape(102...]
    all_gather x1 -> x0, blocking collectives: 7.98 us -> none  [shards(): edges = lax.all_gather(edge, 'grp', axis=0, tiled=True)]
    ppermute x2 -> x4, starting transfers between devices: 1.96 us -> 9.41 us  [the longest x1 4.92 us: shards(): edge_far = lax.ppermute(edge, 'grp', odd)]
    unnamed x27 -> x20, local copies, waits for them, and re-layouts: 6.41 us -> 0.05 us
    ppermute x2 -> x4, waiting for transfers between devices: 5.05 us -> 0.01 us  [the longest x1 0.01 us: shards(): edge_far = lax.ppermute(edge, 'grp', odd)]
    all_to_all x1, waiting for transfers between devices: 5.55 us -> 7.9 us  [shards(): lax.all_to_all(outgoing, 'dom', split_axis=0, concat_axis=0, tiled=True)]
    pallas_call x1, Pallas kernels: 4.79 us -> 5.97 us  [shards(): pl.pallas_call(pack_kernel, out_shape=(shape(32 * BLOCK_ROWS, 128), shape...]
    all_to_all x1, starting transfers between devices: 4.67 us -> 5.58 us  [shards(): lax.all_to_all(send, ('grp', 'dom'), split_axis=0, concat_axis=0, tiled=T...]
  transfers between devices with their start and end apart: 4 -> 6, of which waited for: 3 -> 2; matrix products, arithmetic and copies ran while one was open for 0% -> 0% of each run, Pallas kernels for 8% -> 14%
where the time goes in v2:
time: 68.6 us; the launch traced here: 68.2 us
  starting transfers between devices  26.5 us (39%)
  Pallas kernels  26.2 us (38%)
  waiting for transfers between devices  14.7 us (21%)
  between operations  0.82 us (1%)
    all_to_all x1, starting transfers between devices, shards(): lax.all_to_all(outgoing, 'dom', split_axis=0, concat_axis=0, tiled=True)  11.5 us
    all_to_all x1, waiting for transfers between devices, shards(): lax.all_to_all(outgoing, 'dom', split_axis=0, concat_axis=0, tiled=True)  7.9 us
    pallas_call x1, Pallas kernels, shards(): pl.pallas_call(advect_kernel, out_shape=(shape(32, 128), shape(5, 4096)),...  6.83 us
    all_to_all x1, waiting for transfers between devices, shards(): lax.all_to_all(send, ('grp', 'dom'), split_axis=0, concat_axis=0, tiled=T...  6.81 us
    pallas_call x1, Pallas kernels, shards(): pl.pallas_call(ice_kernel, out_shape=(shape(2, LEVELS, 4, 128), shape(102...  6.15 us
    pallas_call x1, Pallas kernels, shards(): pl.pallas_call(pack_kernel, out_shape=(shape(32 * BLOCK_ROWS, 128), shape...  5.97 us
    all_to_all x1, starting transfers between devices, shards(): lax.all_to_all(send, ('grp', 'dom'), split_axis=0, concat_axis=0, tiled=T...  5.58 us
    ppermute x1, starting transfers between devices, shards(): edge_far = lax.ppermute(edge, 'grp', odd)  4.92 us
  transfers between devices with their start and end apart: 6, of which 2 were waited for; matrix products, arithmetic and copies ran while one was open for 0% of the time, Pallas kernels for 14%

profile of v2, /device:TPU:1, one launch (start us, length us, event | category | flops | bytes accessed | tf_op | source)
XLA Modules:
  0.0 68.2 jit_solution(9575724191972523304)
XLA Ops:
  0.6 6.0 %pack.1 = (f32[1280,128]{1,0:T(8,128)}, f32[136,128]{1,0:T(8,128)}, f32[136,128]{1,0:T(8,128)}, f32[6,32,128]{2,1,0:T(8,128)}) custom-call(f32[32,128]{1,0:T(8,128)} %bitcast.12, f32[20,4096]{1,0:T(8,128)} %heat_in.1, f32[2,4096]{1,0:T(2,128)} %slope_in.1, f32[32,128]{1,0:T(8,128)} %bitcast.13, s32[1,4,32,64]{3,2,1,0:T(8,128)} %donor.1, s32[4,128]{1,0:T(4,128)} %shaft.2, ...), custom_call_target="tpu_custom_call" | custom-call | tf_op jit(solution)/shard_map/pack/pallas_call | solution.py:691
  6.6 0.0 copy-start.9
  6.6 0.0 copy-start.8
  6.6 0.0 copy-start.1
  6.6 11.5 %all-to-all-start = ((f32[32,40,128]{2,1,0:T(8,128)}), f32[32,40,128]{2,1,0:T(8,128)S(1)}, u32[]{:S(2)}, u32[]{:S(2)}) async-start(f32[32,40,128]{2,1,0:T(8,128)} %bitcast.10), calls=%async_computation | async-start | bytes 1310720 | tf_op jit(solution)/shard_map/all_to_all | solution.py:721
  18.1 0.0 copy-start.7
  18.2 0.0 copy-done.9
  18.2 0.7 collective-permute-start.1
  18.8 0.0 copy-done.8
  18.9 3.7 %collective-permute-start = (f32[136,128]{1,0:T(8,128)S(1)}, f32[136,128]{1,0:T(8,128)S(1)}, u32[]{:S(2)}, u32[]{:S(2)}) collective-permute-start(f32[136,128]{1,0:T(8,128)S(1)} %copy-done.8), channel_id=1, source_target_pairs={{0,1},{1,0},{2,3},{3,2},{4,5},{5,4},{6,7},{7,6},{8,9},{9,8},{10,11... | collective-permute-start | bytes 208904 | tf_op jit(solution)/shard_map/ppermute | solution.py:723
  22.6 0.0 copy-done.7
  22.6 0.2 prepare.1.origin
  22.8 7.9 %all-to-all-done = f32[32,40,128]{2,1,0:T(8,128)S(1)} async-done(((f32[32,40,128]{2,1,0:T(8,128)}), f32[32,40,128]{2,1,0:T(8,128)S(1)}, u32[]{:S(2)}, u32[]{:S(2)}) %all-to-all-start) | async-done | bytes 655392 | tf_op jit(solution)/shard_map/all_to_all | solution.py:721
  30.7 0.0 collective-permute-done.1.far
  30.7 0.0 collective-permute-done.near
  30.7 0.0 copy-done.1
  30.7 1.1 %columns.1 = (f32[24,8,128]{2,1,0:T(8,128)S(1)}, f32[42,8,128]{2,1,0:T(8,128)S(1)}, f32[56,128]{1,0:T(8,128)S(1)}) custom-call(f32[1280,128]{1,0:T(8,128)S(1)} %bitcast.8, s32[4,128]{1,0:T(4,128)S(1)} %copy-done.7, f32[136,128]{1,0:T(8,128)S(1)} %collective-permute-done.near, f32[136,128]{1,0:T(8,128)S(1)} %collective-permute-done.1.far, ...), custom_call_target="tpu_custom_call" | custom-call | tf_op jit(solution)/shard_map/columns/pallas_call | solution.py:733
  31.8 4.9 %collective-permute-start.3 = (f32[56,128]{1,0:T(8,128)S(1)}, f32[56,128]{1,0:T(8,128)S(1)}, u32[]{:S(2)}, u32[]{:S(2)}) collective-permute-start(f32[56,128]{1,0:T(8,128)S(1)} %get-tuple-element.28.edge), channel_id=1, source_target_pairs={{32,64},{64,32},{33,65},{65,33},{34,66},{66,34},{35,67},{67,35},{3... | collective-permute-start | bytes 86024 | tf_op jit(solution)/shard_map/ppermute | solution.py:742
  36.7 0.1 collective-permute-start.2
  36.8 2.3 %inner.1.partial = f32[84,8,128]{2,1,0:T(8,128)S(1)} custom-call(f32[24,8,128]{2,1,0:T(8,128)S(1)} %get-tuple-element.26.geo, f32[42,8,128]{2,1,0:T(8,128)S(1)} %get-tuple-element.27.vext), custom_call_target="tpu_custom_call" | custom-call | tf_op jit(solution)/shard_map/inner/pallas_call | solution.py:743
  39.1 0.0 collective-permute-done.3.edge_far
  39.1 0.0 collective-permute-done.2.edge_near
  39.1 0.0 copy-start.6
  39.1 6.2 %velocity.1 = (f32[2,21,4,128]{3,2,1,0:T(4,128)}, f32[1024,128]{1,0:T(8,128)}) custom-call(f32[24,8,128]{2,1,0:T(8,128)S(1)} %get-tuple-element.26.geo, f32[42,8,128]{2,1,0:T(8,128)S(1)} %get-tuple-element.27.vext, f32[84,8,128]{2,1,0:T(8,128)S(1)} %inner.1.partial, f32[56,128]{1,0:T(8,128)S(1)} %get-tuple-element.28.edge, ...), custom_call_target="tpu_custom_call" | custom-call | tf_op jit(solution)/shard_map/velocity/pallas_call | solution.py:749
  45.3 0.0 copy-start
  45.3 0.0 copy-start.3
  45.3 0.0 copy-start.4
  45.3 0.0 copy-start.5
  45.3 5.6 %all-to-all-start.1 = ((f32[128,8,128]{2,1,0:T(8,128)}), f32[128,8,128]{2,1,0:T(8,128)S(1)}, u32[]{:S(2)}, u32[]{:S(2)}) async-start(f32[128,8,128]{2,1,0:T(8,128)} %bitcast.5), calls=%async_computation.1 | async-start | bytes 1048576 | tf_op jit(solution)/shard_map/all_to_all | solution.py:761
  50.9 0.0 copy-done.6
  50.9 0.0 copy-done
  50.9 0.0 copy-done.3
  50.9 0.0 copy-done.4
  50.9 0.0 copy-done.5
  50.9 0.0 copy-start.2
  51.0 6.8 %advect.1 = (f32[32,128]{1,0:T(8,128)}, f32[5,4096]{1,0:T(8,128)}) custom-call(f32[6,32,128]{2,1,0:T(8,128)S(1)} %copy-done.6, s32[6,4096]{1,0:T(8,128)S(1)} %copy-done.3, f32[6,4096]{1,0:T(8,128)S(1)} %copy-done.4, f32[6,4096]{1,0:T(8,128)S(1)} %copy-done.5, f32[5,6,4096]{2,1,0:T(8,128)S(1)} %copy-done, f32[136,128]{1,0:T(8,128)S(1)} %collective-permute-done.near, ...), custom_call_target="tpu_custom_call" | custom-call | tf_op jit(solution)/shard_map/advect/pallas_call | solution.py:762
  57.8 6.8 %all-to-all-done.1 = f32[128,8,128]{2,1,0:T(8,128)S(1)} async-done(((f32[128,8,128]{2,1,0:T(8,128)}), f32[128,8,128]{2,1,0:T(8,128)S(1)}, u32[]{:S(2)}, u32[]{:S(2)}) %all-to-all-start.1) | async-done | bytes 524320 | tf_op jit(solution)/shard_map/all_to_all | solution.py:761
  64.6 0.0 copy-done.2
  64.6 3.6 %totals.1 = f32[5,2,4096]{2,1,0:T(2,128)} custom-call(f32[1024,128]{1,0:T(8,128)S(1)} %bitcast.9, s32[1,4,32,64]{3,2,1,0:T(8,128)S(1)} %copy-done.2), custom_call_target="tpu_custom_call" | custom-call | tf_op jit(solution)/shard_map/totals/pallas_call | solution.py:777
Async XLA Ops:
  6.6 11.5 %copy-start.9 = (f32[136,128]{1,0:T(8,128)S(1)}, f32[136,128]{1,0:T(8,128)}, u32[]{:S(2)}) copy-start(f32[136,128]{1,0:T(8,128)} %get-tuple-element.20) | copy-start | bytes 208900
  6.6 12.2 %copy-start.8 = (f32[136,128]{1,0:T(8,128)S(1)}, f32[136,128]{1,0:T(8,128)}, u32[]{:S(2)}) copy-start(f32[136,128]{1,0:T(8,128)} %get-tuple-element.19) | copy-start | bytes 208900
  6.6 24.0 %copy-start.1 = (f32[2,21,4,128]{3,2,1,0:T(4,128)S(1)}, f32[2,21,4,128]{3,2,1,0:T(4,128)}, u32[]{:S(2)}) copy-start(f32[2,21,4,128]{3,2,1,0:T(4,128)} %prior.1) | copy-start | bytes 258052
  6.6 24.0 %all-to-all-start = ((f32[32,40,128]{2,1,0:T(8,128)}), f32[32,40,128]{2,1,0:T(8,128)S(1)}, u32[]{:S(2)}, u32[]{:S(2)}) async-start(f32[32,40,128]{2,1,0:T(8,128)} %bitcast.10), calls=%async_computation | async-start | bytes 1310720 | tf_op jit(solution)/shard_map/all_to_all | solution.py:721
  18.1 4.4 %copy-start.7 = (s32[4,128]{1,0:T(4,128)S(1)}, s32[4,128]{1,0:T(4,128)}, u32[]{:S(2)}) copy-start(s32[4,128]{1,0:T(4,128)} %shaft.2) | copy-start | bytes 6148
  18.2 12.5 %collective-permute-start.1 = (f32[136,128]{1,0:T(8,128)S(1)}, f32[136,128]{1,0:T(8,128)S(1)}, u32[]{:S(2)}, u32[]{:S(2)}) collective-permute-start(f32[136,128]{1,0:T(8,128)S(1)} %copy-done.9), channel_id=1, source_target_pairs={{1,2},{2,1},{3,4},{4,3},{5,6},{6,5},{7,8},{8,7},{9,10},{10,9},{11,... | collective-permute-start | bytes 208904 | tf_op jit(solution)/shard_map/ppermute | solution.py:724
  18.9 11.8 %collective-permute-start = (f32[136,128]{1,0:T(8,128)S(1)}, f32[136,128]{1,0:T(8,128)S(1)}, u32[]{:S(2)}, u32[]{:S(2)}) collective-permute-start(f32[136,128]{1,0:T(8,128)S(1)} %copy-done.8), channel_id=1, source_target_pairs={{0,1},{1,0},{2,3},{3,2},{4,5},{5,4},{6,7},{7,6},{8,9},{9,8},{10,11... | collective-permute-start | bytes 208904 | tf_op jit(solution)/shard_map/ppermute | solution.py:723
  31.8 7.4 %collective-permute-start.3 = (f32[56,128]{1,0:T(8,128)S(1)}, f32[56,128]{1,0:T(8,128)S(1)}, u32[]{:S(2)}, u32[]{:S(2)}) collective-permute-start(f32[56,128]{1,0:T(8,128)S(1)} %get-tuple-element.28.edge), channel_id=1, source_target_pairs={{32,64},{64,32},{33,65},{65,33},{34,66},{66,34},{35,67},{67,35},{3... | collective-permute-start | bytes 86024 | tf_op jit(solution)/shard_map/ppermute | solution.py:742
  36.7 2.4 %collective-permute-start.2 = (f32[56,128]{1,0:T(8,128)S(1)}, f32[56,128]{1,0:T(8,128)S(1)}, u32[]{:S(2)}, u32[]{:S(2)}) collective-permute-start(f32[56,128]{1,0:T(8,128)S(1)} %get-tuple-element.28.edge), channel_id=1, source_target_pairs={{0,32},{32,0},{64,96},{96,64},{1,33},{33,1},{65,97},{97,65},{2,34}... | collective-permute-start | bytes 86024 | tf_op jit(solution)/shard_map/ppermute | solution.py:741
  39.1 11.8 %copy-start.6 = (f32[6,32,128]{2,1,0:T(8,128)S(1)}, f32[6,32,128]{2,1,0:T(8,128)}, u32[]{:S(2)}) copy-start(f32[6,32,128]{2,1,0:T(8,128)} %get-tuple-element.18.own) | copy-start | bytes 294916
  45.3 5.6 %copy-start = (f32[5,6,4096]{2,1,0:T(8,128)S(1)}, f32[5,6,4096]{2,1,0:T(8,128)}, u32[]{:S(2)}) copy-start(f32[5,6,4096]{2,1,0:T(8,128)} %tier_speed.1) | copy-start | bytes 1474564
  45.3 5.6 %copy-start.3 = (s32[6,4096]{1,0:T(8,128)S(1)}, s32[6,4096]{1,0:T(8,128)}, u32[]{:S(2)}) copy-start(s32[6,4096]{1,0:T(8,128)} %adjacent.1) | copy-start | bytes 294916
  45.3 5.6 %copy-start.4 = (f32[6,4096]{1,0:T(8,128)S(1)}, f32[6,4096]{1,0:T(8,128)}, u32[]{:S(2)}) copy-start(f32[6,4096]{1,0:T(8,128)} %ratio.1) | copy-start | bytes 294916
  45.3 5.6 %copy-start.5 = (f32[6,4096]{1,0:T(8,128)S(1)}, f32[6,4096]{1,0:T(8,128)}, u32[]{:S(2)}) copy-start(f32[6,4096]{1,0:T(8,128)} %mean_speed.1) | copy-start | bytes 294916
  45.3 19.3 %all-to-all-start.1 = ((f32[128,8,128]{2,1,0:T(8,128)}), f32[128,8,128]{2,1,0:T(8,128)S(1)}, u32[]{:S(2)}, u32[]{:S(2)}) async-start(f32[128,8,128]{2,1,0:T(8,128)} %bitcast.5), calls=%async_computation.1 | async-start | bytes 1048576 | tf_op jit(solution)/shard_map/all_to_all | solution.py:761
  50.9 13.6 %copy-start.2 = (s32[1,4,32,64]{3,2,1,0:T(8,128)S(1)}, s32[1,4,32,64]{3,2,1,0:T(8,128)}, u32[]{:S(2)}) copy-start(s32[1,4,32,64]{3,2,1,0:T(8,128)} %donor.1) | copy-start | bytes 98308

commit v3 on v2

--- a/solution.py
+++ b/solution.py
@@ -17,9 +17,7 @@
 PAIRS = 12
 BLOCK_ROWS = 40
 MSG_ROWS = 136
-SPLITS = 2
 STEPS = 4
-UNROLL = 4
 f32 = jnp.float32
 bf16 = jnp.bfloat16
 PARAMS = pltpu.CompilerParams(vmem_limit_bytes=32 * 1024 * 1024)
@@ -49,17 +47,18 @@
 
 
 def pack_kernel(
-    ice_in, heat_in, slope_in, drag_in, donor_in, shaft_in, prior_in, out, near, far, own,
-    ice, heat, slope, drag, donor, shaft, prior, arrivals,
+    ice_in, heat_in, slope_in, drag_in, donor_in, shaft_in, prior_in,
+    out_to, near_to, far_to, own_to,
+    ice, heat, slope, drag, donor, shaft, prior, out, near, far, own, arrivals, leaves,
 ):
     g = lax.axis_index("grp")
     d = lax.axis_index("dom")
     pairs = (
+        (heat_in, heat),
         (donor_in.at[0, g], donor),
         (ice_in, ice),
         (slope_in, slope),
         (drag_in, drag),
-        (heat_in, heat),
         (shaft_in, shaft),
         (prior_in, prior),
     )
@@ -72,11 +71,53 @@
         out[40 * k + 36 : 40 * k + 40, :] = jnp.zeros((4, 128), f32)
     for copy in copies:
         copy.wait()
-    ids = joined_rows(donor)
-    ids = jnp.maximum(ids, 0)
+
+    own[0] = ice[...]
+    for part in range(4):
+
+        @pl.when(g == part)
+        def _():
+            for i in range(5):
+                layer = 5 * part + i
+                for k in range(32):
+                    own[i + 1, k : k + 1, :] = heat[layer : layer + 1, 128 * k : 128 * k + 128]
+
+    def message(msg, row0, chunk0):
+        for c in range(2):
+            for z in range(LEVELS):
+                at = 2 * (c * LEVELS + z)
+                msg[at : at + 2, :] = prior[c, z, row0 : row0 + 2, :]
+        msg[84:86, :] = shaft[row0 : row0 + 2, :].astype(f32)
+        msg[86:88, :] = jnp.zeros((2, 128), f32)
+        for i in range(6):
+            msg[88 + 8 * i : 96 + 8 * i, :] = own[i, chunk0 : chunk0 + 8, :]
+
+    even_device = d % 2 == 0
+
+    @pl.when(even_device)
+    def _():
+        message(near, 2, 24)
+        message(far, 0, 0)
+
+    @pl.when(jnp.logical_not(even_device))
+    def _():
+        message(near, 0, 0)
+        message(far, 2, 24)
+
+    leaving = [
+        pltpu.make_async_copy(near, near_to, leaves.at[0]),
+        pltpu.make_async_copy(far, far_to, leaves.at[1]),
+        pltpu.make_async_copy(own, own_to, leaves.at[2]),
+    ]
+    for copy in leaving:
+        copy.start()
+
+    ids = jnp.maximum(joined_rows(donor), 0)
     high = ids >> 7
     low = ids & 127
-    lane = iota((16, 128), 1)
+    lane = iota((8, 128), 1)
+    highs = [high[:8], high[8:]]
+    lows = [low[:8], low[8:]]
 
     def table(field, k):
         if field == 0:
@@ -87,56 +128,33 @@
             part = drag[k : k + 1, :]
         else:
             part = heat[field - 4 : field - 3, 128 * k : 128 * k + 128]
-        return jnp.broadcast_to(part, (16, 128))
-
-    for pair0 in range(0, PAIRS, 3):
-        pairs = range(pair0, pair0 + 3)
-        fields = [p for p in pairs] + [p + PAIRS for p in pairs]
-        found = {f: jnp.zeros((16, 128), f32) for f in fields}
+        return jnp.broadcast_to(part, (8, 128))
+
+    for v in range(2):
+        found = [jnp.zeros((8, 128), f32)] * FIELDS
         for k in range(32):
-            here = high == k
-            for f in fields:
-                found[f] = jnp.where(here, lanes_of(table(f, k), low), found[f])
-        for p in pairs:
+            here = highs[v] == k
+            for f in range(FIELDS):
+                found[f] = jnp.where(here, lanes_of(table(f, k), lows[v]), found[f])
+        at = 640 * v
+        for p in range(PAIRS):
             even, odd = halves(found[p], found[p + PAIRS], lane)
-            out[pl.ds(12 + p, 16, stride=80), :] = even
-            out[pl.ds(40 + p, 16, stride=80), :] = even
-            out[pl.ds(64 + p, 15, stride=80), :] = even[1:]
-            out[pl.ds(52 + p, 16, stride=80), :] = odd
-            out[pl.ds(24 + p, 16, stride=80), :] = odd
-            out[pl.ds(80 + p, 15, stride=80), :] = odd[:15]
-
-    def message(msg, row0, chunk0):
-        for c in range(2):
-            for z in range(LEVELS):
-                at = 2 * (c * LEVELS + z)
-                msg[at : at + 2, :] = prior[c, z, row0 : row0 + 2, :]
-        msg[84:86, :] = shaft[row0 : row0 + 2, :].astype(f32)
-        msg[86:88, :] = jnp.zeros((2, 128), f32)
-        for i in range(6):
-            msg[88 + 8 * i : 96 + 8 * i, :] = own[i, chunk0 : chunk0 + 8, :]
-
-    own[0] = ice[...]
-    for part in range(4):
-
-        @pl.when(g == part)
-        def _():
-            for i in range(5):
-                layer = 5 * part + i
-                for k in range(32):
-                    own[i + 1, k : k + 1, :] = heat[layer : layer + 1, 128 * k : 128 * k + 128]
-
-    even_device = d % 2 == 0
-
-    @pl.when(even_device)
-    def _():
-        message(near, 2, 24)
-        message(far, 0, 0)
-
-    @pl.when(jnp.logical_not(even_device))
-    def _():
-        message(near, 0, 0)
-        message(far, 2, 24)
+            out[pl.ds(at + 12 + p, 8, stride=80), :] = even
+            out[pl.ds(at + 40 + p, 8, stride=80), :] = even
+            if v == 0:
+                out[pl.ds(64 + p, 7, stride=80), :] = even[1:]
+                out[pl.ds(80 + p, 8, stride=80), :] = odd
+            else:
+                out[pl.ds(at - 16 + p, 8, stride=80), :] = even
+                out[pl.ds(at + 80 + p, 7, stride=80), :] = odd[:7]
+            out[pl.ds(at + 52 + p, 8, stride=80), :] = odd
+            out[pl.ds(at + 24 + p, 8, stride=80), :] = odd
+        span = slice(0, 600) if v == 0 else slice(600, 1280)
+        copy = pltpu.make_async_copy(out.at[span], out_to.at[span], leaves.at[3 + v])
+        copy.start()
+        leaving.append(copy)
+    for copy in leaving:
+        copy.wait()
 
 
 def advect_kernel(own, adjacent, ratio, mean_speed, tier_speed, near, far, depth_out, heat_out, ext):
@@ -429,7 +447,9 @@
         return (*top, *next_tops)
 
     zero = jnp.zeros((8, 128), f32)
-    carry = lax.fori_loop(0, LAYERS, body, (*terms(0), *([zero] * 24)), unroll=UNROLL)
+    carry = (*terms(0), *([zero] * 24))
+    for z in range(LAYERS):
+        carry = body(z, carry)
     finish(LAYERS, node_parts(list(carry[16:])))
 
 
@@ -454,7 +474,10 @@
     levels(vext, beside, beside, hard, inverse2, finish)
 
 
-def ice_kernel(geo, vext, partial, edge, edge_near, edge_far, origin, out_v, send, hard, first, second, means):
+def ice_kernel(
+    geo, vext, partial, edge, edge_near, edge_far, origin, out_v_to, send_to,
+    hard, first, second, means, out_v, send, leaves,
+):
     g = lax.axis_index("grp")
     d = lax.axis_index("dom")
     groups = lax.axis_size("grp")
@@ -488,7 +511,7 @@
         return pltpu.roll(value, 107, 1)
 
     def joined(value, beyond, index):
-        return jnp.where(lane == 127, at_lane(beyond, index), up_y(value))
+        return jnp.where(lane == 127, pltpu.roll(beyond, 127 - index, 1), up_y(value))
 
     edge_log, edge_inv2 = geometry(corners(edge_h, edge_up(edge_h)))
     edge_hard = hardness(edge_log, corners(edge_t, edge_up(edge_t)))
@@ -528,8 +551,8 @@
     for z in range(LEVELS):
         sums = []
         for q, (a, b) in enumerate(parts):
-            rim = jnp.where(lane == 127, at_lane(a, 63 + z), 0.0)
-            rim = jnp.where(lane == 0, at_lane(b, 21 + z), rim)
+            rim = jnp.where(lane == 127, pltpu.roll(a, 64 - z, 1), 0.0)
+            rim = jnp.where(lane == 0, pltpu.roll(b, 107 - z, 1), rim)
             sums.append(partial[q * LEVELS + z] + rim)
         fu, fv, du, dv = sums
         drag = friction if z == 0 else 0.0
@@ -546,16 +569,16 @@
     edge_v = edge_final(1, edge_v, edge_fv)
     for z in range(LEVELS):
         here = lane == 42 + z
-        edge_u = jnp.where(here, at_lane(first[z], 0), edge_u)
-        edge_v = jnp.where(here, at_lane(first[LEVELS + z], 0), edge_v)
+        edge_u = jnp.where(here, pltpu.roll(first[z], 42 + z, 1), edge_u)
+        edge_v = jnp.where(here, pltpu.roll(first[LEVELS + z], 42 + z, 1), edge_v)
     beyond = [b for _, b in edge_parts(edge_u, edge_v)]
 
     def finish(z, results):
         fu, fv, du, dv = [
-            a + jnp.where(lane == 0, at_lane(e, 21 + z), down_y(b))
+            a + jnp.where(lane == 0, pltpu.roll(e, 107 - z, 1), down_y(b))
             for (a, b), e in zip(results, beyond)
         ]
-        drag = jnp.where(z == 0, friction, 0.0)
+        drag = friction if z == 0 else 0.0
         second[z] = stepped(first[z], load_u, fu, du, drag)
         second[LEVELS + z] = stepped(first[LEVELS + z], load_v, fv, dv, drag)
 
@@ -570,33 +593,56 @@
     for c in range(2):
         for z in range(LEVELS):
             out_v[c, z] = second[c * LEVELS + z, 2:6, :]
+    leaving = [pltpu.make_async_copy(out_v, out_v_to, leaves.at[0])]
+    leaving[0].start()
     for c in range(2):
         for l in range(LAYERS):
             at = c * LEVELS + l
             means[8 * (c * LAYERS + l) : 8 * (c * LAYERS + l) + 8, :] = 0.5 * (
                 second[at] + second[at + 1]
             )
-
-    from_x = origin[0:16]
-    from_y = origin[16:32]
-    lane16 = iota((16, 128), 1)
-    here = [from_x == x for x in range(4)]
     send[...] = jnp.zeros(send.shape, f32)
-    for l in range(LAYERS):
-        pair = []
-        for c in range(2):
-            at = 8 * (c * LAYERS + l) + 2
-            value = lanes_of(row_of(means, at, 16), from_y)
-            for x in range(1, 4):
-                value = jnp.where(here[x], lanes_of(row_of(means, at + x, 16), from_y), value)
-            pair.append(value)
-        even, odd = halves(pair[0], pair[1], lane16)
-        start = (l // 5) * 256 + l % 5
-        send[pl.ds(start, 16, stride=16), :] = even
-        send[pl.ds(start + 8, 16, stride=16), :] = odd
-
-
-def prepare_kernel(shaft, origin):
+    for v in range(2):
+        from_x = origin[8 * v : 8 * v + 8]
+        from_y = origin[16 + 8 * v : 24 + 8 * v]
+        here = [from_x == x for x in range(4)]
+        for part in range(4):
+            values = [jnp.zeros((8, 128), f32)] * 10
+            for x in range(4):
+                for i in range(10):
+                    at = 8 * (i // 5 * LAYERS + 5 * part + i % 5) + 2 + x
+                    values[i] = jnp.where(here[x], lanes_of(row_of(means, at, 8), from_y), values[i])
+            for l in range(5):
+                even, odd = halves(values[l], values[5 + l], lane)
+                start = part * 256 + 128 * v + l
+                send[pl.ds(start, 8, stride=16), :] = even
+                send[pl.ds(start + 8, 8, stride=16), :] = odd
+        for part in range(4):
+            span = slice(256 * part + 128 * v, 256 * part + 128 * v + 128)
+            copy = pltpu.make_async_copy(send.at[span], send_to.at[span], leaves.at[1 + 4 * v + part])
+            copy.start()
+            leaving.append(copy)
+    for copy in leaving:
+        copy.wait()
+
+
+def prepare_kernel(donor, shaft, origin, counts, left, hot):
+    row256 = iota((256, 128), 0).astype(bf16)
+    row16 = iota((16, 128), 0).astype(bf16)
+    one = jnp.ones((), bf16)
+    zero = jnp.zeros((), bf16)
+    for g in range(4):
+        ids = joined_rows(donor.at[0, g])
+        for t in range(16):
+            span = slice(2048 * g + 128 * t, 2048 * g + 128 * t + 128)
+            cell = ids[t : t + 1]
+            low = jnp.broadcast_to(cell & 255, (256, 128)).astype(bf16)
+            hot[:, span] = jnp.where(row256 == low, one, zero)
+            high = jnp.broadcast_to(cell >> 8, (16, 128)).astype(bf16)
+            left[:, span] = jnp.where(row16 == high, one, zero)
+    counts[...] = lax.dot_general(
+        left[...], hot[...], (((1,), (1,)), ((), ())), preferred_element_type=f32
+    )
     slot_row = iota((16, 128), 0)
     place = iota((16, 128), 1).astype(f32)
     low_row = iota((128, 128), 0)
@@ -617,48 +663,46 @@
     origin[...] = where_from.astype(jnp.int32) & 127
 
 
-def total_kernel(arrived, donor, out, left, hot):
+def total_kernel(arrived, donor, counts, out, left, hot, rows, sums):
     lane = iota((8, 128), 1)
-    row = iota((8, 128), 0)
     row256 = iota((256, 128), 0).astype(bf16)
+    blocks = [((iota((16, 128), 0) + 16 * t) // 20).astype(bf16) for t in range(20)]
     one = jnp.ones((), bf16)
     zero = jnp.zeros((), bf16)
     ids = [joined_rows(donor.at[0, g]) for g in range(4)]
-    sums = jnp.zeros((256 * SPLITS, 256), f32)
+    result = jnp.zeros((320, 256), f32)
     for step in range(STEPS):
         for part in range(64 // STEPS):
             chunk = 64 // STEPS * step + part
             span = slice(128 * chunk, 128 * chunk + 128)
-            x = arrived[16 * chunk : 16 * chunk + 16, :]
-            u, v = halves(x[:8], x[8:], lane)
-            u = jnp.where(row < 5, u, jnp.where(row == 5, 1.0, 0.0))
-            v = jnp.where(row < 5, v, 0.0)
-            rest = jnp.concatenate([u, v], axis=0)
             cell = ids[chunk // 16][chunk % 16 : chunk % 16 + 1]
             high = jnp.broadcast_to(cell >> 8, (16, 128)).astype(bf16)
             low = jnp.broadcast_to(cell & 255, (256, 128)).astype(bf16)
             hot[:, span] = jnp.where(row256 == low, one, zero)
-            for s in range(SPLITS):
-                piece = rest.astype(bf16)
-                rest = rest - piece.astype(f32)
-                for h in range(16):
-                    at = 256 * s + 16 * h
-                    left[at : at + 16, span] = jnp.where(high == h, piece, zero)
+            x = arrived[16 * chunk : 16 * chunk + 16, :]
+            at = 40 * chunk
+            for c, value in enumerate(halves(x[:8], x[8:], lane)):
+                value = value[:5]
+                big = value.astype(bf16).astype(f32)
+                for i, piece in enumerate((big, value - big)):
+                    start = at + 10 * i + 5 * c
+                    rows[start : start + 5, :] = piece
+                    rows[start + 20 : start + 25, :] = piece
+            tiles = [rows[at + o : at + o + 16, :].astype(bf16) for o in (0, 16, 12, 8, 4)]
+            for t in range(20):
+                left[16 * t : 16 * t + 16, span] = jnp.where(high == blocks[t], tiles[t % 5], zero)
         span = slice(8192 // STEPS * step, 8192 // STEPS * (step + 1))
-        sums = sums + lax.dot_general(
+        result = result + lax.dot_general(
             left[:, span], hot[:, span], (((1,), (1,)), ((), ())), preferred_element_type=f32
         )
+    sums[...] = result
     for h in range(16):
-        total = sums[16 * h : 16 * h + 16]
-        for s in range(1, SPLITS):
-            total = total + sums[256 * s + 16 * h : 256 * s + 16 * h + 16]
-        count = jnp.maximum(total[5:6, :], 1.0)
+        total = sums[20 * h : 20 * h + 10, :] + sums[20 * h + 10 : 20 * h + 20, :]
+        total = total / jnp.maximum(counts[h : h + 1, :], 1.0)
         span = slice(256 * h, 256 * h + 256)
-        u = total[0:5, :] / count
-        v = total[8:13, :] / count
         for l in range(5):
-            out[l, 0:1, span] = u[l : l + 1]
-            out[l, 1:2, span] = v[l : l + 1]
+            out[l, 0:1, span] = total[l : l + 1]
+            out[l, 1:2, span] = total[5 + l : 6 + l]
 
 
 def shape(*sizes):
@@ -697,6 +741,7 @@
             shape(6, 32, 128),
         ),
         in_specs=[pl.BlockSpec(memory_space=pltpu.HBM)] * 7,
+        out_specs=[pl.BlockSpec(memory_space=pltpu.HBM)] * 4,
         scratch_shapes=[
             pltpu.VMEM((32, 128), f32),
             pltpu.VMEM((LAYERS, 4096), f32),
@@ -705,7 +750,12 @@
             pltpu.VMEM((32, 64), jnp.int32),
             pltpu.VMEM((4, 128), jnp.int32),
             pltpu.VMEM((2, LEVELS, 4, 128), f32),
+            pltpu.VMEM((32 * BLOCK_ROWS, 128), f32),
+            pltpu.VMEM((MSG_ROWS, 128), f32),
+            pltpu.VMEM((MSG_ROWS, 128), f32),
+            pltpu.VMEM((6, 32, 128), f32),
             pltpu.SemaphoreType.DMA((7,)),
+            pltpu.SemaphoreType.DMA((5,)),
         ],
         compiler_params=WIDE,
         name="pack",
@@ -722,13 +772,16 @@
     even, odd = near_pairs(lax.axis_size("dom"))
     near = lax.ppermute(near_out, "dom", even)
     far = lax.ppermute(far_out, "dom", odd)
-    shaft, near_out = lax.optimization_barrier((shaft_holding_position, near_out))
-    origin = pl.pallas_call(
+    donor, shaft, near_out = lax.optimization_barrier(
+        (position_donor_polygons, shaft_holding_position, near_out)
+    )
+    origin, counts = pl.pallas_call(
         prepare_kernel,
-        out_shape=jax.ShapeDtypeStruct((32, 128), jnp.int32),
+        out_shape=(jax.ShapeDtypeStruct((32, 128), jnp.int32), shape(16, 256)),
+        scratch_shapes=[pltpu.VMEM((16, 8192), bf16), pltpu.VMEM((256, 8192), bf16)],
         compiler_params=PARAMS,
         name="prepare",
-    )(shaft)
+    )(donor, shaft)
     arrived, origin = lax.optimization_barrier((arrived, origin))
     geo, vext, edge = pl.pallas_call(
         column_kernel,
@@ -754,7 +807,11 @@
             pltpu.VMEM((2 * LEVELS, 8, 128), f32),
             pltpu.VMEM((2 * LEVELS, 8, 128), f32),
             pltpu.VMEM((2 * LAYERS * 8, 128), f32),
+            pltpu.VMEM((2, LEVELS, 4, 128), f32),
+            pltpu.VMEM((1024, 128), f32),
+            pltpu.SemaphoreType.DMA((9,)),
         ],
+        out_specs=[pl.BlockSpec(memory_space=pltpu.HBM)] * 2,
         compiler_params=PARAMS,
         name="velocity",
     )(geo, vext, partial, edge, edge_near, edge_far, origin)
@@ -777,10 +834,15 @@
     tier_motion = pl.pallas_call(
         total_kernel,
         out_shape=shape(5, 2, 4096),
-        scratch_shapes=[pltpu.VMEM((256 * SPLITS, 8192), bf16), pltpu.VMEM((256, 8192), bf16)],
+        scratch_shapes=[
+            pltpu.VMEM((320, 8192), bf16),
+            pltpu.VMEM((256, 8192), bf16),
+            pltpu.VMEM((64 * 40, 128), f32),
+            pltpu.VMEM((320, 256), f32),
+        ],
         compiler_params=PARAMS,
         name="totals",
-    )(back, position_donor_polygons)
+    )(back, position_donor_polygons, counts)
     return (depth.reshape(4096), heat, node_velocity, jnp.transpose(tier_motion, (1, 0, 2)))
 
 

time: 68.6 us -> 64.2 us (0.936)
  Pallas kernels: 26.2 us -> 23 us
  waiting for transfers between devices: 14.7 us -> 13.5 us
    pallas_call x1, Pallas kernels: 6.15 us -> 4.28 us  [shards(): pl.pallas_call(ice_kernel, out_shape=(shape(2, LEVELS, 4, 128), shape(102...]
    pallas_call x1, Pallas kernels: 5.97 us -> 4.16 us  [shards(): pl.pallas_call(pack_kernel, out_shape=(shape(32 * BLOCK_ROWS, 128), shape...]
    all_to_all x1, waiting for transfers between devices: 7.9 us -> 6.67 us  [shards(): lax.all_to_all(outgoing, 'dom', split_axis=0, concat_axis=0, tiled=True)]
    pallas_call x1, Pallas kernels: 0.18 us -> 1.41 us  [shards(): pl.pallas_call(prepare_kernel, out_shape=(jax.ShapeDtypeStruct((32, 128),...]
    pallas_call x1, Pallas kernels: 2.33 us -> 1.59 us  [shards(): pl.pallas_call(inner_kernel, out_shape=shape(4 * LEVELS, 8, 128), compile...]
  transfers between devices with their start and end apart: 6 -> 6, of which waited for: 2 -> 2; matrix products, arithmetic and copies ran while one was open for 0% -> 0% of each run, Pallas kernels for 14% -> 15%
where the time goes in v3:
time: 64.2 us; the launch traced here: 63.9 us
  starting transfers between devices  26.5 us (41%)
  Pallas kernels  23 us (36%)
  waiting for transfers between devices  13.5 us (21%)
  between operations  0.85 us (1%)
    all_to_all x1, starting transfers between devices, shards(): lax.all_to_all(outgoing, 'dom', split_axis=0, concat_axis=0, tiled=True)  11.5 us
    pallas_call x1, Pallas kernels, shards(): pl.pallas_call(advect_kernel, out_shape=(shape(32, 128), shape(5, 4096)),...  6.83 us
    all_to_all x1, waiting for transfers between devices, shards(): lax.all_to_all(send, ('grp', 'dom'), split_axis=0, concat_axis=0, tiled=T...  6.81 us
    all_to_all x1, waiting for transfers between devices, shards(): lax.all_to_all(outgoing, 'dom', split_axis=0, concat_axis=0, tiled=True)  6.67 us
    all_to_all x1, starting transfers between devices, shards(): lax.all_to_all(send, ('grp', 'dom'), split_axis=0, concat_axis=0, tiled=T...  5.59 us
    ppermute x1, starting transfers between devices, shards(): edge_far = lax.ppermute(edge, 'grp', odd)  4.91 us
    pallas_call x1, Pallas kernels, shards(): pl.pallas_call(ice_kernel, out_shape=(shape(2, LEVELS, 4, 128), shape(102...  4.28 us
    pallas_call x1, Pallas kernels, shards(): pl.pallas_call(pack_kernel, out_shape=(shape(32 * BLOCK_ROWS, 128), shape...  4.16 us
  transfers between devices with their start and end apart: 6, of which 2 were waited for; matrix products, arithmetic and copies ran while one was open for 0% of the time, Pallas kernels for 15%

profile of v3, /device:TPU:1, one launch (start us, length us, event | category | flops | bytes accessed | tf_op | source)
XLA Modules:
  0.0 63.9 jit_solution(2905661727329059341)
XLA Ops:
  0.6 4.2 %pack.1 = (f32[1280,128]{1,0:T(8,128)}, f32[136,128]{1,0:T(8,128)}, f32[136,128]{1,0:T(8,128)}, f32[6,32,128]{2,1,0:T(8,128)}) custom-call(f32[32,128]{1,0:T(8,128)} %bitcast.12, f32[20,4096]{1,0:T(8,128)} %heat_in.1, f32[2,4096]{1,0:T(2,128)} %slope_in.1, f32[32,128]{1,0:T(8,128)} %bitcast.13, s32[1,4,32,64]{3,2,1,0:T(8,128)} %donor.2, s32[4,128]{1,0:T(4,128)} %shaft.2, ...), custom_call_target="tpu_custom_call" | custom-call | tf_op jit(solution)/shard_map/pack/pallas_call | solution.py:735
  4.8 0.0 copy-start.9
  4.8 0.0 copy-start.8
  4.8 0.0 copy-start.1
  4.8 0.0 copy-start.2
  4.8 11.5 %all-to-all-start = ((f32[32,40,128]{2,1,0:T(8,128)}), f32[32,40,128]{2,1,0:T(8,128)S(1)}, u32[]{:S(2)}, u32[]{:S(2)}) async-start(f32[32,40,128]{2,1,0:T(8,128)} %bitcast.10), calls=%async_computation | async-start | bytes 1310720 | tf_op jit(solution)/shard_map/all_to_all | solution.py:771
  16.3 0.0 copy-start.7
  16.3 0.0 copy-done.9
  16.4 0.7 %collective-permute-start.1 = (f32[136,128]{1,0:T(8,128)S(1)}, f32[136,128]{1,0:T(8,128)S(1)}, u32[]{:S(2)}, u32[]{:S(2)}) collective-permute-start(f32[136,128]{1,0:T(8,128)S(1)} %copy-done.9), channel_id=1, source_target_pairs={{1,2},{2,1},{3,4},{4,3},{5,6},{6,5},{7,8},{8,7},{9,10},{10,9},{11,... | collective-permute-start | bytes 208904 | tf_op jit(solution)/shard_map/ppermute | solution.py:774
  17.0 0.0 copy-done.8
  17.0 3.7 %collective-permute-start = (f32[136,128]{1,0:T(8,128)S(1)}, f32[136,128]{1,0:T(8,128)S(1)}, u32[]{:S(2)}, u32[]{:S(2)}) collective-permute-start(f32[136,128]{1,0:T(8,128)S(1)} %copy-done.8), channel_id=1, source_target_pairs={{0,1},{1,0},{2,3},{3,2},{4,5},{5,4},{6,7},{7,6},{8,9},{9,8},{10,11... | collective-permute-start | bytes 208904 | tf_op jit(solution)/shard_map/ppermute | solution.py:773
  20.8 0.0 copy-done.1
  20.8 0.0 copy-done.7
  20.8 1.4 %prepare.1 = (s32[32,128]{1,0:T(8,128)S(1)}, f32[16,256]{1,0:T(8,128)S(1)}) custom-call(s32[1,4,32,64]{3,2,1,0:T(8,128)S(1)} %copy-done.1, s32[4,128]{1,0:T(4,128)S(1)} %copy-done.7), custom_call_target="tpu_custom_call" | custom-call | tf_op jit(solution)/shard_map/prepare/pallas_call | solution.py:778
  22.2 6.7 %all-to-all-done = f32[32,40,128]{2,1,0:T(8,128)S(1)} async-done(((f32[32,40,128]{2,1,0:T(8,128)}), f32[32,40,128]{2,1,0:T(8,128)S(1)}, u32[]{:S(2)}, u32[]{:S(2)}) %all-to-all-start) | async-done | bytes 655392 | tf_op jit(solution)/shard_map/all_to_all | solution.py:771
  28.9 0.0 collective-permute-done.1.far
  28.9 0.0 collective-permute-done.near
  28.9 0.0 copy-done.2
  28.9 1.1 %columns.1 = (f32[24,8,128]{2,1,0:T(8,128)S(1)}, f32[42,8,128]{2,1,0:T(8,128)S(1)}, f32[56,128]{1,0:T(8,128)S(1)}) custom-call(f32[1280,128]{1,0:T(8,128)S(1)} %bitcast.8, s32[4,128]{1,0:T(4,128)S(1)} %copy-done.7, f32[136,128]{1,0:T(8,128)S(1)} %collective-permute-done.near, f32[136,128]{1,0:T(8,128)S(1)} %collective-permute-done.1.far, ...), custom_call_target="tpu_custom_call" | custom-call | tf_op jit(solution)/shard_map/columns/pallas_call | solution.py:786
  30.0 4.9 %collective-permute-start.3 = (f32[56,128]{1,0:T(8,128)S(1)}, f32[56,128]{1,0:T(8,128)S(1)}, u32[]{:S(2)}, u32[]{:S(2)}) collective-permute-start(f32[56,128]{1,0:T(8,128)S(1)} %get-tuple-element.33.edge), channel_id=1, source_target_pairs={{32,64},{64,32},{33,65},{65,33},{34,66},{66,34},{35,67},{67,35},{3... | collective-permute-start | bytes 86024 | tf_op jit(solution)/shard_map/ppermute | solution.py:795
  34.9 0.1 collective-permute-start.2
  35.0 1.6 %inner.1.partial = f32[84,8,128]{2,1,0:T(8,128)S(1)} custom-call(f32[24,8,128]{2,1,0:T(8,128)S(1)} %get-tuple-element.31.geo, f32[42,8,128]{2,1,0:T(8,128)S(1)} %get-tuple-element.32.vext), custom_call_target="tpu_custom_call" | custom-call | tf_op jit(solution)/shard_map/inner/pallas_call | solution.py:796
  36.6 0.0 collective-permute-done.3.edge_far
  36.6 0.0 collective-permute-done.2.edge_near
  36.6 0.0 copy-start.6
  36.6 4.3 %velocity.1 = (f32[2,21,4,128]{3,2,1,0:T(4,128)}, f32[1024,128]{1,0:T(8,128)}) custom-call(f32[24,8,128]{2,1,0:T(8,128)S(1)} %get-tuple-element.31.geo, f32[42,8,128]{2,1,0:T(8,128)S(1)} %get-tuple-element.32.vext, f32[84,8,128]{2,1,0:T(8,128)S(1)} %inner.1.partial, f32[56,128]{1,0:T(8,128)S(1)} %get-tuple-element.33.edge, ...), custom_call_target="tpu_custom_call" | custom-call | tf_op jit(solution)/shard_map/velocity/pallas_call | solution.py:802
  40.9 0.0 copy-start
  40.9 0.0 copy-start.3
  40.9 0.0 copy-start.4
  40.9 0.0 copy-start.5
  40.9 5.6 %all-to-all-start.1 = ((f32[128,8,128]{2,1,0:T(8,128)}), f32[128,8,128]{2,1,0:T(8,128)S(1)}, u32[]{:S(2)}, u32[]{:S(2)}) async-start(f32[128,8,128]{2,1,0:T(8,128)} %bitcast.5), calls=%async_computation.1 | async-start | bytes 1048576 | tf_op jit(solution)/shard_map/all_to_all | solution.py:818
  46.5 0.0 copy-done.6
  46.5 0.0 copy-done
  46.5 0.0 copy-done.3
  46.6 0.0 copy-done.4
  46.6 0.0 copy-done.5
  46.6 6.8 %advect.1 = (f32[32,128]{1,0:T(8,128)}, f32[5,4096]{1,0:T(8,128)}) custom-call(f32[6,32,128]{2,1,0:T(8,128)S(1)} %copy-done.6, s32[6,4096]{1,0:T(8,128)S(1)} %copy-done.3, f32[6,4096]{1,0:T(8,128)S(1)} %copy-done.4, f32[6,4096]{1,0:T(8,128)S(1)} %copy-done.5, f32[5,6,4096]{2,1,0:T(8,128)S(1)} %copy-done, f32[136,128]{1,0:T(8,128)S(1)} %collective-permute-done.near, ...), custom_call_target="tpu_custom_call" | custom-call | tf_op jit(solution)/shard_map/advect/pallas_call | solution.py:819
  53.4 6.8 %all-to-all-done.1 = f32[128,8,128]{2,1,0:T(8,128)S(1)} async-done(((f32[128,8,128]{2,1,0:T(8,128)}), f32[128,8,128]{2,1,0:T(8,128)S(1)}, u32[]{:S(2)}, u32[]{:S(2)}) %all-to-all-start.1) | async-done | bytes 524320 | tf_op jit(solution)/shard_map/all_to_all | solution.py:818
  60.2 3.7 %totals.1 = f32[5,2,4096]{2,1,0:T(2,128)} custom-call(f32[1024,128]{1,0:T(8,128)S(1)} %bitcast.9, s32[1,4,32,64]{3,2,1,0:T(8,128)S(1)} %copy-done.1, f32[16,256]{1,0:T(8,128)S(1)} %get-tuple-element.37.counts), custom_call_target="tpu_custom_call" | custom-call | tf_op jit(solution)/shard_map/totals/pallas_call | solution.py:834
Async XLA Ops:
  4.8 11.6 %copy-start.9 = (f32[136,128]{1,0:T(8,128)S(1)}, f32[136,128]{1,0:T(8,128)}, u32[]{:S(2)}) copy-start(f32[136,128]{1,0:T(8,128)} %get-tuple-element.23) | copy-start | bytes 208900
  4.8 12.2 %copy-start.8 = (f32[136,128]{1,0:T(8,128)S(1)}, f32[136,128]{1,0:T(8,128)}, u32[]{:S(2)}) copy-start(f32[136,128]{1,0:T(8,128)} %get-tuple-element.22) | copy-start | bytes 208900
  4.8 16.0 %copy-start.1 = (s32[1,4,32,64]{3,2,1,0:T(8,128)S(1)}, s32[1,4,32,64]{3,2,1,0:T(8,128)}, u32[]{:S(2)}) copy-start(s32[1,4,32,64]{3,2,1,0:T(8,128)} %donor.2) | copy-start | bytes 98308
  4.8 24.0 %copy-start.2 = (f32[2,21,4,128]{3,2,1,0:T(4,128)S(1)}, f32[2,21,4,128]{3,2,1,0:T(4,128)}, u32[]{:S(2)}) copy-start(f32[2,21,4,128]{3,2,1,0:T(4,128)} %prior.1) | copy-start | bytes 258052
  4.8 24.0 %all-to-all-start = ((f32[32,40,128]{2,1,0:T(8,128)}), f32[32,40,128]{2,1,0:T(8,128)S(1)}, u32[]{:S(2)}, u32[]{:S(2)}) async-start(f32[32,40,128]{2,1,0:T(8,128)} %bitcast.10), calls=%async_computation | async-start | bytes 1310720 | tf_op jit(solution)/shard_map/all_to_all | solution.py:771
  16.3 4.4 %copy-start.7 = (s32[4,128]{1,0:T(4,128)S(1)}, s32[4,128]{1,0:T(4,128)}, u32[]{:S(2)}) copy-start(s32[4,128]{1,0:T(4,128)} %shaft.2) | copy-start | bytes 6148
  16.4 12.5 %collective-permute-start.1 = (f32[136,128]{1,0:T(8,128)S(1)}, f32[136,128]{1,0:T(8,128)S(1)}, u32[]{:S(2)}, u32[]{:S(2)}) collective-permute-start(f32[136,128]{1,0:T(8,128)S(1)} %copy-done.9), channel_id=1, source_target_pairs={{1,2},{2,1},{3,4},{4,3},{5,6},{6,5},{7,8},{8,7},{9,10},{10,9},{11,... | collective-permute-start | bytes 208904 | tf_op jit(solution)/shard_map/ppermute | solution.py:774
  17.0 11.8 %collective-permute-start = (f32[136,128]{1,0:T(8,128)S(1)}, f32[136,128]{1,0:T(8,128)S(1)}, u32[]{:S(2)}, u32[]{:S(2)}) collective-permute-start(f32[136,128]{1,0:T(8,128)S(1)} %copy-done.8), channel_id=1, source_target_pairs={{0,1},{1,0},{2,3},{3,2},{4,5},{5,4},{6,7},{7,6},{8,9},{9,8},{10,11... | collective-permute-start | bytes 208904 | tf_op jit(solution)/shard_map/ppermute | solution.py:773
  30.0 6.6 %collective-permute-start.3 = (f32[56,128]{1,0:T(8,128)S(1)}, f32[56,128]{1,0:T(8,128)S(1)}, u32[]{:S(2)}, u32[]{:S(2)}) collective-permute-start(f32[56,128]{1,0:T(8,128)S(1)} %get-tuple-element.33.edge), channel_id=1, source_target_pairs={{32,64},{64,32},{33,65},{65,33},{34,66},{66,34},{35,67},{67,35},{3... | collective-permute-start | bytes 86024 | tf_op jit(solution)/shard_map/ppermute | solution.py:795
  34.9 1.7 %collective-permute-start.2 = (f32[56,128]{1,0:T(8,128)S(1)}, f32[56,128]{1,0:T(8,128)S(1)}, u32[]{:S(2)}, u32[]{:S(2)}) collective-permute-start(f32[56,128]{1,0:T(8,128)S(1)} %get-tuple-element.33.edge), channel_id=1, source_target_pairs={{0,32},{32,0},{64,96},{96,64},{1,33},{33,1},{65,97},{97,65},{2,34}... | collective-permute-start | bytes 86024 | tf_op jit(solution)/shard_map/ppermute | solution.py:794
  36.6 10.0 %copy-start.6 = (f32[6,32,128]{2,1,0:T(8,128)S(1)}, f32[6,32,128]{2,1,0:T(8,128)}, u32[]{:S(2)}) copy-start(f32[6,32,128]{2,1,0:T(8,128)} %get-tuple-element.21.own) | copy-start | bytes 294916
  40.9 5.7 %copy-start = (f32[5,6,4096]{2,1,0:T(8,128)S(1)}, f32[5,6,4096]{2,1,0:T(8,128)}, u32[]{:S(2)}) copy-start(f32[5,6,4096]{2,1,0:T(8,128)} %tier_speed.1) | copy-start | bytes 1474564
  40.9 5.7 %copy-start.3 = (s32[6,4096]{1,0:T(8,128)S(1)}, s32[6,4096]{1,0:T(8,128)}, u32[]{:S(2)}) copy-start(s32[6,4096]{1,0:T(8,128)} %adjacent.1) | copy-start | bytes 294916
  40.9 5.7 %copy-start.4 = (f32[6,4096]{1,0:T(8,128)S(1)}, f32[6,4096]{1,0:T(8,128)}, u32[]{:S(2)}) copy-start(f32[6,4096]{1,0:T(8,128)} %ratio.1) | copy-start | bytes 294916
  40.9 5.7 %copy-start.5 = (f32[6,4096]{1,0:T(8,128)S(1)}, f32[6,4096]{1,0:T(8,128)}, u32[]{:S(2)}) copy-start(f32[6,4096]{1,0:T(8,128)} %mean_speed.1) | copy-start | bytes 294916
  40.9 19.3 %all-to-all-start.1 = ((f32[128,8,128]{2,1,0:T(8,128)}), f32[128,8,128]{2,1,0:T(8,128)S(1)}, u32[]{:S(2)}, u32[]{:S(2)}) async-start(f32[128,8,128]{2,1,0:T(8,128)} %bitcast.5), calls=%async_computation.1 | async-start | bytes 1048576 | tf_op jit(solution)/shard_map/all_to_all | solution.py:818

commit v4 on v3

--- a/solution.py
+++ b/solution.py
@@ -15,9 +15,9 @@
 LEVELS = 21
 FIELDS = 24
 PAIRS = 12
-BLOCK_ROWS = 40
+BLOCK_ROWS = 36
 MSG_ROWS = 136
-STEPS = 4
+STEPS = 8
 f32 = jnp.float32
 bf16 = jnp.bfloat16
 PARAMS = pltpu.CompilerParams(vmem_limit_bytes=32 * 1024 * 1024)
@@ -66,52 +66,10 @@
     for copy in copies:
         copy.start()
     out[0:12, :] = jnp.zeros((12, 128), f32)
-    out[31 * 40 + 24 : 31 * 40 + 36, :] = jnp.zeros((12, 128), f32)
-    for k in range(32):
-        out[40 * k + 36 : 40 * k + 40, :] = jnp.zeros((4, 128), f32)
-    for copy in copies:
+    out[31 * 36 + 24 : 31 * 36 + 36, :] = jnp.zeros((12, 128), f32)
+    for copy in copies[:5]:
         copy.wait()
-
-    own[0] = ice[...]
-    for part in range(4):
-
-        @pl.when(g == part)
-        def _():
-            for i in range(5):
-                layer = 5 * part + i
-                for k in range(32):
-                    own[i + 1, k : k + 1, :] = heat[layer : layer + 1, 128 * k : 128 * k + 128]
-
-    def message(msg, row0, chunk0):
-        for c in range(2):
-            for z in range(LEVELS):
-                at = 2 * (c * LEVELS + z)
-                msg[at : at + 2, :] = prior[c, z, row0 : row0 + 2, :]
-        msg[84:86, :] = shaft[row0 : row0 + 2, :].astype(f32)
-        msg[86:88, :] = jnp.zeros((2, 128), f32)
-        for i in range(6):
-            msg[88 + 8 * i : 96 + 8 * i, :] = own[i, chunk0 : chunk0 + 8, :]
-
-    even_device = d % 2 == 0
-
-    @pl.when(even_device)
-    def _():
-        message(near, 2, 24)
-        message(far, 0, 0)
-
-    @pl.when(jnp.logical_not(even_device))
-    def _():
-        message(near, 0, 0)
-        message(far, 2, 24)
-
-    leaving = [
-        pltpu.make_async_copy(near, near_to, leaves.at[0]),
-        pltpu.make_async_copy(far, far_to, leaves.at[1]),
-        pltpu.make_async_copy(own, own_to, leaves.at[2]),
-    ]
-    for copy in leaving:
-        copy.start()
-
+    leaving = []
     ids = jnp.maximum(joined_rows(donor), 0)
     high = ids >> 7
     low = ids & 127
@@ -136,21 +94,59 @@
             here = highs[v] == k
             for f in range(FIELDS):
                 found[f] = jnp.where(here, lanes_of(table(f, k), lows[v]), found[f])
-        at = 640 * v
+        at = 576 * v
         for p in range(PAIRS):
             even, odd = halves(found[p], found[p + PAIRS], lane)
-            out[pl.ds(at + 12 + p, 8, stride=80), :] = even
-            out[pl.ds(at + 40 + p, 8, stride=80), :] = even
+            out[pl.ds(at + 12 + p, 8, stride=72), :] = even
+            out[pl.ds(at + 36 + p, 8, stride=72), :] = even
             if v == 0:
-                out[pl.ds(64 + p, 7, stride=80), :] = even[1:]
-                out[pl.ds(80 + p, 8, stride=80), :] = odd
+                out[pl.ds(60 + p, 7, stride=72), :] = even[1:]
+                out[pl.ds(72 + p, 8, stride=72), :] = odd
             else:
-                out[pl.ds(at - 16 + p, 8, stride=80), :] = even
-                out[pl.ds(at + 80 + p, 7, stride=80), :] = odd[:7]
-            out[pl.ds(at + 52 + p, 8, stride=80), :] = odd
-            out[pl.ds(at + 24 + p, 8, stride=80), :] = odd
-        span = slice(0, 600) if v == 0 else slice(600, 1280)
+                out[pl.ds(at - 12 + p, 8, stride=72), :] = even
+                out[pl.ds(at + 72 + p, 7, stride=72), :] = odd[:7]
+            out[pl.ds(at + 48 + p, 8, stride=72), :] = odd
+            out[pl.ds(at + 24 + p, 8, stride=72), :] = odd
+        span = slice(0, 536) if v == 0 else slice(536, 1152)
         copy = pltpu.make_async_copy(out.at[span], out_to.at[span], leaves.at[3 + v])
+        copy.start()
+        leaving.append(copy)
+    for copy in copies[5:]:
+        copy.wait()
+    own[0] = ice[...]
+    for part in range(4):
+
+        @pl.when(g == part)
+        def _():
+            for i in range(5):
+                layer = 5 * part + i
+                for k in range(32):
+                    own[i + 1, k : k + 1, :] = heat[layer : layer + 1, 128 * k : 128 * k + 128]
+
+    def message(msg, row0, chunk0):
+        for c in range(2):
+            for z in range(LEVELS):
+                at = 2 * (c * LEVELS + z)
+                msg[at : at + 2, :] = prior[c, z, row0 : row0 + 2, :]
+        msg[84:86, :] = shaft[row0 : row0 + 2, :].astype(f32)
+        msg[86:88, :] = jnp.zeros((2, 128), f32)
+        for i in range(6):
+            msg[88 + 8 * i : 96 + 8 * i, :] = own[i, chunk0 : chunk0 + 8, :]
+
+    even_device = d % 2 == 0
+
+    @pl.when(even_device)
+    def _():
+        message(near, 2, 24)
+        message(far, 0, 0)
+
+    @pl.when(jnp.logical_not(even_device))
+    def _():
+        message(near, 0, 0)
+        message(far, 2, 24)
+
+    for i, (a, b) in enumerate(((near, near_to), (far, far_to), (own, own_to))):
+        copy = pltpu.make_async_copy(a, b, leaves.at[i])
         copy.start()
         leaving.append(copy)
     for copy in leaving:
@@ -768,7 +764,9 @@
         shaft_holding_position,
         prior_node_motion,
     )
-    arrived = lax.all_to_all(outgoing, "dom", split_axis=0, concat_axis=0, tiled=True)
+    arrived = lax.all_to_all(
+        outgoing.reshape(32, 1, BLOCK_ROWS * 128), "dom", split_axis=0, concat_axis=0, tiled=True
+    ).reshape(32 * BLOCK_ROWS, 128)
     even, odd = near_pairs(lax.axis_size("dom"))
     near = lax.ppermute(near_out, "dom", even)
     far = lax.ppermute(far_out, "dom", odd)

time: 64.2 us -> 63.3 us (0.986)
  transfers between devices with their start and end apart: 6 -> 6, of which waited for: 2 -> 2; matrix products, arithmetic and copies ran while one was open for 0% -> 0% of each run, Pallas kernels for 15% -> 16%
where the time goes in v4:
time: 63.3 us; the launch traced here: 63 us
  starting transfers between devices  26.5 us (42%)
  Pallas kernels  22.8 us (36%)
  waiting for transfers between devices  12.9 us (20%)
  between operations  0.85 us (1%)
    all_to_all x1, starting transfers between devices, shards(): lax.all_to_all(outgoing.reshape(32, 1, BLOCK_ROWS * 128), 'dom', split_ax...  11.5 us
    pallas_call x1, Pallas kernels, shards(): pl.pallas_call(advect_kernel, out_shape=(shape(32, 128), shape(5, 4096)),...  6.83 us
    all_to_all x1, waiting for transfers between devices, shards(): lax.all_to_all(send, ('grp', 'dom'), split_axis=0, concat_axis=0, tiled=T...  6.81 us
    all_to_all x1, waiting for transfers between devices, shards(): lax.all_to_all(outgoing.reshape(32, 1, BLOCK_ROWS * 128), 'dom', split_ax...  6.04 us
    all_to_all x1, starting transfers between devices, shards(): lax.all_to_all(send, ('grp', 'dom'), split_axis=0, concat_axis=0, tiled=T...  5.6 us
    ppermute x1, starting transfers between devices, shards(): edge_far = lax.ppermute(edge, 'grp', odd)  4.89 us
    pallas_call x1, Pallas kernels, shards(): pl.pallas_call(ice_kernel, out_shape=(shape(2, LEVELS, 4, 128), shape(102...  4.28 us
    pallas_call x1, Pallas kernels, shards(): pl.pallas_call(pack_kernel, out_shape=(shape(32 * BLOCK_ROWS, 128), shape...  3.96 us
  transfers between devices with their start and end apart: 6, of which 2 were waited for; matrix products, arithmetic and copies ran while one was open for 0% of the time, Pallas kernels for 16%

profile of v4, /device:TPU:1, one launch (start us, length us, event | category | flops | bytes accessed | tf_op | source)
XLA Modules:
  0.0 63.0 jit_solution(5011715903180331291)
XLA Ops:
  0.6 4.0 %pack.1 = (f32[1152,128]{1,0:T(8,128)}, f32[136,128]{1,0:T(8,128)}, f32[136,128]{1,0:T(8,128)}, f32[6,32,128]{2,1,0:T(8,128)}) custom-call(f32[32,128]{1,0:T(8,128)} %bitcast.12, f32[20,4096]{1,0:T(8,128)} %heat_in.1, f32[2,4096]{1,0:T(2,128)} %slope_in.1, f32[32,128]{1,0:T(8,128)} %bitcast.13, s32[1,4,32,64]{3,2,1,0:T(8,128)} %donor.2, s32[4,128]{1,0:T(4,128)} %shaft.2, ...), custom_call_target="tpu_custom_call" | custom-call | tf_op jit(solution)/shard_map/pack/pallas_call | solution.py:731
  4.6 0.0 copy-start.9
  4.6 0.0 copy-start.8
  4.6 0.0 copy-start.1
  4.6 0.0 copy-start.2
  4.6 11.5 %all-to-all-start = ((f32[32,1,4608]{2,1,0:T(1,128)}), f32[32,1,4608]{2,1,0:T(1,128)S(1)}, u32[]{:S(2)}, u32[]{:S(2)}) async-start(f32[32,1,4608]{2,1,0:T(1,128)} %bitcast.10), calls=%async_computation | async-start | bytes 1179648 | tf_op jit(solution)/shard_map/all_to_all | solution.py:767
  16.1 0.0 copy-start.7
  16.2 0.0 copy-done.9
  16.2 0.7 %collective-permute-start.1 = (f32[136,128]{1,0:T(8,128)S(1)}, f32[136,128]{1,0:T(8,128)S(1)}, u32[]{:S(2)}, u32[]{:S(2)}) collective-permute-start(f32[136,128]{1,0:T(8,128)S(1)} %copy-done.9), channel_id=1, source_target_pairs={{1,2},{2,1},{3,4},{4,3},{5,6},{6,5},{7,8},{8,7},{9,10},{10,9},{11,... | collective-permute-start | bytes 208904 | tf_op jit(solution)/shard_map/ppermute | solution.py:772
  16.8 0.0 copy-done.8
  16.8 3.7 %collective-permute-start = (f32[136,128]{1,0:T(8,128)S(1)}, f32[136,128]{1,0:T(8,128)S(1)}, u32[]{:S(2)}, u32[]{:S(2)}) collective-permute-start(f32[136,128]{1,0:T(8,128)S(1)} %copy-done.8), channel_id=1, source_target_pairs={{0,1},{1,0},{2,3},{3,2},{4,5},{5,4},{6,7},{7,6},{8,9},{9,8},{10,11... | collective-permute-start | bytes 208904 | tf_op jit(solution)/shard_map/ppermute | solution.py:771
  20.6 0.0 copy-done.1
  20.6 0.0 copy-done.7
  20.6 1.4 %prepare.1 = (s32[32,128]{1,0:T(8,128)S(1)}, f32[16,256]{1,0:T(8,128)S(1)}) custom-call(s32[1,4,32,64]{3,2,1,0:T(8,128)S(1)} %copy-done.1, s32[4,128]{1,0:T(4,128)S(1)} %copy-done.7), custom_call_target="tpu_custom_call" | custom-call | tf_op jit(solution)/shard_map/prepare/pallas_call | solution.py:776
  22.0 6.0 %all-to-all-done = f32[32,1,4608]{2,1,0:T(1,128)S(1)} async-done(((f32[32,1,4608]{2,1,0:T(1,128)}), f32[32,1,4608]{2,1,0:T(1,128)S(1)}, u32[]{:S(2)}, u32[]{:S(2)}) %all-to-all-start) | async-done | bytes 589856 | tf_op jit(solution)/shard_map/all_to_all | solution.py:767
  28.0 0.0 collective-permute-done.1.far
  28.0 0.0 collective-permute-done.near
  28.0 0.0 copy-done.2
  28.0 1.1 %columns.1 = (f32[24,8,128]{2,1,0:T(8,128)S(1)}, f32[42,8,128]{2,1,0:T(8,128)S(1)}, f32[56,128]{1,0:T(8,128)S(1)}) custom-call(f32[1152,128]{1,0:T(8,128)S(1)} %bitcast.8, s32[4,128]{1,0:T(4,128)S(1)} %copy-done.7, f32[136,128]{1,0:T(8,128)S(1)} %collective-permute-done.near, f32[136,128]{1,0:T(8,128)S(1)} %collective-permute-done.1.far, ...), custom_call_target="tpu_custom_call" | custom-call | tf_op jit(solution)/shard_map/columns/pallas_call | solution.py:784
  29.1 4.9 %collective-permute-start.3 = (f32[56,128]{1,0:T(8,128)S(1)}, f32[56,128]{1,0:T(8,128)S(1)}, u32[]{:S(2)}, u32[]{:S(2)}) collective-permute-start(f32[56,128]{1,0:T(8,128)S(1)} %get-tuple-element.33.edge), channel_id=1, source_target_pairs={{32,64},{64,32},{33,65},{65,33},{34,66},{66,34},{35,67},{67,35},{3... | collective-permute-start | bytes 86024 | tf_op jit(solution)/shard_map/ppermute | solution.py:793
  34.0 0.1 collective-permute-start.2
  34.1 1.6 %inner.1.partial = f32[84,8,128]{2,1,0:T(8,128)S(1)} custom-call(f32[24,8,128]{2,1,0:T(8,128)S(1)} %get-tuple-element.31.geo, f32[42,8,128]{2,1,0:T(8,128)S(1)} %get-tuple-element.32.vext), custom_call_target="tpu_custom_call" | custom-call | tf_op jit(solution)/shard_map/inner/pallas_call | solution.py:794
  35.7 0.0 collective-permute-done.3.edge_far
  35.7 0.0 collective-permute-done.2.edge_near
  35.7 0.0 copy-start.6
  35.7 4.3 %velocity.1 = (f32[2,21,4,128]{3,2,1,0:T(4,128)}, f32[1024,128]{1,0:T(8,128)}) custom-call(f32[24,8,128]{2,1,0:T(8,128)S(1)} %get-tuple-element.31.geo, f32[42,8,128]{2,1,0:T(8,128)S(1)} %get-tuple-element.32.vext, f32[84,8,128]{2,1,0:T(8,128)S(1)} %inner.1.partial, f32[56,128]{1,0:T(8,128)S(1)} %get-tuple-element.33.edge, ...), custom_call_target="tpu_custom_call" | custom-call | tf_op jit(solution)/shard_map/velocity/pallas_call | solution.py:800
  40.0 0.0 copy-start
  40.0 0.0 copy-start.3
  40.1 0.0 copy-start.4
  40.1 0.0 copy-start.5
  40.1 5.6 %all-to-all-start.1 = ((f32[128,8,128]{2,1,0:T(8,128)}), f32[128,8,128]{2,1,0:T(8,128)S(1)}, u32[]{:S(2)}, u32[]{:S(2)}) async-start(f32[128,8,128]{2,1,0:T(8,128)} %bitcast.5), calls=%async_computation.1 | async-start | bytes 1048576 | tf_op jit(solution)/shard_map/all_to_all | solution.py:816
  45.7 0.0 copy-done.6
  45.7 0.0 copy-done
  45.7 0.0 copy-done.3
  45.7 0.0 copy-done.4
  45.7 0.0 copy-done.5
  45.7 6.8 %advect.1 = (f32[32,128]{1,0:T(8,128)}, f32[5,4096]{1,0:T(8,128)}) custom-call(f32[6,32,128]{2,1,0:T(8,128)S(1)} %copy-done.6, s32[6,4096]{1,0:T(8,128)S(1)} %copy-done.3, f32[6,4096]{1,0:T(8,128)S(1)} %copy-done.4, f32[6,4096]{1,0:T(8,128)S(1)} %copy-done.5, f32[5,6,4096]{2,1,0:T(8,128)S(1)} %copy-done, f32[136,128]{1,0:T(8,128)S(1)} %collective-permute-done.near, ...), custom_call_target="tpu_custom_call" | custom-call | tf_op jit(solution)/shard_map/advect/pallas_call | solution.py:817
  52.6 6.8 %all-to-all-done.1 = f32[128,8,128]{2,1,0:T(8,128)S(1)} async-done(((f32[128,8,128]{2,1,0:T(8,128)}), f32[128,8,128]{2,1,0:T(8,128)S(1)}, u32[]{:S(2)}, u32[]{:S(2)}) %all-to-all-start.1) | async-done | bytes 524320 | tf_op jit(solution)/shard_map/all_to_all | solution.py:816
  59.4 3.6 %totals.1 = f32[5,2,4096]{2,1,0:T(2,128)} custom-call(f32[1024,128]{1,0:T(8,128)S(1)} %bitcast.9, s32[1,4,32,64]{3,2,1,0:T(8,128)S(1)} %copy-done.1, f32[16,256]{1,0:T(8,128)S(1)} %get-tuple-element.37.counts), custom_call_target="tpu_custom_call" | custom-call | tf_op jit(solution)/shard_map/totals/pallas_call | solution.py:832
Async XLA Ops:
  4.6 11.6 %copy-start.9 = (f32[136,128]{1,0:T(8,128)S(1)}, f32[136,128]{1,0:T(8,128)}, u32[]{:S(2)}) copy-start(f32[136,128]{1,0:T(8,128)} %get-tuple-element.23) | copy-start | bytes 208900
  4.6 12.2 %copy-start.8 = (f32[136,128]{1,0:T(8,128)S(1)}, f32[136,128]{1,0:T(8,128)}, u32[]{:S(2)}) copy-start(f32[136,128]{1,0:T(8,128)} %get-tuple-element.22) | copy-start | bytes 208900
  4.6 16.0 %copy-start.1 = (s32[1,4,32,64]{3,2,1,0:T(8,128)S(1)}, s32[1,4,32,64]{3,2,1,0:T(8,128)}, u32[]{:S(2)}) copy-start(s32[1,4,32,64]{3,2,1,0:T(8,128)} %donor.2) | copy-start | bytes 98308
  4.6 23.4 %copy-start.2 = (f32[2,21,4,128]{3,2,1,0:T(4,128)S(1)}, f32[2,21,4,128]{3,2,1,0:T(4,128)}, u32[]{:S(2)}) copy-start(f32[2,21,4,128]{3,2,1,0:T(4,128)} %prior.1) | copy-start | bytes 258052
  4.6 23.4 %all-to-all-start = ((f32[32,1,4608]{2,1,0:T(1,128)}), f32[32,1,4608]{2,1,0:T(1,128)S(1)}, u32[]{:S(2)}, u32[]{:S(2)}) async-start(f32[32,1,4608]{2,1,0:T(1,128)} %bitcast.10), calls=%async_computation | async-start | bytes 1179648 | tf_op jit(solution)/shard_map/all_to_all | solution.py:767
  16.1 4.4 %copy-start.7 = (s32[4,128]{1,0:T(4,128)S(1)}, s32[4,128]{1,0:T(4,128)}, u32[]{:S(2)}) copy-start(s32[4,128]{1,0:T(4,128)} %shaft.2) | copy-start | bytes 6148
  16.2 11.9 %collective-permute-start.1 = (f32[136,128]{1,0:T(8,128)S(1)}, f32[136,128]{1,0:T(8,128)S(1)}, u32[]{:S(2)}, u32[]{:S(2)}) collective-permute-start(f32[136,128]{1,0:T(8,128)S(1)} %copy-done.9), channel_id=1, source_target_pairs={{1,2},{2,1},{3,4},{4,3},{5,6},{6,5},{7,8},{8,7},{9,10},{10,9},{11,... | collective-permute-start | bytes 208904 | tf_op jit(solution)/shard_map/ppermute | solution.py:772
  16.8 11.2 %collective-permute-start = (f32[136,128]{1,0:T(8,128)S(1)}, f32[136,128]{1,0:T(8,128)S(1)}, u32[]{:S(2)}, u32[]{:S(2)}) collective-permute-start(f32[136,128]{1,0:T(8,128)S(1)} %copy-done.8), channel_id=1, source_target_pairs={{0,1},{1,0},{2,3},{3,2},{4,5},{5,4},{6,7},{7,6},{8,9},{9,8},{10,11... | collective-permute-start | bytes 208904 | tf_op jit(solution)/shard_map/ppermute | solution.py:771
  29.1 6.6 %collective-permute-start.3 = (f32[56,128]{1,0:T(8,128)S(1)}, f32[56,128]{1,0:T(8,128)S(1)}, u32[]{:S(2)}, u32[]{:S(2)}) collective-permute-start(f32[56,128]{1,0:T(8,128)S(1)} %get-tuple-element.33.edge), channel_id=1, source_target_pairs={{32,64},{64,32},{33,65},{65,33},{34,66},{66,34},{35,67},{67,35},{3... | collective-permute-start | bytes 86024 | tf_op jit(solution)/shard_map/ppermute | solution.py:793
  34.0 1.7 %collective-permute-start.2 = (f32[56,128]{1,0:T(8,128)S(1)}, f32[56,128]{1,0:T(8,128)S(1)}, u32[]{:S(2)}, u32[]{:S(2)}) collective-permute-start(f32[56,128]{1,0:T(8,128)S(1)} %get-tuple-element.33.edge), channel_id=1, source_target_pairs={{0,32},{32,0},{64,96},{96,64},{1,33},{33,1},{65,97},{97,65},{2,34}... | collective-permute-start | bytes 86024 | tf_op jit(solution)/shard_map/ppermute | solution.py:792
  35.7 10.0 %copy-start.6 = (f32[6,32,128]{2,1,0:T(8,128)S(1)}, f32[6,32,128]{2,1,0:T(8,128)}, u32[]{:S(2)}) copy-start(f32[6,32,128]{2,1,0:T(8,128)} %get-tuple-element.21.own) | copy-start | bytes 294916
  40.0 5.7 %copy-start = (f32[5,6,4096]{2,1,0:T(8,128)S(1)}, f32[5,6,4096]{2,1,0:T(8,128)}, u32[]{:S(2)}) copy-start(f32[5,6,4096]{2,1,0:T(8,128)} %tier_speed.1) | copy-start | bytes 1474564
  40.0 5.7 %copy-start.3 = (s32[6,4096]{1,0:T(8,128)S(1)}, s32[6,4096]{1,0:T(8,128)}, u32[]{:S(2)}) copy-start(s32[6,4096]{1,0:T(8,128)} %adjacent.1) | copy-start | bytes 294916
  40.1 5.7 %copy-start.4 = (f32[6,4096]{1,0:T(8,128)S(1)}, f32[6,4096]{1,0:T(8,128)}, u32[]{:S(2)}) copy-start(f32[6,4096]{1,0:T(8,128)} %ratio.1) | copy-start | bytes 294916
  40.1 5.7 %copy-start.5 = (f32[6,4096]{1,0:T(8,128)S(1)}, f32[6,4096]{1,0:T(8,128)}, u32[]{:S(2)}) copy-start(f32[6,4096]{1,0:T(8,128)} %mean_speed.1) | copy-start | bytes 294916
  40.1 19.3 %all-to-all-start.1 = ((f32[128,8,128]{2,1,0:T(8,128)}), f32[128,8,128]{2,1,0:T(8,128)S(1)}, u32[]{:S(2)}, u32[]{:S(2)}) async-start(f32[128,8,128]{2,1,0:T(8,128)} %bitcast.5), calls=%async_computation.1 | async-start | bytes 1048576 | tf_op jit(solution)/shard_map/all_to_all | solution.py:816

commit v5 on v4

--- a/solution.py
+++ b/solution.py
@@ -17,7 +17,7 @@
 PAIRS = 12
 BLOCK_ROWS = 36
 MSG_ROWS = 136
-STEPS = 8
+WIDTH = 256
 f32 = jnp.float32
 bf16 = jnp.bfloat16
 PARAMS = pltpu.CompilerParams(vmem_limit_bytes=32 * 1024 * 1024)
@@ -659,37 +659,38 @@
     origin[...] = where_from.astype(jnp.int32) & 127
 
 
-def total_kernel(arrived, donor, counts, out, left, hot, rows, sums):
+def total_kernel(arrived, donor, counts, out, rows, sums):
     lane = iota((8, 128), 1)
-    row256 = iota((256, 128), 0).astype(bf16)
-    blocks = [((iota((16, 128), 0) + 16 * t) // 20).astype(bf16) for t in range(20)]
+    row256 = iota((256, WIDTH), 0).astype(bf16)
+    blocks = [((iota((16, WIDTH), 0) + 16 * t) // 20).astype(bf16) for t in range(20)]
     one = jnp.ones((), bf16)
     zero = jnp.zeros((), bf16)
     ids = [joined_rows(donor.at[0, g]) for g in range(4)]
     result = jnp.zeros((320, 256), f32)
-    for step in range(STEPS):
-        for part in range(64 // STEPS):
-            chunk = 64 // STEPS * step + part
-            span = slice(128 * chunk, 128 * chunk + 128)
-            cell = ids[chunk // 16][chunk % 16 : chunk % 16 + 1]
-            high = jnp.broadcast_to(cell >> 8, (16, 128)).astype(bf16)
-            low = jnp.broadcast_to(cell & 255, (256, 128)).astype(bf16)
-            hot[:, span] = jnp.where(row256 == low, one, zero)
+    for step in range(8192 // WIDTH):
+        cells = []
+        for part in range(WIDTH // 128):
+            chunk = WIDTH // 128 * step + part
+            cells.append(ids[chunk // 16][chunk % 16 : chunk % 16 + 1])
             x = arrived[16 * chunk : 16 * chunk + 16, :]
-            at = 40 * chunk
+            span = slice(128 * part, 128 * part + 128)
             for c, value in enumerate(halves(x[:8], x[8:], lane)):
                 value = value[:5]
                 big = value.astype(bf16).astype(f32)
                 for i, piece in enumerate((big, value - big)):
-                    start = at + 10 * i + 5 * c
-                    rows[start : start + 5, :] = piece
-                    rows[start + 20 : start + 25, :] = piece
-            tiles = [rows[at + o : at + o + 16, :].astype(bf16) for o in (0, 16, 12, 8, 4)]
-            for t in range(20):
-                left[16 * t : 16 * t + 16, span] = jnp.where(high == blocks[t], tiles[t % 5], zero)
-        span = slice(8192 // STEPS * step, 8192 // STEPS * (step + 1))
+                    start = 40 * step + 10 * i + 5 * c
+                    rows[start : start + 5, span] = piece
+                    rows[start + 20 : start + 25, span] = piece
+        cell = jnp.concatenate(cells, axis=1)
+        high = jnp.broadcast_to(cell >> 8, (16, WIDTH)).astype(bf16)
+        low = jnp.broadcast_to(cell & 255, (256, WIDTH)).astype(bf16)
+        hot = jnp.where(row256 == low, one, zero)
+        tiles = [rows[40 * step + o : 40 * step + o + 16, :].astype(bf16) for o in (0, 16, 12, 8, 4)]
+        left = jnp.concatenate(
+            [jnp.where(high == blocks[t], tiles[t % 5], zero) for t in range(20)], axis=0
+        )
         result = result + lax.dot_general(
-            left[:, span], hot[:, span], (((1,), (1,)), ((), ())), preferred_element_type=f32
+            left, hot, (((1,), (1,)), ((), ())), preferred_element_type=f32
         )
     sums[...] = result
     for h in range(16):
@@ -833,9 +834,7 @@
         total_kernel,
         out_shape=shape(5, 2, 4096),
         scratch_shapes=[
-            pltpu.VMEM((320, 8192), bf16),
-            pltpu.VMEM((256, 8192), bf16),
-            pltpu.VMEM((64 * 40, 128), f32),
+            pltpu.VMEM((8192 // WIDTH * 40, WIDTH), f32),
             pltpu.VMEM((320, 256), f32),
         ],
         compiler_params=PARAMS,

time: 63.3 us -> 62.1 us (0.981)
  Pallas kernels: 22.8 us -> 21.5 us
    pallas_call x1, Pallas kernels: 3.64 us -> 2.39 us  [shards(): pl.pallas_call(total_kernel, out_shape=shape(5, 2, 4096), scratch_shapes=...]
where the time goes in v5:
time: 62.1 us; the launch traced here: 61.8 us
  starting transfers between devices  26.5 us (43%)
  Pallas kernels  21.5 us (35%)
  waiting for transfers between devices  12.9 us (21%)
  between operations  0.85 us (1%)
    all_to_all x1, starting transfers between devices, shards(): lax.all_to_all(outgoing.reshape(32, 1, BLOCK_ROWS * 128), 'dom', split_ax...  11.5 us
    pallas_call x1, Pallas kernels, shards(): pl.pallas_call(advect_kernel, out_shape=(shape(32, 128), shape(5, 4096)),...  6.83 us
    all_to_all x1, waiting for transfers between devices, shards(): lax.all_to_all(send, ('grp', 'dom'), split_axis=0, concat_axis=0, tiled=T...  6.82 us
    all_to_all x1, waiting for transfers between devices, shards(): lax.all_to_all(outgoing.reshape(32, 1, BLOCK_ROWS * 128), 'dom', split_ax...  6.04 us
    all_to_all x1, starting transfers between devices, shards(): lax.all_to_all(send, ('grp', 'dom'), split_axis=0, concat_axis=0, tiled=T...  5.59 us
    ppermute x1, starting transfers between devices, shards(): edge_far = lax.ppermute(edge, 'grp', odd)  4.89 us
    pallas_call x1, Pallas kernels, shards(): pl.pallas_call(ice_kernel, out_shape=(shape(2, LEVELS, 4, 128), shape(102...  4.28 us
    pallas_call x1, Pallas kernels, shards(): pl.pallas_call(pack_kernel, out_shape=(shape(32 * BLOCK_ROWS, 128), shape...  3.96 us
  transfers between devices with their start and end apart: 6, of which 2 were waited for; matrix products, arithmetic and copies ran while one was open for 0% of the time, Pallas kernels for 16%

profile of v5, /device:TPU:1, one launch (start us, length us, event | category | flops | bytes accessed | tf_op | source)
XLA Modules:
  0.0 61.8 jit_solution(4066891971478511449)
XLA Ops:
  0.6 4.0 %pack.1 = (f32[1152,128]{1,0:T(8,128)}, f32[136,128]{1,0:T(8,128)}, f32[136,128]{1,0:T(8,128)}, f32[6,32,128]{2,1,0:T(8,128)}) custom-call(f32[32,128]{1,0:T(8,128)} %bitcast.12, f32[20,4096]{1,0:T(8,128)} %heat_in.1, f32[2,4096]{1,0:T(2,128)} %slope_in.1, f32[32,128]{1,0:T(8,128)} %bitcast.13, s32[1,4,32,64]{3,2,1,0:T(8,128)} %donor.2, s32[4,128]{1,0:T(4,128)} %shaft.2, ...), custom_call_target="tpu_custom_call" | custom-call | tf_op jit(solution)/shard_map/pack/pallas_call | solution.py:732
  4.6 0.0 copy-start.9
  4.6 0.0 copy-start.8
  4.6 0.0 copy-start.1
  4.6 0.0 copy-start.2
  4.6 11.5 %all-to-all-start = ((f32[32,1,4608]{2,1,0:T(1,128)}), f32[32,1,4608]{2,1,0:T(1,128)S(1)}, u32[]{:S(2)}, u32[]{:S(2)}) async-start(f32[32,1,4608]{2,1,0:T(1,128)} %bitcast.10), calls=%async_computation | async-start | bytes 1179648 | tf_op jit(solution)/shard_map/all_to_all | solution.py:768
  16.1 0.0 copy-start.7
  16.2 0.0 copy-done.9
  16.2 0.7 %collective-permute-start.1 = (f32[136,128]{1,0:T(8,128)S(1)}, f32[136,128]{1,0:T(8,128)S(1)}, u32[]{:S(2)}, u32[]{:S(2)}) collective-permute-start(f32[136,128]{1,0:T(8,128)S(1)} %copy-done.9), channel_id=1, source_target_pairs={{1,2},{2,1},{3,4},{4,3},{5,6},{6,5},{7,8},{8,7},{9,10},{10,9},{11,... | collective-permute-start | bytes 208904 | tf_op jit(solution)/shard_map/ppermute | solution.py:773
  16.8 0.0 copy-done.8
  16.8 3.7 %collective-permute-start = (f32[136,128]{1,0:T(8,128)S(1)}, f32[136,128]{1,0:T(8,128)S(1)}, u32[]{:S(2)}, u32[]{:S(2)}) collective-permute-start(f32[136,128]{1,0:T(8,128)S(1)} %copy-done.8), channel_id=1, source_target_pairs={{0,1},{1,0},{2,3},{3,2},{4,5},{5,4},{6,7},{7,6},{8,9},{9,8},{10,11... | collective-permute-start | bytes 208904 | tf_op jit(solution)/shard_map/ppermute | solution.py:772
  20.6 0.0 copy-done.1
  20.6 0.0 copy-done.7
  20.6 1.4 %prepare.1 = (s32[32,128]{1,0:T(8,128)S(1)}, f32[16,256]{1,0:T(8,128)S(1)}) custom-call(s32[1,4,32,64]{3,2,1,0:T(8,128)S(1)} %copy-done.1, s32[4,128]{1,0:T(4,128)S(1)} %copy-done.7), custom_call_target="tpu_custom_call" | custom-call | tf_op jit(solution)/shard_map/prepare/pallas_call | solution.py:777
  22.0 6.0 %all-to-all-done = f32[32,1,4608]{2,1,0:T(1,128)S(1)} async-done(((f32[32,1,4608]{2,1,0:T(1,128)}), f32[32,1,4608]{2,1,0:T(1,128)S(1)}, u32[]{:S(2)}, u32[]{:S(2)}) %all-to-all-start) | async-done | bytes 589856 | tf_op jit(solution)/shard_map/all_to_all | solution.py:768
  28.0 0.0 collective-permute-done.1.far
  28.0 0.0 collective-permute-done.near
  28.0 0.0 copy-done.2
  28.0 1.1 %columns.1 = (f32[24,8,128]{2,1,0:T(8,128)S(1)}, f32[42,8,128]{2,1,0:T(8,128)S(1)}, f32[56,128]{1,0:T(8,128)S(1)}) custom-call(f32[1152,128]{1,0:T(8,128)S(1)} %bitcast.8, s32[4,128]{1,0:T(4,128)S(1)} %copy-done.7, f32[136,128]{1,0:T(8,128)S(1)} %collective-permute-done.near, f32[136,128]{1,0:T(8,128)S(1)} %collective-permute-done.1.far, ...), custom_call_target="tpu_custom_call" | custom-call | tf_op jit(solution)/shard_map/columns/pallas_call | solution.py:785
  29.1 4.9 %collective-permute-start.3 = (f32[56,128]{1,0:T(8,128)S(1)}, f32[56,128]{1,0:T(8,128)S(1)}, u32[]{:S(2)}, u32[]{:S(2)}) collective-permute-start(f32[56,128]{1,0:T(8,128)S(1)} %get-tuple-element.33.edge), channel_id=1, source_target_pairs={{32,64},{64,32},{33,65},{65,33},{34,66},{66,34},{35,67},{67,35},{3... | collective-permute-start | bytes 86024 | tf_op jit(solution)/shard_map/ppermute | solution.py:794
  34.0 0.1 collective-permute-start.2
  34.1 1.6 %inner.1.partial = f32[84,8,128]{2,1,0:T(8,128)S(1)} custom-call(f32[24,8,128]{2,1,0:T(8,128)S(1)} %get-tuple-element.31.geo, f32[42,8,128]{2,1,0:T(8,128)S(1)} %get-tuple-element.32.vext), custom_call_target="tpu_custom_call" | custom-call | tf_op jit(solution)/shard_map/inner/pallas_call | solution.py:795
  35.7 0.0 collective-permute-done.3.edge_far
  35.7 0.0 collective-permute-done.2.edge_near
  35.7 0.0 copy-start.6
  35.7 4.3 %velocity.1 = (f32[2,21,4,128]{3,2,1,0:T(4,128)}, f32[1024,128]{1,0:T(8,128)}) custom-call(f32[24,8,128]{2,1,0:T(8,128)S(1)} %get-tuple-element.31.geo, f32[42,8,128]{2,1,0:T(8,128)S(1)} %get-tuple-element.32.vext, f32[84,8,128]{2,1,0:T(8,128)S(1)} %inner.1.partial, f32[56,128]{1,0:T(8,128)S(1)} %get-tuple-element.33.edge, ...), custom_call_target="tpu_custom_call" | custom-call | tf_op jit(solution)/shard_map/velocity/pallas_call | solution.py:801
  40.0 0.0 copy-start
  40.0 0.0 copy-start.3
  40.1 0.0 copy-start.4
  40.1 0.0 copy-start.5
  40.1 5.6 %all-to-all-start.1 = ((f32[128,8,128]{2,1,0:T(8,128)}), f32[128,8,128]{2,1,0:T(8,128)S(1)}, u32[]{:S(2)}, u32[]{:S(2)}) async-start(f32[128,8,128]{2,1,0:T(8,128)} %bitcast.5), calls=%async_computation.1 | async-start | bytes 1048576 | tf_op jit(solution)/shard_map/all_to_all | solution.py:817
  45.7 0.0 copy-done.6
  45.7 0.0 copy-done
  45.7 0.0 copy-done.3
  45.7 0.0 copy-done.4
  45.7 0.0 copy-done.5
  45.7 6.8 %advect.1 = (f32[32,128]{1,0:T(8,128)}, f32[5,4096]{1,0:T(8,128)}) custom-call(f32[6,32,128]{2,1,0:T(8,128)S(1)} %copy-done.6, s32[6,4096]{1,0:T(8,128)S(1)} %copy-done.3, f32[6,4096]{1,0:T(8,128)S(1)} %copy-done.4, f32[6,4096]{1,0:T(8,128)S(1)} %copy-done.5, f32[5,6,4096]{2,1,0:T(8,128)S(1)} %copy-done, f32[136,128]{1,0:T(8,128)S(1)} %collective-permute-done.near, ...), custom_call_target="tpu_custom_call" | custom-call | tf_op jit(solution)/shard_map/advect/pallas_call | solution.py:818
  52.6 6.8 %all-to-all-done.1 = f32[128,8,128]{2,1,0:T(8,128)S(1)} async-done(((f32[128,8,128]{2,1,0:T(8,128)}), f32[128,8,128]{2,1,0:T(8,128)S(1)}, u32[]{:S(2)}, u32[]{:S(2)}) %all-to-all-start.1) | async-done | bytes 524320 | tf_op jit(solution)/shard_map/all_to_all | solution.py:817
  59.4 2.4 %totals.1 = f32[5,2,4096]{2,1,0:T(2,128)} custom-call(f32[1024,128]{1,0:T(8,128)S(1)} %bitcast.9, s32[1,4,32,64]{3,2,1,0:T(8,128)S(1)} %copy-done.1, f32[16,256]{1,0:T(8,128)S(1)} %get-tuple-element.37.counts), custom_call_target="tpu_custom_call" | custom-call | tf_op jit(solution)/shard_map/totals/pallas_call | solution.py:833
Async XLA Ops:
  4.6 11.6 %copy-start.9 = (f32[136,128]{1,0:T(8,128)S(1)}, f32[136,128]{1,0:T(8,128)}, u32[]{:S(2)}) copy-start(f32[136,128]{1,0:T(8,128)} %get-tuple-element.23) | copy-start | bytes 208900
  4.6 12.2 %copy-start.8 = (f32[136,128]{1,0:T(8,128)S(1)}, f32[136,128]{1,0:T(8,128)}, u32[]{:S(2)}) copy-start(f32[136,128]{1,0:T(8,128)} %get-tuple-element.22) | copy-start | bytes 208900
  4.6 16.0 %copy-start.1 = (s32[1,4,32,64]{3,2,1,0:T(8,128)S(1)}, s32[1,4,32,64]{3,2,1,0:T(8,128)}, u32[]{:S(2)}) copy-start(s32[1,4,32,64]{3,2,1,0:T(8,128)} %donor.2) | copy-start | bytes 98308
  4.6 23.4 %copy-start.2 = (f32[2,21,4,128]{3,2,1,0:T(4,128)S(1)}, f32[2,21,4,128]{3,2,1,0:T(4,128)}, u32[]{:S(2)}) copy-start(f32[2,21,4,128]{3,2,1,0:T(4,128)} %prior.1) | copy-start | bytes 258052
  4.6 23.4 %all-to-all-start = ((f32[32,1,4608]{2,1,0:T(1,128)}), f32[32,1,4608]{2,1,0:T(1,128)S(1)}, u32[]{:S(2)}, u32[]{:S(2)}) async-start(f32[32,1,4608]{2,1,0:T(1,128)} %bitcast.10), calls=%async_computation | async-start | bytes 1179648 | tf_op jit(solution)/shard_map/all_to_all | solution.py:768
  16.1 4.4 %copy-start.7 = (s32[4,128]{1,0:T(4,128)S(1)}, s32[4,128]{1,0:T(4,128)}, u32[]{:S(2)}) copy-start(s32[4,128]{1,0:T(4,128)} %shaft.2) | copy-start | bytes 6148
  16.2 11.9 %collective-permute-start.1 = (f32[136,128]{1,0:T(8,128)S(1)}, f32[136,128]{1,0:T(8,128)S(1)}, u32[]{:S(2)}, u32[]{:S(2)}) collective-permute-start(f32[136,128]{1,0:T(8,128)S(1)} %copy-done.9), channel_id=1, source_target_pairs={{1,2},{2,1},{3,4},{4,3},{5,6},{6,5},{7,8},{8,7},{9,10},{10,9},{11,... | collective-permute-start | bytes 208904 | tf_op jit(solution)/shard_map/ppermute | solution.py:773
  16.8 11.2 %collective-permute-start = (f32[136,128]{1,0:T(8,128)S(1)}, f32[136,128]{1,0:T(8,128)S(1)}, u32[]{:S(2)}, u32[]{:S(2)}) collective-permute-start(f32[136,128]{1,0:T(8,128)S(1)} %copy-done.8), channel_id=1, source_target_pairs={{0,1},{1,0},{2,3},{3,2},{4,5},{5,4},{6,7},{7,6},{8,9},{9,8},{10,11... | collective-permute-start | bytes 208904 | tf_op jit(solution)/shard_map/ppermute | solution.py:772
  29.1 6.6 %collective-permute-start.3 = (f32[56,128]{1,0:T(8,128)S(1)}, f32[56,128]{1,0:T(8,128)S(1)}, u32[]{:S(2)}, u32[]{:S(2)}) collective-permute-start(f32[56,128]{1,0:T(8,128)S(1)} %get-tuple-element.33.edge), channel_id=1, source_target_pairs={{32,64},{64,32},{33,65},{65,33},{34,66},{66,34},{35,67},{67,35},{3... | collective-permute-start | bytes 86024 | tf_op jit(solution)/shard_map/ppermute | solution.py:794
  34.0 1.7 %collective-permute-start.2 = (f32[56,128]{1,0:T(8,128)S(1)}, f32[56,128]{1,0:T(8,128)S(1)}, u32[]{:S(2)}, u32[]{:S(2)}) collective-permute-start(f32[56,128]{1,0:T(8,128)S(1)} %get-tuple-element.33.edge), channel_id=1, source_target_pairs={{0,32},{32,0},{64,96},{96,64},{1,33},{33,1},{65,97},{97,65},{2,34}... | collective-permute-start | bytes 86024 | tf_op jit(solution)/shard_map/ppermute | solution.py:793
  35.7 10.0 %copy-start.6 = (f32[6,32,128]{2,1,0:T(8,128)S(1)}, f32[6,32,128]{2,1,0:T(8,128)}, u32[]{:S(2)}) copy-start(f32[6,32,128]{2,1,0:T(8,128)} %get-tuple-element.21.own) | copy-start | bytes 294916
  40.0 5.7 %copy-start = (f32[5,6,4096]{2,1,0:T(8,128)S(1)}, f32[5,6,4096]{2,1,0:T(8,128)}, u32[]{:S(2)}) copy-start(f32[5,6,4096]{2,1,0:T(8,128)} %tier_speed.1) | copy-start | bytes 1474564
  40.0 5.7 %copy-start.3 = (s32[6,4096]{1,0:T(8,128)S(1)}, s32[6,4096]{1,0:T(8,128)}, u32[]{:S(2)}) copy-start(s32[6,4096]{1,0:T(8,128)} %adjacent.1) | copy-start | bytes 294916
  40.1 5.7 %copy-start.4 = (f32[6,4096]{1,0:T(8,128)S(1)}, f32[6,4096]{1,0:T(8,128)}, u32[]{:S(2)}) copy-start(f32[6,4096]{1,0:T(8,128)} %ratio.1) | copy-start | bytes 294916
  40.1 5.7 %copy-start.5 = (f32[6,4096]{1,0:T(8,128)S(1)}, f32[6,4096]{1,0:T(8,128)}, u32[]{:S(2)}) copy-start(f32[6,4096]{1,0:T(8,128)} %mean_speed.1) | copy-start | bytes 294916
  40.1 19.3 %all-to-all-start.1 = ((f32[128,8,128]{2,1,0:T(8,128)}), f32[128,8,128]{2,1,0:T(8,128)S(1)}, u32[]{:S(2)}, u32[]{:S(2)}) async-start(f32[128,8,128]{2,1,0:T(8,128)} %bitcast.5), calls=%async_computation.1 | async-start | bytes 1048576 | tf_op jit(solution)/shard_map/all_to_all | solution.py:817

commit v6 on v5

--- a/solution.py
+++ b/solution.py
@@ -16,7 +16,8 @@
 FIELDS = 24
 PAIRS = 12
 BLOCK_ROWS = 36
-MSG_ROWS = 136
+MSG_ROWS = 88
+RIM_ROWS = 48
 WIDTH = 256
 f32 = jnp.float32
 bf16 = jnp.bfloat16
@@ -48,8 +49,8 @@
 
 def pack_kernel(
     ice_in, heat_in, slope_in, drag_in, donor_in, shaft_in, prior_in,
-    out_to, near_to, far_to, own_to,
-    ice, heat, slope, drag, donor, shaft, prior, out, near, far, own, arrivals, leaves,
+    out_to, near_to, far_to, own_to, near_rim_to, far_rim_to,
+    ice, heat, slope, drag, donor, shaft, prior, out, near, far, own, near_rim, far_rim, arrivals, leaves,
 ):
     g = lax.axis_index("grp")
     d = lax.axis_index("dom")
@@ -108,7 +109,7 @@
             out[pl.ds(at + 48 + p, 8, stride=72), :] = odd
             out[pl.ds(at + 24 + p, 8, stride=72), :] = odd
         span = slice(0, 536) if v == 0 else slice(536, 1152)
-        copy = pltpu.make_async_copy(out.at[span], out_to.at[span], leaves.at[3 + v])
+        copy = pltpu.make_async_copy(out.at[span], out_to.at[span], leaves.at[5 + v])
         copy.start()
         leaving.append(copy)
     for copy in copies[5:]:
@@ -123,7 +124,7 @@
                 for k in range(32):
                     own[i + 1, k : k + 1, :] = heat[layer : layer + 1, 128 * k : 128 * k + 128]
 
-    def message(msg, row0, chunk0):
+    def message(msg, rim, row0, chunk0):
         for c in range(2):
             for z in range(LEVELS):
                 at = 2 * (c * LEVELS + z)
@@ -131,21 +132,29 @@
         msg[84:86, :] = shaft[row0 : row0 + 2, :].astype(f32)
         msg[86:88, :] = jnp.zeros((2, 128), f32)
         for i in range(6):
-            msg[88 + 8 * i : 96 + 8 * i, :] = own[i, chunk0 : chunk0 + 8, :]
+            rim[8 * i : 8 * i + 8, :] = own[i, chunk0 : chunk0 + 8, :]
 
     even_device = d % 2 == 0
 
     @pl.when(even_device)
     def _():
-        message(near, 2, 24)
-        message(far, 0, 0)
+        message(near, near_rim, 2, 24)
+        message(far, far_rim, 0, 0)
 
     @pl.when(jnp.logical_not(even_device))
     def _():
-        message(near, 0, 0)
-        message(far, 2, 24)
-
-    for i, (a, b) in enumerate(((near, near_to), (far, far_to), (own, own_to))):
+        message(near, near_rim, 0, 0)
+        message(far, far_rim, 2, 24)
+
+    for i, (a, b) in enumerate(
+        (
+            (near, near_to),
+            (far, far_to),
+            (own, own_to),
+            (near_rim, near_rim_to),
+            (far_rim, far_rim_to),
+        )
+    ):
         copy = pltpu.make_async_copy(a, b, leaves.at[i])
         copy.start()
         leaving.append(copy)
@@ -157,8 +166,8 @@
     d = lax.axis_index("dom")
     even_device = d % 2 == 0
     for i in range(6):
-        a = near[88 + 8 * i : 96 + 8 * i, :]
-        b = far[88 + 8 * i : 96 + 8 * i, :]
+        a = near[8 * i : 8 * i + 8, :]
+        b = far[8 * i : 8 * i + 8, :]
         ext[i, 0:8, :] = jnp.where(even_device, b, a)
         ext[i, 40:48, :] = jnp.where(even_device, a, b)
         ext[i, 8:40, :] = own[i]
@@ -729,16 +738,18 @@
 ):
     ice = ice_depth.reshape(32, 128)
     drag = sliding_drag.reshape(32, 128)
-    outgoing, near_out, far_out, own = pl.pallas_call(
+    outgoing, near_out, far_out, own, near_rim, far_rim = pl.pallas_call(
         pack_kernel,
         out_shape=(
             shape(32 * BLOCK_ROWS, 128),
             shape(MSG_ROWS, 128),
             shape(MSG_ROWS, 128),
             shape(6, 32, 128),
+            shape(RIM_ROWS, 128),
+            shape(RIM_ROWS, 128),
         ),
         in_specs=[pl.BlockSpec(memory_space=pltpu.HBM)] * 7,
-        out_specs=[pl.BlockSpec(memory_space=pltpu.HBM)] * 4,
+        out_specs=[pl.BlockSpec(memory_space=pltpu.HBM)] * 6,
         scratch_shapes=[
             pltpu.VMEM((32, 128), f32),
             pltpu.VMEM((LAYERS, 4096), f32),
@@ -751,8 +762,10 @@
             pltpu.VMEM((MSG_ROWS, 128), f32),
             pltpu.VMEM((MSG_ROWS, 128), f32),
             pltpu.VMEM((6, 32, 128), f32),
+            pltpu.VMEM((RIM_ROWS, 128), f32),
+            pltpu.VMEM((RIM_ROWS, 128), f32),
             pltpu.SemaphoreType.DMA((7,)),
-            pltpu.SemaphoreType.DMA((5,)),
+            pltpu.SemaphoreType.DMA((7,)),
         ],
         compiler_params=WIDE,
         name="pack",
@@ -789,6 +802,7 @@
         compiler_params=PARAMS,
         name="columns",
     )(arrived, shaft_holding_position, near, far, prior_node_motion)
+    rims = near_pairs(lax.axis_size("dom"))
     even, odd = near_pairs(lax.axis_size("grp"))
     edge_near = lax.ppermute(edge, "grp", even)
     edge_far = lax.ppermute(edge, "grp", odd)
@@ -815,6 +829,9 @@
         name="velocity",
     )(geo, vext, partial, edge, edge_near, edge_far, origin)
     back = lax.all_to_all(send, ("grp", "dom"), split_axis=0, concat_axis=0, tiled=True)
+    near_rim, far_rim, send = lax.optimization_barrier((near_rim, far_rim, send))
+    near_rim = lax.ppermute(near_rim, "dom", rims[0])
+    far_rim = lax.ppermute(far_rim, "dom", rims[1])
     depth, heat = pl.pallas_call(
         advect_kernel,
         out_shape=(shape(32, 128), shape(5, 4096)),
@@ -827,8 +844,8 @@
         edge_timing_ratio,
         edge_average_normal_speed,
         tier_edge_normal_speed,
-        near,
-        far,
+        near_rim,
+        far_rim,
     )
     tier_motion = pl.pallas_call(
         total_kernel,

time: 62.1 us -> 67 us (1.079)
  the two profiles are of different devices: /device:TPU:1 before, /device:TPU:6 now
where the time goes in v6:
time: 67 us; the launch traced here: 66.7 us
  starting transfers between devices  34.9 us (52%)
  Pallas kernels  21.5 us (32%)
  waiting for transfers between devices  9.38 us (14%)
  between operations  0.86 us (1%)
    all_to_all x1, starting transfers between devices, shards(): lax.all_to_all(outgoing.reshape(32, 1, BLOCK_ROWS * 128), 'dom', split_ax...  11.2 us
    ppermute x1, starting transfers between devices, shards(): far_rim = lax.ppermute(far_rim, 'dom', rims[1])  7.78 us
    pallas_call x1, Pallas kernels, shards(): pl.pallas_call(advect_kernel, out_shape=(shape(32, 128), shape(5, 4096)),...  6.83 us
    ppermute x1, starting transfers between devices, shards(): far = lax.ppermute(far_out, 'dom', odd)  6.69 us
    all_to_all x1, starting transfers between devices, shards(): lax.all_to_all(send, ('grp', 'dom'), split_axis=0, concat_axis=0, tiled=T...  5.53 us
    pallas_call x1, Pallas kernels, shards(): pl.pallas_call(ice_kernel, out_shape=(shape(2, LEVELS, 4, 128), shape(102...  4.27 us
    pallas_call x1, Pallas kernels, shards(): pl.pallas_call(pack_kernel, out_shape=(shape(32 * BLOCK_ROWS, 128), shape...  3.97 us
    ppermute x1, waiting for transfers between devices, shards(): far_rim = lax.ppermute(far_rim, 'dom', rims[1])  3.68 us
  transfers between devices with their start and end apart: 8, of which 4 were waited for; matrix products, arithmetic and copies ran while one was open for 0% of the time, Pallas kernels for 15%

profile of v6, /device:TPU:6, one launch (start us, length us, event | category | flops | bytes accessed | tf_op | source)
XLA Modules:
  0.0 66.7 jit_solution(18071127346140994168)
XLA Ops:
  0.6 4.0 %pack.1 = (f32[1152,128]{1,0:T(8,128)}, f32[88,128]{1,0:T(8,128)}, f32[88,128]{1,0:T(8,128)}, f32[6,32,128]{2,1,0:T(8,128)}, f32[48,128]{1,0:T(8,128)}, /*index=5*/f32[48,128]{1,0:T(8,128)}) custom-call(f32[32,128]{1,0:T(8,128)} %bitcast.12, f32[20,4096]{1,0:T(8,128)} %heat_in.1, f32[2,4096]{1,0:T(2,128)} %slope_in.1, f32[32,128]{1,0:T(8,128)} %bitcast.13, ...), custom_call_target="tpu_custom_call" | custom-call | tf_op jit(solution)/shard_map/pack/pallas_call | solution.py:741
  4.6 0.0 copy-start.9
  4.6 0.0 copy-start.8
  4.6 0.0 copy-start.1
  4.6 0.0 copy-start.2
  4.7 11.2 %all-to-all-start = ((f32[32,1,4608]{2,1,0:T(1,128)}), f32[32,1,4608]{2,1,0:T(1,128)S(1)}, u32[]{:S(2)}, u32[]{:S(2)}) async-start(f32[32,1,4608]{2,1,0:T(1,128)} %bitcast.10), calls=%async_computation | async-start | bytes 1179648 | tf_op jit(solution)/shard_map/all_to_all | solution.py:781
  15.9 0.0 copy-start.7
  15.9 0.0 copy-done.9
  15.9 6.7 %collective-permute-start.1 = (f32[88,128]{1,0:T(8,128)S(1)}, f32[88,128]{1,0:T(8,128)S(1)}, u32[]{:S(2)}, u32[]{:S(2)}) collective-permute-start(f32[88,128]{1,0:T(8,128)S(1)} %copy-done.9), channel_id=1, source_target_pairs={{1,2},{2,1},{3,4},{4,3},{5,6},{6,5},{7,8},{8,7},{9,10},{10,9},{11,... | collective-permute-start | bytes 135176 | tf_op jit(solution)/shard_map/ppermute | solution.py:786
  22.6 0.0 copy-done.8
  22.6 0.1 collective-permute-start
  22.7 0.0 copy-done.1
  22.7 0.0 copy-done.7
  22.7 1.4 %prepare.1 = (s32[32,128]{1,0:T(8,128)S(1)}, f32[16,256]{1,0:T(8,128)S(1)}) custom-call(s32[1,4,32,64]{3,2,1,0:T(8,128)S(1)} %copy-done.1, s32[4,128]{1,0:T(4,128)S(1)} %copy-done.7), custom_call_target="tpu_custom_call" | custom-call | tf_op jit(solution)/shard_map/prepare/pallas_call | solution.py:790
  24.1 3.4 %all-to-all-done = f32[32,1,4608]{2,1,0:T(1,128)S(1)} async-done(((f32[32,1,4608]{2,1,0:T(1,128)}), f32[32,1,4608]{2,1,0:T(1,128)S(1)}, u32[]{:S(2)}, u32[]{:S(2)}) %all-to-all-start) | async-done | bytes 589856 | tf_op jit(solution)/shard_map/all_to_all | solution.py:781
  27.6 0.7 %collective-permute-done.1.far = f32[88,128]{1,0:T(8,128)S(1)} collective-permute-done((f32[88,128]{1,0:T(8,128)S(1)}, f32[88,128]{1,0:T(8,128)S(1)}, u32[]{:S(2)}, u32[]{:S(2)}) %collective-permute-start.1) | collective-permute-done | bytes 45088 | tf_op jit(solution)/shard_map/ppermute | solution.py:786
  28.3 0.0 collective-permute-done.near
  28.3 0.0 copy-done.2
  28.3 1.1 %columns.1 = (f32[24,8,128]{2,1,0:T(8,128)S(1)}, f32[42,8,128]{2,1,0:T(8,128)S(1)}, f32[56,128]{1,0:T(8,128)S(1)}) custom-call(f32[1152,128]{1,0:T(8,128)S(1)} %bitcast.8, s32[4,128]{1,0:T(4,128)S(1)} %copy-done.7, f32[88,128]{1,0:T(8,128)S(1)} %collective-permute-done.near, f32[88,128]{1,0:T(8,128)S(1)} %collective-permute-done.1.far, ...), custom_call_target="tpu_custom_call" | custom-call | tf_op jit(solution)/shard_map/columns/pallas_call | solution.py:798
  29.3 1.9 %collective-permute-start.3 = (f32[56,128]{1,0:T(8,128)S(1)}, f32[56,128]{1,0:T(8,128)S(1)}, u32[]{:S(2)}, u32[]{:S(2)}) collective-permute-start(f32[56,128]{1,0:T(8,128)S(1)} %get-tuple-element.37.edge), channel_id=1, source_target_pairs={{32,64},{64,32},{33,65},{65,33},{34,66},{66,34},{35,67},{67,35},{3... | collective-permute-start | bytes 86024 | tf_op jit(solution)/shard_map/ppermute | solution.py:808
  31.3 0.1 collective-permute-start.2
  31.4 1.6 %inner.1.partial = f32[84,8,128]{2,1,0:T(8,128)S(1)} custom-call(f32[24,8,128]{2,1,0:T(8,128)S(1)} %get-tuple-element.35.geo, f32[42,8,128]{2,1,0:T(8,128)S(1)} %get-tuple-element.36.vext), custom_call_target="tpu_custom_call" | custom-call | tf_op jit(solution)/shard_map/inner/pallas_call | solution.py:809
  32.9 1.6 %collective-permute-done.3.edge_far = f32[56,128]{1,0:T(8,128)S(1)} collective-permute-done((f32[56,128]{1,0:T(8,128)S(1)}, f32[56,128]{1,0:T(8,128)S(1)}, u32[]{:S(2)}, u32[]{:S(2)}) %collective-permute-start.3) | collective-permute-done | bytes 28704 | tf_op jit(solution)/shard_map/ppermute | solution.py:808
  34.5 0.0 collective-permute-done.2.edge_near
  34.5 0.0 copy-start.11
  34.5 0.0 copy-start.10
  34.5 0.0 copy-start.6
  34.5 4.3 %velocity.1 = (f32[2,21,4,128]{3,2,1,0:T(4,128)}, f32[1024,128]{1,0:T(8,128)}) custom-call(f32[24,8,128]{2,1,0:T(8,128)S(1)} %get-tuple-element.35.geo, f32[42,8,128]{2,1,0:T(8,128)S(1)} %get-tuple-element.36.vext, f32[84,8,128]{2,1,0:T(8,128)S(1)} %inner.1.partial, f32[56,128]{1,0:T(8,128)S(1)} %get-tuple-element.37.edge, ...), custom_call_target="tpu_custom_call" | custom-call | tf_op jit(solution)/shard_map/velocity/pallas_call | solution.py:815
  38.8 0.0 copy-start
  38.8 0.0 copy-start.3
  38.8 0.0 copy-start.4
  38.8 0.0 copy-start.5
  38.9 5.5 %all-to-all-start.1 = ((f32[128,8,128]{2,1,0:T(8,128)}), f32[128,8,128]{2,1,0:T(8,128)S(1)}, u32[]{:S(2)}, u32[]{:S(2)}) async-start(f32[128,8,128]{2,1,0:T(8,128)} %bitcast.5), calls=%async_computation.1 | async-start | bytes 1048576 | tf_op jit(solution)/shard_map/all_to_all | solution.py:831
  44.4 0.0 copy-done.11
  44.4 1.5 %collective-permute-start.4 = (f32[48,128]{1,0:T(8,128)S(1)}, f32[48,128]{1,0:T(8,128)S(1)}, u32[]{:S(2)}, u32[]{:S(2)}) collective-permute-start(f32[48,128]{1,0:T(8,128)S(1)} %copy-done.11), channel_id=1, source_target_pairs={{0,1},{1,0},{2,3},{3,2},{4,5},{5,4},{6,7},{7,6},{8,9},{9,8},{10,11... | collective-permute-start | bytes 73736 | tf_op jit(solution)/shard_map/ppermute | solution.py:833
  46.0 0.0 copy-done.10
  46.0 7.8 %collective-permute-start.5 = (f32[48,128]{1,0:T(8,128)S(1)}, f32[48,128]{1,0:T(8,128)S(1)}, u32[]{:S(2)}, u32[]{:S(2)}) collective-permute-start(f32[48,128]{1,0:T(8,128)S(1)} %copy-done.10), channel_id=1, source_target_pairs={{1,2},{2,1},{3,4},{4,3},{5,6},{6,5},{7,8},{8,7},{9,10},{10,9},{11,... | collective-permute-start | bytes 73736 | tf_op jit(solution)/shard_map/ppermute | solution.py:834
  53.7 0.0 collective-permute-done.4.near
  53.8 3.7 %collective-permute-done.5.far = f32[48,128]{1,0:T(8,128)S(1)} collective-permute-done((f32[48,128]{1,0:T(8,128)S(1)}, f32[48,128]{1,0:T(8,128)S(1)}, u32[]{:S(2)}, u32[]{:S(2)}) %collective-permute-start.5) | collective-permute-done | bytes 24608 | tf_op jit(solution)/shard_map/ppermute | solution.py:834
  57.4 0.0 copy-done.6
  57.4 0.0 copy-done
  57.4 0.0 copy-done.3
  57.4 0.0 copy-done.4
  57.5 0.0 copy-done.5
  57.5 6.8 %advect.1 = (f32[32,128]{1,0:T(8,128)}, f32[5,4096]{1,0:T(8,128)}) custom-call(f32[6,32,128]{2,1,0:T(8,128)S(1)} %copy-done.6, s32[6,4096]{1,0:T(8,128)S(1)} %copy-done.3, f32[6,4096]{1,0:T(8,128)S(1)} %copy-done.4, f32[6,4096]{1,0:T(8,128)S(1)} %copy-done.5, f32[5,6,4096]{2,1,0:T(8,128)S(1)} %copy-done, f32[48,128]{1,0:T(8,128)S(1)} %collective-permute-done.4.near, ...), custom_call_target="tpu_custom_call" | custom-call | tf_op jit(solution)/shard_map/advect/pallas_call | solution.py:835
  64.3 0.0 all-to-all-done.1
  64.3 2.4 %totals.1 = f32[5,2,4096]{2,1,0:T(2,128)} custom-call(f32[1024,128]{1,0:T(8,128)S(1)} %bitcast.9, s32[1,4,32,64]{3,2,1,0:T(8,128)S(1)} %copy-done.1, f32[16,256]{1,0:T(8,128)S(1)} %get-tuple-element.45.counts), custom_call_target="tpu_custom_call" | custom-call | tf_op jit(solution)/shard_map/totals/pallas_call | solution.py:850
Async XLA Ops:
  4.6 11.3 %copy-start.9 = (f32[88,128]{1,0:T(8,128)S(1)}, f32[88,128]{1,0:T(8,128)}, u32[]{:S(2)}) copy-start(f32[88,128]{1,0:T(8,128)} %get-tuple-element.34) | copy-start | bytes 135172
  4.6 18.0 %copy-start.8 = (f32[88,128]{1,0:T(8,128)S(1)}, f32[88,128]{1,0:T(8,128)}, u32[]{:S(2)}) copy-start(f32[88,128]{1,0:T(8,128)} %get-tuple-element.29) | copy-start | bytes 135172
  4.6 18.1 %copy-start.1 = (s32[1,4,32,64]{3,2,1,0:T(8,128)S(1)}, s32[1,4,32,64]{3,2,1,0:T(8,128)}, u32[]{:S(2)}) copy-start(s32[1,4,32,64]{3,2,1,0:T(8,128)} %donor.2) | copy-start | bytes 98308
  4.6 23.6 %copy-start.2 = (f32[2,21,4,128]{3,2,1,0:T(4,128)S(1)}, f32[2,21,4,128]{3,2,1,0:T(4,128)}, u32[]{:S(2)}) copy-start(f32[2,21,4,128]{3,2,1,0:T(4,128)} %prior.1) | copy-start | bytes 258052
  4.7 22.9 %all-to-all-start = ((f32[32,1,4608]{2,1,0:T(1,128)}), f32[32,1,4608]{2,1,0:T(1,128)S(1)}, u32[]{:S(2)}, u32[]{:S(2)}) async-start(f32[32,1,4608]{2,1,0:T(1,128)} %bitcast.10), calls=%async_computation | async-start | bytes 1179648 | tf_op jit(solution)/shard_map/all_to_all | solution.py:781
  15.9 6.8 %copy-start.7 = (s32[4,128]{1,0:T(4,128)S(1)}, s32[4,128]{1,0:T(4,128)}, u32[]{:S(2)}) copy-start(s32[4,128]{1,0:T(4,128)} %shaft.2) | copy-start | bytes 6148
  15.9 12.4 %collective-permute-start.1 = (f32[88,128]{1,0:T(8,128)S(1)}, f32[88,128]{1,0:T(8,128)S(1)}, u32[]{:S(2)}, u32[]{:S(2)}) collective-permute-start(f32[88,128]{1,0:T(8,128)S(1)} %copy-done.9), channel_id=1, source_target_pairs={{1,2},{2,1},{3,4},{4,3},{5,6},{6,5},{7,8},{8,7},{9,10},{10,9},{11,... | collective-permute-start | bytes 135176 | tf_op jit(solution)/shard_map/ppermute | solution.py:786
  22.6 5.6 %collective-permute-start = (f32[88,128]{1,0:T(8,128)S(1)}, f32[88,128]{1,0:T(8,128)S(1)}, u32[]{:S(2)}, u32[]{:S(2)}) collective-permute-start(f32[88,128]{1,0:T(8,128)S(1)} %copy-done.8), channel_id=1, source_target_pairs={{0,1},{1,0},{2,3},{3,2},{4,5},{5,4},{6,7},{7,6},{8,9},{9,8},{10,11... | collective-permute-start | bytes 135176 | tf_op jit(solution)/shard_map/ppermute | solution.py:785
  29.3 5.2 %collective-permute-start.3 = (f32[56,128]{1,0:T(8,128)S(1)}, f32[56,128]{1,0:T(8,128)S(1)}, u32[]{:S(2)}, u32[]{:S(2)}) collective-permute-start(f32[56,128]{1,0:T(8,128)S(1)} %get-tuple-element.37.edge), channel_id=1, source_target_pairs={{32,64},{64,32},{33,65},{65,33},{34,66},{66,34},{35,67},{67,35},{3... | collective-permute-start | bytes 86024 | tf_op jit(solution)/shard_map/ppermute | solution.py:808
  31.3 3.3 %collective-permute-start.2 = (f32[56,128]{1,0:T(8,128)S(1)}, f32[56,128]{1,0:T(8,128)S(1)}, u32[]{:S(2)}, u32[]{:S(2)}) collective-permute-start(f32[56,128]{1,0:T(8,128)S(1)} %get-tuple-element.37.edge), channel_id=1, source_target_pairs={{0,32},{32,0},{64,96},{96,64},{1,33},{33,1},{65,97},{97,65},{2,34}... | collective-permute-start | bytes 86024 | tf_op jit(solution)/shard_map/ppermute | solution.py:807
  34.5 9.9 %copy-start.11 = (f32[48,128]{1,0:T(8,128)S(1)}, f32[48,128]{1,0:T(8,128)}, u32[]{:S(2)}) copy-start(f32[48,128]{1,0:T(8,128)} %get-tuple-element.40) | copy-start | bytes 73732
  34.5 11.4 %copy-start.10 = (f32[48,128]{1,0:T(8,128)S(1)}, f32[48,128]{1,0:T(8,128)}, u32[]{:S(2)}) copy-start(f32[48,128]{1,0:T(8,128)} %get-tuple-element.41) | copy-start | bytes 73732
  34.5 22.9 %copy-start.6 = (f32[6,32,128]{2,1,0:T(8,128)S(1)}, f32[6,32,128]{2,1,0:T(8,128)}, u32[]{:S(2)}) copy-start(f32[6,32,128]{2,1,0:T(8,128)} %get-tuple-element.25.own) | copy-start | bytes 294916
  38.8 18.6 %copy-start = (f32[5,6,4096]{2,1,0:T(8,128)S(1)}, f32[5,6,4096]{2,1,0:T(8,128)}, u32[]{:S(2)}) copy-start(f32[5,6,4096]{2,1,0:T(8,128)} %tier_speed.1) | copy-start | bytes 1474564
  38.8 18.6 %copy-start.3 = (s32[6,4096]{1,0:T(8,128)S(1)}, s32[6,4096]{1,0:T(8,128)}, u32[]{:S(2)}) copy-start(s32[6,4096]{1,0:T(8,128)} %adjacent.1) | copy-start | bytes 294916
  38.8 18.6 %copy-start.4 = (f32[6,4096]{1,0:T(8,128)S(1)}, f32[6,4096]{1,0:T(8,128)}, u32[]{:S(2)}) copy-start(f32[6,4096]{1,0:T(8,128)} %ratio.1) | copy-start | bytes 294916
  38.8 18.6 %copy-start.5 = (f32[6,4096]{1,0:T(8,128)S(1)}, f32[6,4096]{1,0:T(8,128)}, u32[]{:S(2)}) copy-start(f32[6,4096]{1,0:T(8,128)} %mean_speed.1) | copy-start | bytes 294916
  38.9 25.4 %all-to-all-start.1 = ((f32[128,8,128]{2,1,0:T(8,128)}), f32[128,8,128]{2,1,0:T(8,128)S(1)}, u32[]{:S(2)}, u32[]{:S(2)}) async-start(f32[128,8,128]{2,1,0:T(8,128)} %bitcast.5), calls=%async_computation.1 | async-start | bytes 1048576 | tf_op jit(solution)/shard_map/all_to_all | solution.py:831
  44.4 9.3 %collective-permute-start.4 = (f32[48,128]{1,0:T(8,128)S(1)}, f32[48,128]{1,0:T(8,128)S(1)}, u32[]{:S(2)}, u32[]{:S(2)}) collective-permute-start(f32[48,128]{1,0:T(8,128)S(1)} %copy-done.11), channel_id=1, source_target_pairs={{0,1},{1,0},{2,3},{3,2},{4,5},{5,4},{6,7},{7,6},{8,9},{9,8},{10,11... | collective-permute-start | bytes 73736 | tf_op jit(solution)/shard_map/ppermute | solution.py:833
  46.0 11.5 %collective-permute-start.5 = (f32[48,128]{1,0:T(8,128)S(1)}, f32[48,128]{1,0:T(8,128)S(1)}, u32[]{:S(2)}, u32[]{:S(2)}) collective-permute-start(f32[48,128]{1,0:T(8,128)S(1)} %copy-done.10), channel_id=1, source_target_pairs={{1,2},{2,1},{3,4},{4,3},{5,6},{6,5},{7,8},{8,7},{9,10},{10,9},{11,... | collective-permute-start | bytes 73736 | tf_op jit(solution)/shard_map/ppermute | solution.py:834
